TPU v7x, 256 devices: a whole 4x4x8 slice. The times are simulated.
256 devices in a mesh: grp: 16 (over z, y_lo), tp: 16 (over y_hi, x, core).
Axes of the slice: x: 4, y: 4 (y_hi: 2, y_lo: 2; y = y_hi * 2 + y_lo), z: 8, core: 2. Of those that a mesh axis runs over, the one named last changes fastest.
Arguments:
- activations: bfloat16 [98304, 8192], P('grp', 'tp'), may hold values from -6 to 6
- cotangents: bfloat16 [98304, 8192], P('grp', 'tp'), may hold values from -6 to 6
- adapter_down_weight: bfloat16 [8192, 16], P('tp'), may hold values from -0.0625 to 0.0625
- adapter_up_weight: bfloat16 [16, 8192], P(None, 'tp'), may hold values from -1.5 to 1.5
- sign_flag_bits: int32 [8192, 256], P('tp'), may hold values from 0 to 1
- validation_feature_rows: float32 [512, 8192], P('grp', 'tp'), may hold values from -6 to 6
Outputs:
- scores: float32 [96, 512], P('grp', 'tp')
All inputs are finite; a program needn't handle non-finite values.
Results may differ from a plain program's by a relative error of at most 0.0003.
Values sent between devices are 32-bit elements; how exact they have to be, the bound alone decides.
No kernel may reach another device: no remote copies, remote signals or barrier semaphores. Data moves between devices by JAX's collectives and lax.ppermute only.
A program may use at most 128 MiB of HBM per device.

v0:
```python
import math

import jax
import jax.numpy as jnp
from jax import lax
from jax.sharding import PartitionSpec as P

LEN = 1024
K = 8192


def masked_features(proj_x, proj_g, down_activation, up_gradient, member):
    seq_count = member.shape[1]
    rank_index = up_gradient.shape[1]
    width = proj_x.shape[1]
    weighted_up = (member[:, :, None] * up_gradient[:, None, :]).reshape(-1, seq_count * rank_index)
    weighted_down = (member[:, :, None] * down_activation[:, None, :]).reshape(
        -1, seq_count * rank_index
    )
    grad_a = jnp.einsum("tk,tm->km", proj_x, weighted_up, precision=lax.Precision.HIGHEST).reshape(
        width, seq_count, rank_index
    )
    grad_b = jnp.einsum(
        "tk,tm->km", proj_g, weighted_down, precision=lax.Precision.HIGHEST
    ).reshape(width, seq_count, rank_index)
    stacked = jnp.stack([grad_a, grad_b], 0)
    return jnp.transpose(stacked, (2, 0, 1, 3)).reshape(seq_count, -1)


def on_device(
    activations,
    cotangents,
    adapter_down_weight,
    adapter_up_weight,
    sign_flag_bits,
    validation_feature_rows,
):
    sign_projector = (2 * sign_flag_bits - 1).astype(jnp.bfloat16)
    up_weight_columns = jnp.transpose(adapter_up_weight)
    seq_count = activations.shape[0] // LEN
    width = sign_projector.shape[1]
    rank_index = adapter_down_weight.shape[1]
    left_factor = jnp.concatenate([sign_projector, adapter_down_weight], 1)
    right_mat = jnp.concatenate([sign_projector, up_weight_columns], 1)
    local_rows = activations.shape[0] // lax.axis_size("tp")
    reduced = lax.psum_scatter(
        jnp.concatenate(
            [
                jnp.dot(activations, left_factor, preferred_element_type=jnp.float32),
                jnp.dot(cotangents, right_mat, preferred_element_type=jnp.float32),
            ],
            1,
        ),
        "tp",
        scatter_dimension=0,
        tiled=True,
    )
    proj_x = reduced[:, :width]
    down_activation = reduced[:, width : width + rank_index]
    proj_g = reduced[:, width + rank_index : 2 * width + rank_index]
    up_gradient = reduced[:, 2 * width + rank_index :]
    positions = lax.axis_index("tp") * local_rows + jnp.arange(local_rows, dtype=jnp.int32)
    member = (positions[:, None] // LEN == jnp.arange(seq_count, dtype=jnp.int32)[None, :]).astype(
        jnp.float32
    )
    features = masked_features(proj_x, proj_g, down_activation, up_gradient, member)
    summed = lax.psum_scatter(features, "tp", scatter_dimension=1, tiled=True)
    train_part = jnp.sum(summed * summed, axis=1)
    valid_part = jnp.sum(validation_feature_rows * validation_feature_rows, axis=1)
    train_sq, valid_sq = lax.psum((train_part, valid_part), "tp")
    unit_train = summed * (math.sqrt(K) / jnp.sqrt(train_sq + 1e-06))[:, None]
    unit_valid = validation_feature_rows / jnp.sqrt(valid_sq + 1e-06)[:, None]
    partial_dot = lax.dot_general(
        unit_train,
        lax.all_gather(unit_valid, "grp", axis=0, tiled=True),
        (((1,), (1,)), ((), ())),
        precision=lax.Precision.HIGHEST,
    )
    return lax.psum_scatter(partial_dot, "tp", scatter_dimension=1, tiled=True)


def solution(mesh):
    return jax.shard_map(
        on_device,
        mesh=mesh,
        in_specs=(
            P("grp", "tp"),
            P("grp", "tp"),
            P("tp", None),
            P(None, "tp"),
            P("tp", None),
            P("grp", "tp"),
        ),
        out_specs=P("grp", "tp"),
        check_vma=False,
    )
```

profile of v0, /device:TPU:1, one launch (start us, length us, event | category | flops | bytes accessed | tf_op | source)
XLA Modules:
  0.0 423.5 jit_solution(12728523424381783939)
XLA Ops:
  6.5 0.0 reduce-scatter.6.cloned.1.call-start
  6.5 1.1 add_convert_fusion
  7.6 0.8 copy.17
  8.5 0.0 slice-start
  8.5 1.0 copy.16
  9.5 0.0 slice-start.1
  9.5 5.7 %convolution_bitcast_fusion = f32[6144,272]{0,1:T(8,128)S(1)} fusion(bf16[6144,512]{1,0:T(8,128)(2,1)} %param.7, bf16[512,256]{1,0:T(8,128)(2,1)S(1)} %add_convert_fusion, bf16[512,16]{1,0:T(8,128)(2,1)S(1)} %bitcast.41), kind=kOutput, calls=%fused_computation.1 | convolution fusion | flops 1711833088 | bytes 13254656 | tf_op jit(solution)/shard_map/dot_general | solution.py:50
  15.2 0.0 slice-done
  15.2 0.0 slice-done.1
  15.2 2.8 convolution_bitcast_fusion.1
  18.0 5.3 %pad_maximum_fusion = f32[6144,544]{0,1:T(8,128)} fusion(f32[6144,272]{0,1:T(8,128)S(1)} %convolution_bitcast_fusion, f32[6144,272]{0,1:T(8,128)S(1)} %convolution_bitcast_fusion.1), kind=kLoop, calls=%fused_computation | loop fusion | flops 3342336 | bytes 26738688 | tf_op jit(solution)/shard_map/concatenate | solution.py:47
  23.4 0.0 copy-start
  23.4 0.0 reduce-scatter.6.cloned.1.call-update
  23.4 0.0 reduce-scatter.8.cloned.1.call-start
  23.5 136.6 %reduce-scatter.6.cloned.1.call-done = f32[384,544]{0,1:T(8,128)} async-done(((f32[6144,544]{0,1:T(8,128)}), f32[384,544]{0,1:T(8,128)}) %reduce-scatter.6.cloned.1.call-update) | async-done | bytes 835600 | tf_op jit(solution)/shard_map/reduce_scatter | solution.py:46
  160.1 0.8 fusion.18
  160.9 1.5 convolution_bitcast_fusion.4
  162.4 1.5 convolution_bitcast_fusion.3
  163.9 0.5 copy.20
  164.3 1.6 reshape.83
  165.9 0.0 reduce-scatter.8.cloned.1.call-update
  166.0 0.0 all-gather.2.cloned.1.call-start
  166.0 0.0 copy-done
  166.0 0.1 multiply_reduce_fusion
  166.1 69.7 %reduce-scatter.8.cloned.1.call-done = f32[6,512]{1,0:T(8,128)} async-done(((f32[6,8192]{1,0:T(8,128)}), f32[6,512]{1,0:T(8,128)}) %reduce-scatter.8.cloned.1.call-update) | async-done | bytes 12304 | tf_op jit(solution)/shard_map/reduce_scatter | solution.py:67
  235.8 0.8 multiply_reduce_fusion.1
  236.6 35.0 %all-reduce = (f32[32]{0:T(128)S(1)}, f32[6]{0:T(128)S(1)}) all-reduce(f32[32]{0:T(128)S(1)} %multiply_reduce_fusion, f32[6]{0:T(128)S(1)} %multiply_reduce_fusion.1), channel_id=1, replica_groups=mesh['grp'=16,'tp'=16] {'tp'}, use_global_device_ids=true, to_apply=%region_5.6 | all-reduce | flops 38 | bytes 304 | tf_op jit(solution)/shard_map/psum | solution.py:70
  271.7 0.7 broadcast_divide_fusion
  272.4 0.0 all-gather.2.cloned.1.call-update
  272.4 0.0 reduce-scatter.10.cloned.1.call-start
  272.5 57.1 %all-gather.2.cloned.1.call-done = f32[512,512]{1,0:T(8,128)} async-done(((f32[32,512]{1,0:T(8,128)}), f32[512,512]{1,0:T(8,128)}) %all-gather.2.cloned.1.call-update) | async-done | bytes 1048592 | tf_op jit(solution)/shard_map/all_gather | solution.py:75
  329.5 3.0 convolution_bitcast_fusion.2
  332.5 0.0 reduce-scatter.10.cloned.1.call-update
  332.6 83.0 %reduce-scatter.10.cloned.1.call-done = f32[32,6]{1,0:T(8,128)} async-done(((f32[512,6]{1,0:T(8,128)}), f32[32,6]{1,0:T(8,128)}) %reduce-scatter.10.cloned.1.call-update) | async-done | bytes 784
  415.5 1.4 copy.26
  (6 shorter events, 0.0 us)
Async XLA Ops:
  6.5 153.6 %reduce-scatter.6.cloned.1.call-start = ((), (), s32[]{:S(2)}) async-start(), calls=%async_computation.3 | async-start | bytes 14204928 | tf_op jit(solution)/shard_map/reduce_scatter | solution.py:46
  8.5 6.7 %slice-start = ((s8[6291456]{0:T(1024)(128)(4,1)}), s8[2097152]{0:T(1024)(128)(4,1)S(1)}, s32[]{:S(2)}) async-start(s8[6291456]{0:T(1024)(128)(4,1)} %bitcast.39), calls=%async_computation.7 | async-start | bytes 4194304
  9.5 5.7 %slice-start.1 = ((s8[6291456]{0:T(1024)(128)(4,1)}), s8[4194304]{0:T(1024)(128)(4,1)S(1)}, s32[]{:S(2)}) async-start(s8[6291456]{0:T(1024)(128)(4,1)} %bitcast.39), calls=%async_computation.8 | async-start | bytes 8388608
  23.4 142.6 %copy-start = (f32[32,512]{1,0:T(8,128)S(1)}, f32[32,512]{1,0:T(8,128)}, u32[]{:S(2)}) copy-start(f32[32,512]{1,0:T(8,128)} %param.11) | copy-start | bytes 196612
  23.4 212.4 %reduce-scatter.8.cloned.1.call-start = ((), (), s32[]{:S(2)}) async-start(), calls=%async_computation.4 | async-start | bytes 278528 | tf_op jit(solution)/shard_map/reduce_scatter | solution.py:67
  166.0 163.6 %all-gather.2.cloned.1.call-start = ((), (), s32[]{:S(2)}) async-start(), calls=%async_computation.5 | async-start | bytes 1114112 | tf_op jit(solution)/shard_map/all_gather | solution.py:75
  272.4 143.1 %reduce-scatter.10.cloned.1.call-start = ((), (), s32[]{:S(2)}) async-start(), calls=%async_computation.6 | async-start | bytes 278528
Sparse Core Ops, SparseCore 0:
  23.5 136.5 reduce-scatter.5
  166.1 69.6 reduce-scatter.7
  272.6 56.9 all-gather.1
  333.9 81.5 reduce-scatter.9
where the time goes:
time: 425 us; the launch traced here: 423 us
  waiting for transfers between devices  346 us (81%)
  blocking collectives  35 us (8%)
  matrix products  14.4 us (3%)
  between operations  13.2 us (3%)
  other arithmetic  8.16 us (2%)
  local copies, waits for them, and re-layouts  6.04 us (1%)
    reduce_scatter x1, waiting for transfers between devices, on_device(): lax.psum_scatter(jnp.concatenate([jnp.dot(activations, left_factor, prefe...  137 us
    unnamed x5, waiting for transfers between devices  83.1 us
    reduce_scatter x1, waiting for transfers between devices, on_device(): summed = lax.psum_scatter(features, 'tp', scatter_dimension=1, tiled=True)  69.7 us
    all_gather x1, waiting for transfers between devices, on_device(): lax.all_gather(unit_valid, 'grp', axis=0, tiled=True)  57.1 us
    psum x1, blocking collectives, on_device(): train_sq, valid_sq = lax.psum((train_part, valid_part), 'tp')  35 us
  transfers between devices with their start and end apart: 4, of which 4 were waited for; matrix products, arithmetic and copies ran while one was open for 0% of the time, Pallas kernels for 0%

commit v1 on v0

v1 whole, which is shorter than its diff:
```python
import functools
import math

import jax
import jax.numpy as jnp
from jax import lax
from jax.experimental import pallas as pl
from jax.experimental.pallas import tpu as pltpu
from jax.sharding import PartitionSpec as P

LEN = 1024
K = 8192
TB = 512
EPS = 1e-06
VMEM = 48 * 1024 * 1024

NT = (((1,), (1,)), ((), ()))
NN = (((1,), (0,)), ((), ()))


def mm(a, b, dims):
    return lax.dot_general(a, b, dims, preferred_element_type=jnp.float32)


def halves(a):
    hi = a.astype(jnp.bfloat16)
    lo = (a - hi.astype(jnp.float32)).astype(jnp.bfloat16)
    return jnp.concatenate([hi, lo], 0)


def rows_kernel(core_ref, x_ref, g_ref, a_ref, b_ref, keep_ref, send_ref, at_ref):
    @pl.when(pl.program_id(0) == 0)
    def _():
        at_ref[...] = jnp.transpose(a_ref[...].astype(jnp.float32)).astype(jnp.bfloat16)

    down = mm(at_ref[...], x_ref[...], NT)
    up = mm(b_ref[...], g_ref[...], NT)
    first = core_ref[0] == 0
    keep_ref[0] = jnp.where(first, down, up)
    send_ref[0] = jnp.where(first, up, down)


def rank_rows(core, x, g, a, b):
    tokens, width = x.shape
    rank = b.shape[0]
    chunk = tokens // 4
    per = chunk // TB
    out = jax.ShapeDtypeStruct((4, rank, chunk), jnp.float32)
    out_spec = pl.BlockSpec((1, rank, TB), lambda i: (i // per, 0, i % per))
    return pl.pallas_call(
        rows_kernel,
        grid=(tokens // TB,),
        in_specs=[
            pl.BlockSpec(memory_space=pltpu.SMEM),
            pl.BlockSpec((TB, width), lambda i: (i, 0)),
            pl.BlockSpec((TB, width), lambda i: (i, 0)),
            pl.BlockSpec((width, rank), lambda i: (0, 0)),
            pl.BlockSpec((rank, width), lambda i: (0, 0)),
        ],
        out_specs=[out_spec, out_spec],
        out_shape=[out, out],
        scratch_shapes=[pltpu.VMEM((rank, width), jnp.bfloat16)],
        compiler_params=pltpu.CompilerParams(vmem_limit_bytes=VMEM),
        cost_estimate=pl.CostEstimate(
            flops=4 * tokens * width * rank, bytes_accessed=4 * tokens * width, transcendentals=0
        ),
        name="rank_rows",
    )(core, x, g, a, b)


def share_kernel(core_ref, x_ref, g_ref, own_ref, other_ref, s_ref, out_ref, v_ref):
    i = pl.program_id(0)
    rank = own_ref.shape[1]
    first = core_ref[0] == 0
    own, other = own_ref[0], other_ref[0]
    up = halves(jnp.where(first, other, own))
    down = halves(jnp.where(first, own, other))
    va = mm(up, x_ref[...], NN)
    vb = mm(down, g_ref[...], NN)
    va = va[:rank] + va[rank:]
    vb = vb[:rank] + vb[rank:]
    here = pl.ds(pl.multiple_of((i * TB // LEN) * rank, rank), rank)

    @pl.when(i == 0)
    def _():
        v_ref[...] = jnp.zeros_like(v_ref)

    v_ref[0, here, :] += va
    v_ref[1, here, :] += vb

    @pl.when(i == pl.num_programs(0) - 1)
    def _():
        sign = (2 * s_ref[...] - 1).astype(jnp.float32).astype(jnp.bfloat16)
        each = out_ref.shape[0] // 2
        for m in range(2):
            f = mm(halves(v_ref[m]), sign, NN)
            f = jnp.transpose(f[:128] + f[128:])
            out_ref[m * each : (m + 1) * each] = f.reshape(each, -1, 128)


def feature_shares(core, x, g, own, other, bits, parts):
    tokens, width = x.shape
    rank, chunk = own.shape[1:]
    per = chunk // TB
    kd = bits.shape[1]
    row_spec = pl.BlockSpec((1, rank, TB), lambda i: (i // per, 0, i % per))
    return pl.pallas_call(
        share_kernel,
        grid=(tokens // TB,),
        in_specs=[
            pl.BlockSpec(memory_space=pltpu.SMEM),
            pl.BlockSpec((TB, width), lambda i: (i, 0)),
            pl.BlockSpec((TB, width), lambda i: (i, 0)),
            row_spec,
            row_spec,
            pl.BlockSpec((width, kd), lambda i: (0, 0)),
        ],
        out_specs=pl.BlockSpec((parts, 2 * kd // parts, 128), lambda i: (0, 0, 0)),
        out_shape=jax.ShapeDtypeStruct((parts, 2 * kd // parts, 128), jnp.float32),
        scratch_shapes=[pltpu.VMEM((2, 128, width), jnp.float32)],
        compiler_params=pltpu.CompilerParams(vmem_limit_bytes=VMEM),
        cost_estimate=pl.CostEstimate(
            flops=8 * tokens * width * rank, bytes_accessed=4 * tokens * width, transcendentals=0
        ),
        name="feature_shares",
    )(core, x, g, own, other, bits)


def valid_kernel(rank, v_ref, hl_ref, sq_ref):
    v = v_ref[...]
    rows, cols = v.shape
    ks = cols // rank
    came = lax.broadcasted_iota(jnp.int32, (cols, cols), 0)
    goes = lax.broadcasted_iota(jnp.int32, (cols, cols), 1)
    move = jnp.where((came % rank) * ks + came // rank == goes, 1.0, 0.0).astype(jnp.bfloat16)
    hl_ref[...] = mm(halves(v), move, NN).astype(jnp.bfloat16)
    sq = halves(v * v)
    total = mm(jnp.ones((8, cols), jnp.bfloat16), sq, NT)
    sq_ref[...] = total[:, :rows] + total[:, rows:]


def valid_terms(v, rank):
    rows, cols = v.shape
    return pl.pallas_call(
        functools.partial(valid_kernel, rank),
        out_shape=[
            jax.ShapeDtypeStruct((2 * rows, cols), jnp.bfloat16),
            jax.ShapeDtypeStruct((8, rows), jnp.float32),
        ],
        compiler_params=pltpu.CompilerParams(vmem_limit_bytes=VMEM),
        cost_estimate=pl.CostEstimate(
            flops=4 * rows * cols * cols, bytes_accessed=8 * rows * cols, transcendentals=0
        ),
        name="valid_terms",
    )(v)


def dot_kernel(rank, f_ref, hl_ref, sq_ref, out_ref, t_ref):
    parts = f_ref.shape[0]
    rows = sq_ref.shape[1]
    each = rows // parts
    t_ref[...] = jnp.transpose(jnp.sum(f_ref[...], 0))
    f = jnp.concatenate([t_ref[pl.ds(r, 8, stride=rank), :] for r in range(rank)], 1)
    prod = mm(halves(f), hl_ref[...], NT)
    dots = prod[:8, :rows] + (prod[8:, :rows] + prod[:8, rows:]) + prod[8:, rows:]
    line = lax.broadcasted_iota(jnp.int32, dots.shape, 0)
    dots = jnp.where(line == 6, sq_ref[...], dots)
    own_sq = jnp.broadcast_to(jnp.sum(f * f, 1, keepdims=True), (8, each))
    for part in range(parts):
        out_ref[part, :, :each] = dots[:, part * each : (part + 1) * each]
        out_ref[part, :, each : 2 * each] = own_sq


def partial_dots(f, hl, sq, rank):
    return pl.pallas_call(
        functools.partial(dot_kernel, rank),
        out_shape=jax.ShapeDtypeStruct((f.shape[0], 8, 128), jnp.float32),
        scratch_shapes=[pltpu.VMEM((128, f.shape[1]), jnp.float32)],
        compiler_params=pltpu.CompilerParams(vmem_limit_bytes=VMEM),
        name="partial_dots",
    )(f, hl, sq)


def score_kernel(p_ref, out_ref):
    seqs, each = out_ref.shape
    p = jnp.sum(p_ref[...], 0)
    train = math.sqrt(K) / jnp.sqrt(p[:seqs, each : 2 * each] + EPS)
    valid = jnp.sqrt(p[6:7, :each] + EPS)
    out_ref[...] = p[:seqs, :each] * train / valid


def on_device(x, g, a, b, bits, valid):
    tp = lax.axis_size("tp")
    grp = lax.axis_size("grp")
    rank = b.shape[0]
    seqs = x.shape[0] // LEN
    core = (lax.axis_index("tp") % 2).astype(jnp.int32).reshape(1)
    swap_core = [(i, i ^ 1) for i in range(tp)]
    swap_y = [(i, i ^ 8) for i in range(tp)]
    along_x = [[(y << 3) | (q << 1) | c for q in range(4)] for y in range(2) for c in range(2)]

    everyone = jnp.broadcast_to(valid[None], (grp, *valid.shape))
    gathered = lax.all_to_all(everyone, "grp", 0, 0, tiled=True).reshape(-1, valid.shape[1])

    keep, send = rank_rows(core, x, g, a, b)
    mine = keep + lax.ppermute(send, "tp", swap_core)
    mine = lax.all_to_all(mine, "tp", 0, 0, axis_index_groups=along_x, tiled=True)
    mine = jnp.sum(mine, 0)
    mine = mine + lax.ppermute(mine, "tp", swap_y)
    mine = jnp.broadcast_to(mine[None], (4, *mine.shape))
    mine = lax.all_to_all(mine, "tp", 0, 0, axis_index_groups=along_x, tiled=True)
    other = lax.ppermute(mine, "tp", swap_core)

    hl, sq = valid_terms(gathered, rank)
    shares = feature_shares(core, x, g, mine, other, bits, tp)
    shares = lax.all_to_all(shares, "tp", 0, 0, tiled=True)
    dots = partial_dots(shares, hl, sq, rank)
    dots = lax.all_to_all(dots, "tp", 0, 0, tiled=True)
    return pl.pallas_call(
        score_kernel,
        out_shape=jax.ShapeDtypeStruct((seqs, grp * valid.shape[0] // tp), jnp.float32),
        name="scores",
    )(dots)


def solution(mesh):
    return jax.shard_map(
        on_device,
        mesh=mesh,
        in_specs=(
            P("grp", "tp"),
            P("grp", "tp"),
            P("tp", None),
            P(None, "tp"),
            P("tp", None),
            P("grp", "tp"),
        ),
        out_specs=P("grp", "tp"),
        check_vma=False,
    )
```

time: 425 us -> 107 us (0.25)
  waiting for transfers between devices: 346 us -> 20 us
  starting transfers between devices: 0.13 us -> 28.7 us
  Pallas kernels: 0 us -> 24.6 us
  matrix products: 14.4 us -> 0 us
  between operations: 13.2 us -> 0.07 us
  other arithmetic: 8.16 us -> 0.09 us
  blocking collectives: 35 us -> 30.1 us
    reduce_scatter x2 -> x0, waiting for transfers between devices: 206 us -> none  [the longest x1 137 us: on_device(): lax.psum_scatter(jnp.concatenate([jnp.dot(activations, left_factor, prefe...]
    unnamed x5 -> x0, waiting for transfers between devices: 83.1 us -> none
    all_gather x1 -> x0, waiting for transfers between devices: 57.1 us -> none  [on_device(): lax.all_gather(unit_valid, 'grp', axis=0, tiled=True)]
    psum x1 -> x0, blocking collectives: 35 us -> none  [on_device(): train_sq, valid_sq = lax.psum((train_part, valid_part), 'tp')]
    all_to_all x0 -> x3, blocking collectives: none -> 30.1 us  [the longest x2 18.8 us: on_device(): lax.all_to_all(mine, 'tp', 0, 0, axis_index_groups=along_x, tiled=True)]
    pallas_call x0 -> x5, Pallas kernels: none -> 24.6 us  [the longest x1 10.8 us: rank_rows(): pl.pallas_call(rows_kernel, grid=(tokens // TB,), in_specs=[pl.BlockSpec(...]
    all_to_all x0 -> x2, starting transfers between devices: none -> 18.8 us  [the longest x1 10.4 us: on_device(): shares = lax.all_to_all(shares, 'tp', 0, 0, tiled=True)]
    all_to_all x0 -> x2, waiting for transfers between devices: none -> 14.3 us  [the longest x1 7.77 us: on_device(): shares = lax.all_to_all(shares, 'tp', 0, 0, tiled=True)]
  transfers between devices with their start and end apart: 4 -> 5, of which waited for: 4 -> 5; matrix products, arithmetic and copies ran while one was open for 0% -> 0% of each run, Pallas kernels for 0% -> 11%
where the time goes in v1:
time: 107 us; the launch traced here: 106 us
  blocking collectives  30.1 us (28%)
  starting transfers between devices  28.7 us (27%)
  Pallas kernels  24.6 us (23%)
  waiting for transfers between devices  20 us (19%)
  local copies, waits for them, and re-layouts  2.68 us (3%)
    all_to_all x2, blocking collectives, on_device(): lax.all_to_all(mine, 'tp', 0, 0, axis_index_groups=along_x, tiled=True)  18.8 us
    all_to_all x1, blocking collectives, on_device(): dots = lax.all_to_all(dots, 'tp', 0, 0, tiled=True)  11.3 us
    pallas_call x1, Pallas kernels, rank_rows(): pl.pallas_call(rows_kernel, grid=(tokens // TB,), in_specs=[pl.BlockSpec(...  10.8 us
    pallas_call x1, Pallas kernels, feature_shares(): pl.pallas_call(share_kernel, grid=(tokens // TB,), in_specs=[pl.BlockSpec...  10.7 us
    all_to_all x1, starting transfers between devices, on_device(): shares = lax.all_to_all(shares, 'tp', 0, 0, tiled=True)  10.4 us
    all_to_all x1, starting transfers between devices, on_device(): lax.all_to_all(everyone, 'grp', 0, 0, tiled=True)  8.37 us
    all_to_all x1, waiting for transfers between devices, on_device(): shares = lax.all_to_all(shares, 'tp', 0, 0, tiled=True)  7.77 us
    all_to_all x1, waiting for transfers between devices, on_device(): lax.all_to_all(everyone, 'grp', 0, 0, tiled=True)  6.51 us
  transfers between devices with their start and end apart: 5, of which 5 were waited for; matrix products, arithmetic and copies ran while one was open for 0% of the time, Pallas kernels for 11%

profile of v1, /device:TPU:1, one launch (start us, length us, event | category | flops | bytes accessed | tf_op | source)
XLA Modules:
  0.0 106.1 jit_solution(18396122226330053783)
XLA Ops:
  0.0 0.8 copy.7.a_ref
  0.8 0.0 copy-start.1
  0.9 0.7 copy-done.1
  1.6 0.0 copy-start.2
  1.6 10.8 %rank_rows.1 = (f32[4,16,1536]{2,1,0:T(8,128)S(1)}, f32[4,16,1536]{2,1,0:T(8,128)S(1)}) custom-call(s32[1]{0:T(128)} %bitcast.core_ref, bf16[6144,512]{1,0:T(8,128)(2,1)} %x_ref.3, bf16[6144,512]{1,0:T(8,128)(2,1)} %g_ref.3, bf16[512,16]{1,0:T(8,128)(2,1)S(1)} %copy.7.a_ref, bf16[16,512]{1,0:T(8,128)(2,1)S(1)} %copy-done.1), custom_call_target="tpu_custom_call" | custom-call | flops 201326592 | bytes 12582912 | tf_op jit(solution)/shard_map/rank_rows/pallas_call | solution.py:50
  12.3 0.0 copy-start
  12.3 3.3 %collective-permute-start = (f32[4,16,1536]{2,1,0:T(8,128)S(1)}, f32[4,16,1536]{2,1,0:T(8,128)S(1)}, u32[]{:S(2)}, u32[]{:S(2)}) collective-permute-start(f32[4,16,1536]{2,1,0:T(8,128)S(1)} %get-tuple-element.10), channel_id=1, source_target_pairs={{0,1},{1,0},{2,3},{3,2},{4,5},{5,4},{6,7},{7,6},{8,9},{9,8},{10,11... | collective-permute-start | bytes 1179656 | tf_op jit(solution)/shard_map/ppermute | solution.py:206
  15.7 1.3 %collective-permute-done = f32[4,16,1536]{2,1,0:T(8,128)S(1)} collective-permute-done((f32[4,16,1536]{2,1,0:T(8,128)S(1)}, f32[4,16,1536]{2,1,0:T(8,128)S(1)}, u32[]{:S(2)}, u32[]{:S(2)}) %collective-permute-start) | collective-permute-done | bytes 393248 | tf_op jit(solution)/shard_map/ppermute | solution.py:206
  17.0 0.1 add.11
  17.1 10.2 %all_to_all.25 = f32[4,16,1536]{2,1,0:T(8,128)S(1)} all-to-all(f32[4,16,1536]{2,1,0:T(8,128)S(1)} %add.11), channel_id=1, replica_groups={{0,2,4,6},{1,3,5,7},{8,10,12,14},{9,11,13,15},{16,18,20,22},{17,19,21,2..., dimensions={0} | all-to-all | bytes 786432 | tf_op jit(solution)/shard_map/all_to_all | solution.py:207
  27.3 2.1 %collective-permute-start.1 = (f32[16,1536]{1,0:T(8,128)S(1)}, f32[16,1536]{1,0:T(8,128)S(1)}, u32[]{:S(2)}, u32[]{:S(2)}) collective-permute-start(f32[16,1536]{1,0:T(8,128)S(1)} %reduce_sum.9), channel_id=1, source_target_pairs={{0,8},{1,9},{2,10},{3,11},{4,12},{5,13},{6,14},{7,15},{8,0},{9,1},... | collective-permute-start | bytes 294920 | tf_op jit(solution)/shard_map/ppermute | solution.py:209
  29.4 3.0 %collective-permute-done.1 = f32[16,1536]{1,0:T(8,128)S(1)} collective-permute-done((f32[16,1536]{1,0:T(8,128)S(1)}, f32[16,1536]{1,0:T(8,128)S(1)}, u32[]{:S(2)}, u32[]{:S(2)}) %collective-permute-start.1) | collective-permute-done | bytes 98336 | tf_op jit(solution)/shard_map/ppermute | solution.py:209
  32.4 8.6 %all_to_all.26.own_ref = f32[4,16,1536]{2,1,0:T(8,128)S(1)} all-to-all(f32[4,16,1536]{2,1,0:T(8,128)S(1)} %broadcast_in_dim.4), channel_id=1, replica_groups={{0,2,4,6},{1,3,5,7},{8,10,12,14},{9,11,13,15},{16,18,20,22},{17,19,21,2..., dimensions={0} | all-to-all | bytes 786432 | tf_op jit(solution)/shard_map/all_to_all | solution.py:211
  41.1 0.0 copy-done.2
  41.1 1.1 %broadcast_in_dim.5 = f32[16,32,512]{2,1,0:T(8,128)} broadcast(f32[32,512]{1,0:T(8,128)S(1)} %copy-done.2), dimensions={1,2} | broadcast | bytes 1114112 | tf_op jit(solution)/shard_map/broadcast_in_dim | solution.py:202
  42.2 8.4 %all-to-all-start.3 = ((f32[16,32,512]{2,1,0:T(8,128)}), f32[16,32,512]{2,1,0:T(8,128)S(1)}, u32[]{:S(2)}, u32[]{:S(2)}) async-start(f32[16,32,512]{2,1,0:T(8,128)} %broadcast_in_dim.5), calls=%async_computation.3 | async-start | bytes 2097152 | tf_op jit(solution)/shard_map/all_to_all | solution.py:203
  50.5 4.5 %collective-permute-start.2 = (f32[4,16,1536]{2,1,0:T(8,128)S(1)}, f32[4,16,1536]{2,1,0:T(8,128)S(1)}, u32[]{:S(2)}, u32[]{:S(2)}) collective-permute-start(f32[4,16,1536]{2,1,0:T(8,128)S(1)} %all_to_all.26.own_ref), channel_id=1, source_target_pairs={{0,1},{1,0},{2,3},{3,2},{4,5},{5,4},{6,7},{7,6},{8,9},{9,8},{10,11... | collective-permute-start | bytes 1179656 | tf_op jit(solution)/shard_map/ppermute | solution.py:212
  55.0 1.3 %collective-permute-done.2.other_ref = f32[4,16,1536]{2,1,0:T(8,128)S(1)} collective-permute-done((f32[4,16,1536]{2,1,0:T(8,128)S(1)}, f32[4,16,1536]{2,1,0:T(8,128)S(1)}, u32[]{:S(2)}, u32[]{:S(2)}) %collective-permute-start.2) | collective-permute-done | bytes 393248 | tf_op jit(solution)/shard_map/ppermute | solution.py:212
  56.4 0.0 copy-done
  56.4 10.7 %feature_shares.1 = f32[16,32,128]{2,1,0:T(8,128)} custom-call(s32[1]{0:T(128)} %bitcast.core_ref, bf16[6144,512]{1,0:T(8,128)(2,1)} %x_ref.3, bf16[6144,512]{1,0:T(8,128)(2,1)} %g_ref.3, f32[4,16,1536]{2,1,0:T(8,128)S(1)} %all_to_all.26.own_ref, f32[4,16,1536]{2,1,0:T(8,128)S(1)} %collective-permute-done.2.other_ref, s32[512,256]{1,0:T(8,128)S(1)} %copy-done), custom_call_target="tpu_custom_call" | custom-call | flops 402653184 | bytes 12582912 | tf_op jit(solution)/shard_map/feature_shares/pallas_call | solution.py:107
  67.1 6.5 %all-to-all-done.3 = f32[16,32,512]{2,1,0:T(8,128)S(1)} async-done(((f32[16,32,512]{2,1,0:T(8,128)}), f32[16,32,512]{2,1,0:T(8,128)S(1)}, u32[]{:S(2)}, u32[]{:S(2)}) %all-to-all-start.3) | async-done | bytes 1048608 | tf_op jit(solution)/shard_map/all_to_all | solution.py:203
  73.6 10.4 %all-to-all-start.2 = ((f32[16,32,128]{2,1,0:T(8,128)}), f32[16,32,128]{2,1,0:T(8,128)S(1)}, u32[]{:S(2)}, u32[]{:S(2)}) async-start(f32[16,32,128]{2,1,0:T(8,128)} %feature_shares.1), calls=%async_computation.2 | async-start | bytes 524288 | tf_op jit(solution)/shard_map/all_to_all | solution.py:216
  84.0 0.9 valid_terms.1
  85.0 7.8 %all-to-all-done.2.f_ref = f32[16,32,128]{2,1,0:T(8,128)S(1)} async-done(((f32[16,32,128]{2,1,0:T(8,128)}), f32[16,32,128]{2,1,0:T(8,128)S(1)}, u32[]{:S(2)}, u32[]{:S(2)}) %all-to-all-start.2) | async-done | bytes 262176 | tf_op jit(solution)/shard_map/all_to_all | solution.py:216
  92.7 0.6 partial_dots.1
  93.3 11.3 %all_to_all.27.p_ref = f32[16,8,128]{2,1,0:T(8,128)} all-to-all(f32[16,8,128]{2,1,0:T(8,128)S(1)} %partial_dots.1), channel_id=1, replica_groups=mesh['grp'=16,'tp'=16] {'tp'}, dimensions={0} | all-to-all | bytes 131072 | tf_op jit(solution)/shard_map/all_to_all | solution.py:218
  104.6 1.5 %scores.1 = f32[6,32]{1,0:T(8,128)} custom-call(f32[16,8,128]{2,1,0:T(8,128)} %all_to_all.27.p_ref), custom_call_target="tpu_custom_call" | custom-call | tf_op jit(solution)/shard_map/scores/pallas_call | solution.py:219
  (3 shorter events, 0.1 us)
Async XLA Ops:
  0.8 0.7 copy-start.1
  1.6 39.5 %copy-start.2 = (f32[32,512]{1,0:T(8,128)S(1)}, f32[32,512]{1,0:T(8,128)}, u32[]{:S(2)}) copy-start(f32[32,512]{1,0:T(8,128)} %param.11) | copy-start | bytes 196612
  12.3 44.0 %copy-start = (s32[512,256]{1,0:T(8,128)S(1)}, s32[512,256]{1,0:T(8,128)}, u32[]{:S(2)}) copy-start(s32[512,256]{1,0:T(8,128)} %s_ref.1) | copy-start | bytes 1572868
  12.3 4.7 %collective-permute-start = (f32[4,16,1536]{2,1,0:T(8,128)S(1)}, f32[4,16,1536]{2,1,0:T(8,128)S(1)}, u32[]{:S(2)}, u32[]{:S(2)}) collective-permute-start(f32[4,16,1536]{2,1,0:T(8,128)S(1)} %get-tuple-element.10), channel_id=1, source_target_pairs={{0,1},{1,0},{2,3},{3,2},{4,5},{5,4},{6,7},{7,6},{8,9},{9,8},{10,11... | collective-permute-start | bytes 1179656 | tf_op jit(solution)/shard_map/ppermute | solution.py:206
  27.3 5.1 %collective-permute-start.1 = (f32[16,1536]{1,0:T(8,128)S(1)}, f32[16,1536]{1,0:T(8,128)S(1)}, u32[]{:S(2)}, u32[]{:S(2)}) collective-permute-start(f32[16,1536]{1,0:T(8,128)S(1)} %reduce_sum.9), channel_id=1, source_target_pairs={{0,8},{1,9},{2,10},{3,11},{4,12},{5,13},{6,14},{7,15},{8,0},{9,1},... | collective-permute-start | bytes 294920 | tf_op jit(solution)/shard_map/ppermute | solution.py:209
  42.2 31.5 %all-to-all-start.3 = ((f32[16,32,512]{2,1,0:T(8,128)}), f32[16,32,512]{2,1,0:T(8,128)S(1)}, u32[]{:S(2)}, u32[]{:S(2)}) async-start(f32[16,32,512]{2,1,0:T(8,128)} %broadcast_in_dim.5), calls=%async_computation.3 | async-start | bytes 2097152 | tf_op jit(solution)/shard_map/all_to_all | solution.py:203
  50.5 5.8 %collective-permute-start.2 = (f32[4,16,1536]{2,1,0:T(8,128)S(1)}, f32[4,16,1536]{2,1,0:T(8,128)S(1)}, u32[]{:S(2)}, u32[]{:S(2)}) collective-permute-start(f32[4,16,1536]{2,1,0:T(8,128)S(1)} %all_to_all.26.own_ref), channel_id=1, source_target_pairs={{0,1},{1,0},{2,3},{3,2},{4,5},{5,4},{6,7},{7,6},{8,9},{9,8},{10,11... | collective-permute-start | bytes 1179656 | tf_op jit(solution)/shard_map/ppermute | solution.py:212
  73.6 19.1 %all-to-all-start.2 = ((f32[16,32,128]{2,1,0:T(8,128)}), f32[16,32,128]{2,1,0:T(8,128)S(1)}, u32[]{:S(2)}, u32[]{:S(2)}) async-start(f32[16,32,128]{2,1,0:T(8,128)} %feature_shares.1), calls=%async_computation.2 | async-start | bytes 524288 | tf_op jit(solution)/shard_map/all_to_all | solution.py:216

commit v2 on v1

v2 whole, which is shorter than its diff:
```python
import functools
import math

import jax
import jax.numpy as jnp
from jax import lax
from jax.experimental import pallas as pl
from jax.experimental.pallas import tpu as pltpu
from jax.sharding import PartitionSpec as P

LEN = 1024
K = 8192
TB = 512
EPS = 1e-06
VMEM = 20 * 1024 * 1024
STEPS = (2, 2, 2, 2, 2, 1, 1)

NT = (((1,), (1,)), ((), ()))
NN = (((1,), (0,)), ((), ()))


def mm(a, b, dims):
    return lax.dot_general(a, b, dims, preferred_element_type=jnp.float32)


def halves(a):
    hi = a.astype(jnp.bfloat16)
    lo = (a - hi.astype(jnp.float32)).astype(jnp.bfloat16)
    return jnp.concatenate([hi, lo], 0)


def rows_kernel(steps, where_ref, x_ref, g_ref, a_ref, b_ref, keep_ref, send_ref, xs_ref, gs_ref, at_ref, bs_ref, sem, sem_w):
    first = where_ref[0] == 0
    per = keep_ref.shape[2] // TB
    weights = [
        pltpu.make_async_copy(src, dst, sem_w.at[j])
        for j, (src, dst) in enumerate(((a_ref, at_ref), (b_ref, bs_ref)))
    ]
    for copy in weights:
        copy.start()
    copies, start = [], 0
    for c, blocks in enumerate(steps):
        rows = pl.ds(start * TB, blocks * TB)
        pair = [
            pltpu.make_async_copy(src.at[rows], dst.at[rows], sem.at[j, c])
            for j, (src, dst) in enumerate(((x_ref, xs_ref), (g_ref, gs_ref)))
        ]
        for copy in pair:
            copy.start()
        copies.append((start, blocks, pair))
        start += blocks
    for copy in weights:
        copy.wait()
    for start, blocks, pair in copies:
        for copy in pair:
            copy.wait()
        for i in range(start, start + blocks):
            rows = slice(i * TB, (i + 1) * TB)
            cols = slice(i % per * TB, (i % per + 1) * TB)
            down = mm(at_ref[...], xs_ref[rows], NT)
            up = mm(bs_ref[...], gs_ref[rows], NT)
            slot = (i // per - where_ref[2]) & 3
            keep_ref[slot, :, cols] = jnp.where(first, down, up)
            send_ref[slot, :, cols] = jnp.where(first, up, down)


def rank_rows(where, x, g, a, b):
    tokens, width = x.shape
    rank = b.shape[0]
    chunk = tokens // 4
    steps = STEPS
    out = jax.ShapeDtypeStruct((4, rank, chunk), jnp.float32)
    near = pltpu.VMEM((tokens, width), jnp.bfloat16)
    whole = pl.BlockSpec(memory_space=pltpu.VMEM)
    far = pl.BlockSpec(memory_space=pl.ANY)
    x, g, a, b = (pltpu.with_memory_space_constraint(v, pltpu.HBM) for v in (x, g, a, b))
    return pl.pallas_call(
        functools.partial(rows_kernel, steps),
        in_specs=[pl.BlockSpec(memory_space=pltpu.SMEM), far, far, far, far],
        out_specs=[whole] * 4,
        out_shape=[out, out, near, near],
        scratch_shapes=[
            pltpu.VMEM((rank, width), jnp.bfloat16),
            pltpu.VMEM((rank, width), jnp.bfloat16),
            pltpu.SemaphoreType.DMA((2, len(steps))),
            pltpu.SemaphoreType.DMA((2,)),
        ],
        compiler_params=pltpu.CompilerParams(vmem_limit_bytes=VMEM),
        cost_estimate=pl.CostEstimate(
            flops=4 * tokens * width * rank, bytes_accessed=4 * tokens * width, transcendentals=0
        ),
        name="rank_rows",
    )(where, x, g, a, b)


def share_kernel(where_ref, x_ref, g_ref, *refs):
    own_refs, (other_ref, s_ref, out_ref, v_ref) = refs[:4], refs[4:]
    rank, chunk = own_refs[0].shape
    per = chunk // TB
    first = where_ref[0] == 0
    for j, own_ref in enumerate(own_refs):
        begin = ((where_ref[2] - j) & 3) * per
        for c in range(per):
            rows = pl.ds(pl.multiple_of((begin + c) * TB, TB), TB)
            cols = slice(c * TB, (c + 1) * TB)
            own, other = own_ref[:, cols], other_ref[j, :, cols]
            a = mm(halves(jnp.where(first, other, own)), x_ref[rows], NN)
            b = mm(halves(jnp.where(first, own, other)), g_ref[rows], NN)
            v_ref[0, begin + c] = a[:rank] + a[rank:]
            v_ref[1, begin + c] = b[:rank] + b[rank:]
    sign = (2 * s_ref[...] - 1).astype(jnp.float32).astype(jnp.bfloat16)
    each = out_ref.shape[0] // 2
    blocks, step = v_ref.shape[1], LEN // TB
    pad = jnp.zeros((128 - blocks // step * rank, x_ref.shape[1]), jnp.float32)
    for m in range(2):
        v = [sum(v_ref[m, i + k] for k in range(step)) for i in range(0, blocks, step)]
        f = mm(halves(jnp.concatenate(v + [pad], 0)), sign, NN)
        f = jnp.transpose(f[:128] + f[128:])
        out_ref[m * each : (m + 1) * each] = f.reshape(each, -1, 128)


def feature_shares(where, x, g, own, other, bits, parts):
    tokens, width = x.shape
    rank = own[0].shape[0]
    kd = bits.shape[1]
    whole = pl.BlockSpec(memory_space=pltpu.VMEM)
    x, g = (pltpu.with_memory_space_constraint(v, pltpu.VMEM) for v in (x, g))
    return pl.pallas_call(
        share_kernel,
        in_specs=[pl.BlockSpec(memory_space=pltpu.SMEM)] + [whole] * (len(own) + 4),
        out_specs=whole,
        out_shape=jax.ShapeDtypeStruct((parts, 2 * kd // parts, 128), jnp.float32),
        scratch_shapes=[pltpu.VMEM((2, tokens // TB, rank, width), jnp.float32)],
        compiler_params=pltpu.CompilerParams(vmem_limit_bytes=VMEM),
        cost_estimate=pl.CostEstimate(
            flops=8 * tokens * width * rank, bytes_accessed=4 * tokens * width, transcendentals=0
        ),
        name="feature_shares",
    )(where, x, g, *own, other, bits)


def valid_kernel(rank, near_ref, far_ref, hl_ref, sq_ref):
    v = jnp.concatenate([near_ref[...], far_ref[...]], 0)
    rows, cols = v.shape
    ks = cols // rank
    came = lax.broadcasted_iota(jnp.int32, (cols, cols), 0)
    goes = lax.broadcasted_iota(jnp.int32, (cols, cols), 1)
    move = jnp.where((came % rank) * ks + came // rank == goes, 1.0, 0.0).astype(jnp.bfloat16)
    hl_ref[...] = mm(halves(v), move, NN).astype(jnp.bfloat16)
    sq = halves(v * v)
    total = mm(jnp.ones((8, cols), jnp.bfloat16), sq, NT)
    sq_ref[...] = total[:, :rows] + total[:, rows:]


def valid_terms(near, far, rank):
    rows, cols = 2 * near.shape[0], near.shape[1]
    return pl.pallas_call(
        functools.partial(valid_kernel, rank),
        out_shape=[
            jax.ShapeDtypeStruct((2 * rows, cols), jnp.bfloat16),
            jax.ShapeDtypeStruct((8, rows), jnp.float32),
        ],
        compiler_params=pltpu.CompilerParams(vmem_limit_bytes=VMEM),
        cost_estimate=pl.CostEstimate(
            flops=4 * rows * cols * cols, bytes_accessed=8 * rows * cols, transcendentals=0
        ),
        name="valid_terms",
    )(near, far)


def flip(step, z, y):
    if step == 0:
        return z ^ 4, y
    if step == 1:
        return z ^ 1, y
    if step == 2:
        return z, y ^ 1
    return (z + 2 * (z & 1) - 1) & 7, y


def flips(step):
    pairs = []
    for i in range(16):
        z, y = flip(step, i >> 1, i & 1)
        pairs.append((i, z * 2 + y))
    return pairs


def origin(place, index):
    z, y = index >> 1, index & 1
    for step in (3, 2, 1, 0):
        if place >> step & 1:
            z, y = flip(step, z, y)
    return z * 2 + y


def dot_kernel(rank, where_ref, f_ref, hl_ref, sq_ref, out_ref, t_ref):
    parts = f_ref.shape[0]
    rows = sq_ref.shape[1]
    each = rows // parts
    t_ref[...] = jnp.transpose(jnp.sum(f_ref[...], 0))
    f = jnp.concatenate([t_ref[pl.ds(r, 8, stride=rank), :] for r in range(rank)], 1)
    prod = mm(halves(f), hl_ref[...], NT)
    dots = prod[:8, :rows] + (prod[8:, :rows] + prod[:8, rows:]) + prod[8:, rows:]
    line = lax.broadcasted_iota(jnp.int32, dots.shape, 0)
    dots = jnp.where(line == 6, sq_ref[...], dots)
    own_sq = jnp.broadcast_to(jnp.sum(f * f, 1, keepdims=True), (8, each))
    for place in range(parts):
        part = origin(place, where_ref[1])
        out_ref[part, :, :each] = dots[:, place * each : (place + 1) * each]
        out_ref[part, :, each : 2 * each] = own_sq


def partial_dots(where, f, hl, sq, rank):
    whole = pl.BlockSpec(memory_space=pltpu.VMEM)
    return pl.pallas_call(
        functools.partial(dot_kernel, rank),
        in_specs=[pl.BlockSpec(memory_space=pltpu.SMEM), whole, whole, whole],
        out_shape=jax.ShapeDtypeStruct((f.shape[0], 8, 128), jnp.float32),
        scratch_shapes=[pltpu.VMEM((128, f.shape[1]), jnp.float32)],
        compiler_params=pltpu.CompilerParams(vmem_limit_bytes=VMEM),
        name="partial_dots",
    )(where, f, hl, sq)


def on_device(x, g, a, b, bits, valid):
    tp = lax.axis_size("tp")
    rank = b.shape[0]
    seqs = x.shape[0] // LEN
    each = 16 * valid.shape[0] // tp
    index = lax.axis_index("tp")
    where = jnp.stack([index & 1, lax.axis_index("grp"), index >> 1 & 3]).astype(jnp.int32)
    swap_core = [(i, i ^ 1) for i in range(tp)]
    swap_y = [(i, i ^ 8) for i in range(tp)]
    turn_x = [[(i, (i & 9) | (((i >> 1) + k & 3) << 1)) for i in range(tp)] for k in range(4)]

    def gather(step, rows, after):
        rows, after = lax.optimization_barrier((rows, after))
        return rows, lax.ppermute(rows, "grp", flips(step)), after

    keep, send, x, g = rank_rows(where, x, g, jnp.transpose(a), b)
    near, far, send = gather(0, valid, send)
    mine = keep + lax.ppermute(send, "tp", swap_core)
    came = [lax.ppermute(mine[k], "tp", turn_x[k]) for k in (1, 2, 3)]
    mine = mine[0] + came[0] + came[1] + came[2]
    near, far, mine = gather(1, jnp.concatenate([near, far], 0), mine)
    mine = mine + lax.ppermute(mine, "tp", swap_y)
    near, far, mine = gather(2, jnp.concatenate([near, far], 0), mine)
    own = [mine] + [lax.ppermute(mine, "tp", turn_x[k]) for k in (1, 2, 3)]
    near, far, own = gather(3, jnp.concatenate([near, far], 0), own)
    other = lax.ppermute(jnp.stack(own), "tp", swap_core)

    shares = feature_shares(where, x, g, own, other, bits, tp)
    hl, sq = valid_terms(near, far, rank)
    shares = lax.all_to_all(shares, "tp", 0, 0, tiled=True)
    dots = partial_dots(where, shares, hl, sq, rank)
    dots = lax.all_to_all(dots, "tp", 0, 0, tiled=True)
    total = jnp.sum(dots, 0)
    train = math.sqrt(K) / jnp.sqrt(total[:seqs, each : 2 * each] + EPS)
    return total[:seqs, :each] * train / jnp.sqrt(total[6:7, :each] + EPS)


def solution(mesh):
    return jax.shard_map(
        on_device,
        mesh=mesh,
        in_specs=(
            P("grp", "tp"),
            P("grp", "tp"),
            P("tp", None),
            P(None, "tp"),
            P("tp", None),
            P("grp", "tp"),
        ),
        out_specs=P("grp", "tp"),
        check_vma=False,
    )
```

time: 107 us -> 77.6 us (0.73)
  blocking collectives: 30.1 us -> 10.6 us
  Pallas kernels: 24.6 us -> 14.8 us
  starting transfers between devices: 28.7 us -> 31.5 us
  local copies, waits for them, and re-layouts: 2.68 us -> 0.03 us
    all_to_all x2 -> x0, blocking collectives: 18.8 us -> none  [on_device(): lax.all_to_all(mine, 'tp', 0, 0, axis_index_groups=along_x, tiled=True)]
    ppermute x1 -> x11, starting transfers between devices: 4.48 us -> 19.8 us  [the longest x4 7.41 us: gather(): return (rows, lax.ppermute(rows, 'grp', flips(step)), after)]
    ppermute x1 -> x11, waiting for transfers between devices: 1.35 us -> 13.8 us  [the longest x4 5.64 us: gather(): return (rows, lax.ppermute(rows, 'grp', flips(step)), after)]
    pallas_call x4 -> x3, Pallas kernels: 23.6 us -> 13.9 us  [the longest x1 9.19 us: rank_rows(): pl.pallas_call(functools.partial(rows_kernel, steps), in_specs=[pl.BlockS...]
    all_to_all x1 -> x0, starting transfers between devices: 8.37 us -> none  [on_device(): lax.all_to_all(everyone, 'grp', 0, 0, tiled=True)]
    all_to_all x1 -> x0, waiting for transfers between devices: 6.51 us -> none  [on_device(): lax.all_to_all(everyone, 'grp', 0, 0, tiled=True)]
    all_to_all x1, starting transfers between devices: 10.4 us -> 5.53 us  [on_device(): shares = lax.all_to_all(shares, 'tp', 0, 0, tiled=True)]
    all_to_all x1, waiting for transfers between devices: 7.77 us -> 3.52 us  [on_device(): shares = lax.all_to_all(shares, 'tp', 0, 0, tiled=True)]
  transfers between devices with their start and end apart: 5 -> 14, of which waited for: 5 -> 9; matrix products, arithmetic and copies ran while one was open for 0% -> 0% of each run, Pallas kernels for 11% -> 6%
where the time goes in v2:
time: 77.6 us; the launch traced here: 77.4 us
  starting transfers between devices  31.5 us (41%)
  waiting for transfers between devices  19.3 us (25%)
  Pallas kernels  14.8 us (19%)
  blocking collectives  10.6 us (14%)
  other arithmetic  0.95 us (1%)
    all_to_all x1, blocking collectives, on_device(): dots = lax.all_to_all(dots, 'tp', 0, 0, tiled=True)  10.6 us
    pallas_call x1, Pallas kernels, rank_rows(): pl.pallas_call(functools.partial(rows_kernel, steps), in_specs=[pl.BlockS...  9.19 us
    ppermute x4, starting transfers between devices, gather(): return (rows, lax.ppermute(rows, 'grp', flips(step)), after)  7.41 us
    ppermute x4, waiting for transfers between devices, gather(): return (rows, lax.ppermute(rows, 'grp', flips(step)), after)  5.64 us
    all_to_all x1, starting transfers between devices, on_device(): shares = lax.all_to_all(shares, 'tp', 0, 0, tiled=True)  5.53 us
    ppermute x1, starting transfers between devices, on_device(): other = lax.ppermute(jnp.stack(own), 'tp', swap_core)  5.05 us
    ppermute x3, starting transfers between devices, on_device(): came = [lax.ppermute(mine[k], 'tp', turn_x[k]) for k in (1, 2, 3)]  4.29 us
    pallas_call x1, Pallas kernels, feature_shares(): pl.pallas_call(share_kernel, in_specs=[pl.BlockSpec(memory_space=pltpu.SM...  3.57 us
  transfers between devices with their start and end apart: 14, of which 9 were waited for; matrix products, arithmetic and copies ran while one was open for 0% of the time, Pallas kernels for 6%

profile of v2, /device:TPU:1, one launch (start us, length us, event | category | flops | bytes accessed | tf_op | source)
XLA Modules:
  0.0 77.4 jit_solution(4869507437977277849)
XLA Ops:
  0.0 0.1 pad_add_fusion.where_ref
  0.1 0.0 copy-start.1
  0.1 0.0 copy-start
  0.1 9.2 %rank_rows.1 = (f32[4,16,1536]{2,1,0:T(8,128)S(1)}, f32[4,16,1536]{2,1,0:T(8,128)S(1)}, bf16[6144,512]{1,0:T(8,128)(2,1)S(1)}, bf16[6144,512]{1,0:T(8,128)(2,1)S(1)}) custom-call(s32[3]{0:T(128)S(1)} %pad_add_fusion.where_ref, bf16[6144,512]{1,0:T(8,128)(2,1)} %x_ref.1, bf16[6144,512]{1,0:T(8,128)(2,1)} %g_ref.1, bf16[16,512]{1,0:T(8,128)(2,1)} %bitcast.28, ...), custom_call_target="tpu_custom_call" | custom-call | flops 201326592 | bytes 12582912 | tf_op jit(solution)/shard_map/rank_rows/pallas_call | solution.py:77
  9.3 3.3 %collective-permute-start.1 = (f32[4,16,1536]{2,1,0:T(8,128)S(1)}, f32[4,16,1536]{2,1,0:T(8,128)S(1)}, u32[]{:S(2)}, u32[]{:S(2)}) collective-permute-start(f32[4,16,1536]{2,1,0:T(8,128)S(1)} %get-tuple-element.27), channel_id=1, source_target_pairs={{0,1},{1,0},{2,3},{3,2},{4,5},{5,4},{6,7},{7,6},{8,9},{9,8},{10,11... | collective-permute-start | bytes 1179656 | tf_op jit(solution)/shard_map/ppermute | solution.py:243
  12.6 0.0 copy-done.1
  12.6 5.2 %collective-permute-start = (f32[32,512]{1,0:T(8,128)S(1)}, f32[32,512]{1,0:T(8,128)S(1)}, u32[]{:S(2)}, u32[]{:S(2)}) collective-permute-start(f32[32,512]{1,0:T(8,128)S(1)} %copy-done.1), channel_id=1, source_target_pairs={{0,128},{16,144},{32,160},{48,176},{64,192},{80,208},{96,224},{112... | collective-permute-start | bytes 196616 | tf_op jit(solution)/shard_map/ppermute | solution.py:239
  17.8 0.0 collective-permute-done.1
  17.9 1.3 %collective-permute-start.2 = (f32[16,1536]{1,0:T(8,128)S(1)}, f32[16,1536]{1,0:T(8,128)S(1)}, u32[]{:S(2)}, u32[]{:S(2)}) collective-permute-start(f32[16,1536]{1,0:T(8,128)S(1)} %get-tuple-element.39), channel_id=1, source_target_pairs={{0,2},{1,3},{2,4},{3,5},{4,6},{5,7},{6,0},{7,1},{8,10},{9,11},{10,... | collective-permute-start | bytes 294920 | tf_op jit(solution)/shard_map/ppermute | solution.py:244
  19.2 1.5 %collective-permute-start.4 = (f32[16,1536]{1,0:T(8,128)S(1)}, f32[16,1536]{1,0:T(8,128)S(1)}, u32[]{:S(2)}, u32[]{:S(2)}) collective-permute-start(f32[16,1536]{1,0:T(8,128)S(1)} %get-tuple-element.40), channel_id=1, source_target_pairs={{0,6},{1,7},{2,0},{3,1},{4,2},{5,3},{6,4},{7,5},{8,14},{9,15},{10,... | collective-permute-start | bytes 294920 | tf_op jit(solution)/shard_map/ppermute | solution.py:244
  20.6 1.5 %collective-permute-start.3 = (f32[16,1536]{1,0:T(8,128)S(1)}, f32[16,1536]{1,0:T(8,128)S(1)}, u32[]{:S(2)}, u32[]{:S(2)}) collective-permute-start(f32[16,1536]{1,0:T(8,128)S(1)} %get-tuple-element.41), channel_id=1, source_target_pairs={{0,4},{1,5},{2,6},{3,7},{4,0},{5,1},{6,2},{7,3},{8,12},{9,13},{10,... | collective-permute-start | bytes 294920 | tf_op jit(solution)/shard_map/ppermute | solution.py:244
  22.2 0.0 collective-permute-done
  22.2 1.0 %collective-permute-done.2 = f32[16,1536]{1,0:T(8,128)S(1)} collective-permute-done((f32[16,1536]{1,0:T(8,128)S(1)}, f32[16,1536]{1,0:T(8,128)S(1)}, u32[]{:S(2)}, u32[]{:S(2)}) %collective-permute-start.2) | collective-permute-done | bytes 98336 | tf_op jit(solution)/shard_map/ppermute | solution.py:244
  23.2 0.0 collective-permute-done.4
  23.2 2.5 %collective-permute-done.3 = f32[16,1536]{1,0:T(8,128)S(1)} collective-permute-done((f32[16,1536]{1,0:T(8,128)S(1)}, f32[16,1536]{1,0:T(8,128)S(1)}, u32[]{:S(2)}, u32[]{:S(2)}) %collective-permute-start.3) | collective-permute-done | bytes 98336 | tf_op jit(solution)/shard_map/ppermute | solution.py:244
  25.8 0.8 %collective-permute-start.5 = (f32[64,512]{1,0:T(8,128)S(1)}, f32[64,512]{1,0:T(8,128)S(1)}, u32[]{:S(2)}, u32[]{:S(2)}) collective-permute-start(f32[64,512]{1,0:T(8,128)S(1)} %pad_maximum_fusion.3), channel_id=1, source_target_pairs={{0,32},{16,48},{32,0},{48,16},{64,96},{80,112},{96,64},{112,80},{1... | collective-permute-start | bytes 393224 | tf_op jit(solution)/shard_map/ppermute | solution.py:239
  26.6 2.9 %collective-permute-start.6 = (f32[16,1536]{1,0:T(8,128)S(1)}, f32[16,1536]{1,0:T(8,128)S(1)}, u32[]{:S(2)}, u32[]{:S(2)}) collective-permute-start(f32[16,1536]{1,0:T(8,128)S(1)} %fusion.2), channel_id=1, source_target_pairs={{0,8},{1,9},{2,10},{3,11},{4,12},{5,13},{6,14},{7,15},{8,0},{9,1},... | collective-permute-start | bytes 294920 | tf_op jit(solution)/shard_map/ppermute | solution.py:247
  29.5 2.1 %collective-permute-done.6 = f32[16,1536]{1,0:T(8,128)S(1)} collective-permute-done((f32[16,1536]{1,0:T(8,128)S(1)}, f32[16,1536]{1,0:T(8,128)S(1)}, u32[]{:S(2)}, u32[]{:S(2)}) %collective-permute-start.6) | collective-permute-done | bytes 98336 | tf_op jit(solution)/shard_map/ppermute | solution.py:247
  31.6 0.0 collective-permute-done.5
  31.6 1.4 %collective-permute-start.7 = (f32[128,512]{1,0:T(8,128)S(1)}, f32[128,512]{1,0:T(8,128)S(1)}, u32[]{:S(2)}, u32[]{:S(2)}) collective-permute-start(f32[128,512]{1,0:T(8,128)S(1)} %pad_maximum_fusion.2), channel_id=1, source_target_pairs={{0,16},{16,0},{32,48},{48,32},{64,80},{80,64},{96,112},{112,96},{1... | collective-permute-start | bytes 786440 | tf_op jit(solution)/shard_map/ppermute | solution.py:239
  33.0 1.5 %collective-permute-start.10 = (f32[16,1536]{1,0:T(8,128)S(1)}, f32[16,1536]{1,0:T(8,128)S(1)}, u32[]{:S(2)}, u32[]{:S(2)}) collective-permute-start(f32[16,1536]{1,0:T(8,128)S(1)} %add.31.refs_0_), channel_id=1, source_target_pairs={{0,6},{1,7},{2,0},{3,1},{4,2},{5,3},{6,4},{7,5},{8,14},{9,15},{10,... | collective-permute-start | bytes 294920 | tf_op jit(solution)/shard_map/ppermute | solution.py:249
  34.5 1.5 %collective-permute-start.9 = (f32[16,1536]{1,0:T(8,128)S(1)}, f32[16,1536]{1,0:T(8,128)S(1)}, u32[]{:S(2)}, u32[]{:S(2)}) collective-permute-start(f32[16,1536]{1,0:T(8,128)S(1)} %add.31.refs_0_), channel_id=1, source_target_pairs={{0,4},{1,5},{2,6},{3,7},{4,0},{5,1},{6,2},{7,3},{8,12},{9,13},{10,... | collective-permute-start | bytes 294920 | tf_op jit(solution)/shard_map/ppermute | solution.py:249
  36.0 0.0 collective-permute-start.8
  36.0 1.4 %collective-permute-done.7 = f32[128,512]{1,0:T(8,128)S(1)} collective-permute-done((f32[128,512]{1,0:T(8,128)S(1)}, f32[128,512]{1,0:T(8,128)S(1)}, u32[]{:S(2)}, u32[]{:S(2)}) %collective-permute-start.7) | collective-permute-done | bytes 262176 | tf_op jit(solution)/shard_map/ppermute | solution.py:239
  37.4 0.0 collective-permute-done.10.refs_3_
  37.4 2.0 %collective-permute-done.9.refs_2_ = f32[16,1536]{1,0:T(8,128)S(1)} collective-permute-done((f32[16,1536]{1,0:T(8,128)S(1)}, f32[16,1536]{1,0:T(8,128)S(1)}, u32[]{:S(2)}, u32[]{:S(2)}) %collective-permute-start.9) | collective-permute-done | bytes 98336 | tf_op jit(solution)/shard_map/ppermute | solution.py:249
  39.5 1.2 %collective-permute-done.8.refs_1_ = f32[16,1536]{1,0:T(8,128)S(1)} collective-permute-done((f32[16,1536]{1,0:T(8,128)S(1)}, f32[16,1536]{1,0:T(8,128)S(1)}, u32[]{:S(2)}, u32[]{:S(2)}) %collective-permute-start.8) | collective-permute-done | bytes 98336 | tf_op jit(solution)/shard_map/ppermute | solution.py:249
  40.7 5.0 %collective-permute-start.11 = (f32[4,16,1536]{2,1,0:T(8,128)S(1)}, f32[4,16,1536]{2,1,0:T(8,128)S(1)}, u32[]{:S(2)}, u32[]{:S(2)}) collective-permute-start(f32[4,16,1536]{2,1,0:T(8,128)S(1)} %pad_maximum_fusion.1), channel_id=1, source_target_pairs={{0,1},{1,0},{2,3},{3,2},{4,5},{5,4},{6,7},{7,6},{8,9},{9,8},{10,11... | collective-permute-start | bytes 1179656 | tf_op jit(solution)/shard_map/ppermute | solution.py:251
  45.8 0.0 collective-permute-start.12
  45.8 1.3 %collective-permute-done.11.refs_4_ = f32[4,16,1536]{2,1,0:T(8,128)S(1)} collective-permute-done((f32[4,16,1536]{2,1,0:T(8,128)S(1)}, f32[4,16,1536]{2,1,0:T(8,128)S(1)}, u32[]{:S(2)}, u32[]{:S(2)}) %collective-permute-start.11) | collective-permute-done | bytes 393248 | tf_op jit(solution)/shard_map/ppermute | solution.py:251
  47.1 0.0 copy-done
  47.1 3.6 %feature_shares.1 = f32[16,32,128]{2,1,0:T(8,128)} custom-call(s32[3]{0:T(128)S(1)} %pad_add_fusion.where_ref, bf16[6144,512]{1,0:T(8,128)(2,1)S(1)} %get-tuple-element.22.x_ref, bf16[6144,512]{1,0:T(8,128)(2,1)S(1)} %get-tuple-element.23.g_ref, f32[16,1536]{1,0:T(8,128)S(1)} %add.31.refs_0_, f32[16,1536]{1,0:T(8,128)S(1)} %collective-permute-done.8.refs_1_, ...), custom_call_target="tpu_custom_call" | custom-call | flops 402653184 | bytes 12582912 | tf_op jit(solution)/shard_map/feature_shares/pallas_call | solution.py:128
  50.7 5.5 %all-to-all-start = ((f32[16,32,128]{2,1,0:T(8,128)}), f32[16,32,128]{2,1,0:T(8,128)S(1)}, u32[]{:S(2)}, u32[]{:S(2)}) async-start(f32[16,32,128]{2,1,0:T(8,128)} %feature_shares.1), calls=%async_computation | async-start | bytes 524288 | tf_op jit(solution)/shard_map/all_to_all | solution.py:255
  56.2 4.2 %collective-permute-done.12.far_ref = f32[256,512]{1,0:T(8,128)S(1)} collective-permute-done((f32[256,512]{1,0:T(8,128)S(1)}, f32[256,512]{1,0:T(8,128)S(1)}, u32[]{:S(2)}, u32[]{:S(2)}) %collective-permute-start.12) | collective-permute-done | bytes 524320 | tf_op jit(solution)/shard_map/ppermute | solution.py:239
  60.5 0.9 %valid_terms.1 = (bf16[1024,512]{1,0:T(8,128)(2,1)S(1)}, f32[8,512]{1,0:T(8,128)S(1)}) custom-call(f32[256,512]{1,0:T(8,128)S(1)} %pad_maximum_fusion.near_ref, f32[256,512]{1,0:T(8,128)S(1)} %collective-permute-done.12.far_ref), custom_call_target="tpu_custom_call" | custom-call | flops 536870912 | bytes 2097152 | tf_op jit(solution)/shard_map/valid_terms/pallas_call | solution.py:157
  61.4 3.5 %all-to-all-done.f_ref = f32[16,32,128]{2,1,0:T(8,128)S(1)} async-done(((f32[16,32,128]{2,1,0:T(8,128)}), f32[16,32,128]{2,1,0:T(8,128)S(1)}, u32[]{:S(2)}, u32[]{:S(2)}) %all-to-all-start) | async-done | bytes 262176 | tf_op jit(solution)/shard_map/all_to_all | solution.py:255
  64.9 1.1 %partial_dots.1 = f32[16,8,128]{2,1,0:T(8,128)S(1)} custom-call(s32[3]{0:T(128)S(1)} %pad_add_fusion.where_ref, f32[16,32,128]{2,1,0:T(8,128)S(1)} %all-to-all-done.f_ref, bf16[1024,512]{1,0:T(8,128)(2,1)S(1)} %get-tuple-element.37.hl_ref, f32[8,512]{1,0:T(8,128)S(1)} %get-tuple-element.38.sq_ref), custom_call_target="tpu_custom_call" | custom-call | tf_op jit(solution)/shard_map/partial_dots/pallas_call | solution.py:216
  66.0 10.6 %all_to_all.10 = f32[16,8,128]{2,1,0:T(8,128)S(1)} all-to-all(f32[16,8,128]{2,1,0:T(8,128)S(1)} %partial_dots.1), channel_id=1, replica_groups=mesh['grp'=16,'tp'=16] {'tp'}, dimensions={0} | all-to-all | bytes 131072 | tf_op jit(solution)/shard_map/all_to_all | solution.py:257
  76.7 0.7 multiply_divide_fusion
  (10 shorter events, 0.2 us)
Async XLA Ops:
  0.1 12.5 %copy-start.1 = (f32[32,512]{1,0:T(8,128)S(1)}, f32[32,512]{1,0:T(8,128)}, u32[]{:S(2)}) copy-start(f32[32,512]{1,0:T(8,128)} %param.11) | copy-start | bytes 196612
  0.1 47.0 %copy-start = (s32[512,256]{1,0:T(8,128)S(1)}, s32[512,256]{1,0:T(8,128)}, u32[]{:S(2)}) copy-start(s32[512,256]{1,0:T(8,128)} %refs_5_.1) | copy-start | bytes 1572868
  9.3 8.5 %collective-permute-start.1 = (f32[4,16,1536]{2,1,0:T(8,128)S(1)}, f32[4,16,1536]{2,1,0:T(8,128)S(1)}, u32[]{:S(2)}, u32[]{:S(2)}) collective-permute-start(f32[4,16,1536]{2,1,0:T(8,128)S(1)} %get-tuple-element.27), channel_id=1, source_target_pairs={{0,1},{1,0},{2,3},{3,2},{4,5},{5,4},{6,7},{7,6},{8,9},{9,8},{10,11... | collective-permute-start | bytes 1179656 | tf_op jit(solution)/shard_map/ppermute | solution.py:243
  12.6 9.6 %collective-permute-start = (f32[32,512]{1,0:T(8,128)S(1)}, f32[32,512]{1,0:T(8,128)S(1)}, u32[]{:S(2)}, u32[]{:S(2)}) collective-permute-start(f32[32,512]{1,0:T(8,128)S(1)} %copy-done.1), channel_id=1, source_target_pairs={{0,128},{16,144},{32,160},{48,176},{64,192},{80,208},{96,224},{112... | collective-permute-start | bytes 196616 | tf_op jit(solution)/shard_map/ppermute | solution.py:239
  17.9 5.3 %collective-permute-start.2 = (f32[16,1536]{1,0:T(8,128)S(1)}, f32[16,1536]{1,0:T(8,128)S(1)}, u32[]{:S(2)}, u32[]{:S(2)}) collective-permute-start(f32[16,1536]{1,0:T(8,128)S(1)} %get-tuple-element.39), channel_id=1, source_target_pairs={{0,2},{1,3},{2,4},{3,5},{4,6},{5,7},{6,0},{7,1},{8,10},{9,11},{10,... | collective-permute-start | bytes 294920 | tf_op jit(solution)/shard_map/ppermute | solution.py:244
  19.2 4.0 %collective-permute-start.4 = (f32[16,1536]{1,0:T(8,128)S(1)}, f32[16,1536]{1,0:T(8,128)S(1)}, u32[]{:S(2)}, u32[]{:S(2)}) collective-permute-start(f32[16,1536]{1,0:T(8,128)S(1)} %get-tuple-element.40), channel_id=1, source_target_pairs={{0,6},{1,7},{2,0},{3,1},{4,2},{5,3},{6,4},{7,5},{8,14},{9,15},{10,... | collective-permute-start | bytes 294920 | tf_op jit(solution)/shard_map/ppermute | solution.py:244
  20.6 5.1 %collective-permute-start.3 = (f32[16,1536]{1,0:T(8,128)S(1)}, f32[16,1536]{1,0:T(8,128)S(1)}, u32[]{:S(2)}, u32[]{:S(2)}) collective-permute-start(f32[16,1536]{1,0:T(8,128)S(1)} %get-tuple-element.41), channel_id=1, source_target_pairs={{0,4},{1,5},{2,6},{3,7},{4,0},{5,1},{6,2},{7,3},{8,12},{9,13},{10,... | collective-permute-start | bytes 294920 | tf_op jit(solution)/shard_map/ppermute | solution.py:244
  25.8 5.8 %collective-permute-start.5 = (f32[64,512]{1,0:T(8,128)S(1)}, f32[64,512]{1,0:T(8,128)S(1)}, u32[]{:S(2)}, u32[]{:S(2)}) collective-permute-start(f32[64,512]{1,0:T(8,128)S(1)} %pad_maximum_fusion.3), channel_id=1, source_target_pairs={{0,32},{16,48},{32,0},{48,16},{64,96},{80,112},{96,64},{112,80},{1... | collective-permute-start | bytes 393224 | tf_op jit(solution)/shard_map/ppermute | solution.py:239
  26.6 5.0 %collective-permute-start.6 = (f32[16,1536]{1,0:T(8,128)S(1)}, f32[16,1536]{1,0:T(8,128)S(1)}, u32[]{:S(2)}, u32[]{:S(2)}) collective-permute-start(f32[16,1536]{1,0:T(8,128)S(1)} %fusion.2), channel_id=1, source_target_pairs={{0,8},{1,9},{2,10},{3,11},{4,12},{5,13},{6,14},{7,15},{8,0},{9,1},... | collective-permute-start | bytes 294920 | tf_op jit(solution)/shard_map/ppermute | solution.py:247
  31.6 5.8 %collective-permute-start.7 = (f32[128,512]{1,0:T(8,128)S(1)}, f32[128,512]{1,0:T(8,128)S(1)}, u32[]{:S(2)}, u32[]{:S(2)}) collective-permute-start(f32[128,512]{1,0:T(8,128)S(1)} %pad_maximum_fusion.2), channel_id=1, source_target_pairs={{0,16},{16,0},{32,48},{48,32},{64,80},{80,64},{96,112},{112,96},{1... | collective-permute-start | bytes 786440 | tf_op jit(solution)/shard_map/ppermute | solution.py:239
  33.0 4.4 %collective-permute-start.10 = (f32[16,1536]{1,0:T(8,128)S(1)}, f32[16,1536]{1,0:T(8,128)S(1)}, u32[]{:S(2)}, u32[]{:S(2)}) collective-permute-start(f32[16,1536]{1,0:T(8,128)S(1)} %add.31.refs_0_), channel_id=1, source_target_pairs={{0,6},{1,7},{2,0},{3,1},{4,2},{5,3},{6,4},{7,5},{8,14},{9,15},{10,... | collective-permute-start | bytes 294920 | tf_op jit(solution)/shard_map/ppermute | solution.py:249
  34.5 5.0 %collective-permute-start.9 = (f32[16,1536]{1,0:T(8,128)S(1)}, f32[16,1536]{1,0:T(8,128)S(1)}, u32[]{:S(2)}, u32[]{:S(2)}) collective-permute-start(f32[16,1536]{1,0:T(8,128)S(1)} %add.31.refs_0_), channel_id=1, source_target_pairs={{0,4},{1,5},{2,6},{3,7},{4,0},{5,1},{6,2},{7,3},{8,12},{9,13},{10,... | collective-permute-start | bytes 294920 | tf_op jit(solution)/shard_map/ppermute | solution.py:249
  36.0 4.7 %collective-permute-start.8 = (f32[16,1536]{1,0:T(8,128)S(1)}, f32[16,1536]{1,0:T(8,128)S(1)}, u32[]{:S(2)}, u32[]{:S(2)}) collective-permute-start(f32[16,1536]{1,0:T(8,128)S(1)} %add.31.refs_0_), channel_id=1, source_target_pairs={{0,2},{1,3},{2,4},{3,5},{4,6},{5,7},{6,0},{7,1},{8,10},{9,11},{10,... | collective-permute-start | bytes 294920 | tf_op jit(solution)/shard_map/ppermute | solution.py:249
  40.7 6.4 %collective-permute-start.11 = (f32[4,16,1536]{2,1,0:T(8,128)S(1)}, f32[4,16,1536]{2,1,0:T(8,128)S(1)}, u32[]{:S(2)}, u32[]{:S(2)}) collective-permute-start(f32[4,16,1536]{2,1,0:T(8,128)S(1)} %pad_maximum_fusion.1), channel_id=1, source_target_pairs={{0,1},{1,0},{2,3},{3,2},{4,5},{5,4},{6,7},{7,6},{8,9},{9,8},{10,11... | collective-permute-start | bytes 1179656 | tf_op jit(solution)/shard_map/ppermute | solution.py:251
  45.8 14.7 %collective-permute-start.12 = (f32[256,512]{1,0:T(8,128)S(1)}, f32[256,512]{1,0:T(8,128)S(1)}, u32[]{:S(2)}, u32[]{:S(2)}) collective-permute-start(f32[256,512]{1,0:T(8,128)S(1)} %pad_maximum_fusion.near_ref), channel_id=1, source_target_pairs={{0,224},{16,240},{32,64},{48,80},{64,32},{80,48},{96,128},{112,144... | collective-permute-start | bytes 1572872 | tf_op jit(solution)/shard_map/ppermute | solution.py:239
  50.7 14.2 %all-to-all-start = ((f32[16,32,128]{2,1,0:T(8,128)}), f32[16,32,128]{2,1,0:T(8,128)S(1)}, u32[]{:S(2)}, u32[]{:S(2)}) async-start(f32[16,32,128]{2,1,0:T(8,128)} %feature_shares.1), calls=%async_computation | async-start | bytes 524288 | tf_op jit(solution)/shard_map/all_to_all | solution.py:255

commit v3 on v2

v3 whole, which is shorter than its diff:
```python
import functools
import math

import jax
import jax.numpy as jnp
from jax import lax
from jax.experimental import pallas as pl
from jax.experimental.pallas import tpu as pltpu
from jax.sharding import PartitionSpec as P

LEN = 1024
K = 8192
TB = 512
EPS = 1e-06
STEP_A, STEP_F, STEP_Y, STEP_B = 0, 1, 2, 3
VMEM = 20 * 1024 * 1024
STEPS = (3, 3, 3, 3)
DEPTH = 3

NT = (((1,), (1,)), ((), ()))
NN = (((1,), (0,)), ((), ()))


def mm(a, b, dims):
    return lax.dot_general(a, b, dims, preferred_element_type=jnp.float32)


def halves(a):
    hi = a.astype(jnp.bfloat16)
    lo = (a - hi.astype(jnp.float32)).astype(jnp.bfloat16)
    return jnp.concatenate([hi, lo], 0)


def rows_kernel(where_ref, x_ref, g_ref, a_ref, b_ref, keep_ref, send_ref, xs_ref, gs_ref, at_ref, bs_ref, sem, sem_w):
    first = where_ref[0] == 0
    per = keep_ref.shape[2] // TB
    weights = [
        pltpu.make_async_copy(src, dst, sem_w.at[j])
        for j, (src, dst) in enumerate(((a_ref, at_ref), (b_ref, bs_ref)))
    ]
    for copy in weights:
        copy.start()
    jobs, start = [], 0
    for c, blocks in enumerate(STEPS):
        rows = pl.ds(start * TB, blocks * TB)
        for j, (src, dst) in enumerate(((x_ref, xs_ref), (g_ref, gs_ref))):
            copy = pltpu.make_async_copy(src.at[rows], dst.at[rows], sem.at[j, c])
            jobs.append((j, range(start, start + blocks), copy))
        start += blocks
    for _, _, copy in jobs[:DEPTH]:
        copy.start()
    for copy in weights:
        copy.wait()
    for n, (j, blocks, copy) in enumerate(jobs):
        copy.wait()
        if n + DEPTH < len(jobs):
            jobs[n + DEPTH][2].start()
        for i in blocks:
            rows = slice(i * TB, (i + 1) * TB)
            cols = slice(i % per * TB, (i % per + 1) * TB)
            slot = (i // per - where_ref[2]) & 3
            if j == 0:
                keep_ref[slot, :, cols] = mm(at_ref[...], xs_ref[rows], NT)
            else:
                down = keep_ref[slot, :, cols]
                up = mm(bs_ref[...], gs_ref[rows], NT)
                keep_ref[slot, :, cols] = jnp.where(first, down, up)
                send_ref[slot, :, cols] = jnp.where(first, up, down)


def rank_rows(where, x, g, a, b):
    tokens, width = x.shape
    rank = b.shape[0]
    chunk = tokens // 4
    out = jax.ShapeDtypeStruct((4, rank, chunk), jnp.float32)
    near = pltpu.VMEM((tokens, width), jnp.bfloat16)
    whole = pl.BlockSpec(memory_space=pltpu.VMEM)
    far = pl.BlockSpec(memory_space=pl.ANY)
    x, g, a, b = (pltpu.with_memory_space_constraint(v, pltpu.HBM) for v in (x, g, a, b))
    return pl.pallas_call(
        rows_kernel,
        in_specs=[pl.BlockSpec(memory_space=pltpu.SMEM), far, far, far, far],
        out_specs=[whole] * 4,
        out_shape=[out, out, near, near],
        scratch_shapes=[
            pltpu.VMEM((rank, width), jnp.bfloat16),
            pltpu.VMEM((rank, width), jnp.bfloat16),
            pltpu.SemaphoreType.DMA((2, len(STEPS))),
            pltpu.SemaphoreType.DMA((2,)),
        ],
        compiler_params=pltpu.CompilerParams(vmem_limit_bytes=VMEM),
        cost_estimate=pl.CostEstimate(
            flops=4 * tokens * width * rank, bytes_accessed=4 * tokens * width, transcendentals=0
        ),
        name="rank_rows",
    )(where, x, g, a, b)


def share_kernel(where_ref, x_ref, g_ref, *refs):
    own_refs, (other_ref, s_ref, keep_ref, send_ref, v_ref) = refs[:4], refs[4:]
    rank, chunk = own_refs[0].shape
    per = chunk // TB
    first = where_ref[0] == 0
    for j, own_ref in enumerate(own_refs):
        begin = ((where_ref[2] - j) & 3) * per
        for c in range(per):
            rows = pl.ds(pl.multiple_of((begin + c) * TB, TB), TB)
            cols = slice(c * TB, (c + 1) * TB)
            own, other = own_ref[:, cols], other_ref[j, :, cols]
            a = mm(halves(jnp.where(first, other, own)), x_ref[rows], NN)
            b = mm(halves(jnp.where(first, own, other)), g_ref[rows], NN)
            v_ref[0, begin + c] = a[:rank] + a[rank:]
            v_ref[1, begin + c] = b[:rank] + b[rank:]
    sign = (2 * s_ref[...] - 1).astype(jnp.float32).astype(jnp.bfloat16)
    each = keep_ref.shape[0] // 2
    blocks, step = v_ref.shape[1], LEN // TB
    pad = jnp.zeros((128 - blocks // step * rank, x_ref.shape[1]), jnp.float32)
    for m in range(2):
        v = [sum(v_ref[m, i + k] for k in range(step)) for i in range(0, blocks, step)]
        f = mm(halves(jnp.concatenate(v + [pad], 0)), sign, NN)
        f = jnp.transpose(f[:128] + f[128:]).reshape(each, 2, -1, 128)
        for n in range(each):
            keep_ref[m * each + n] = jnp.where(first, f[n, 0], f[n, 1])
            send_ref[m * each + n] = jnp.where(first, f[n, 1], f[n, 0])


def feature_shares(where, x, g, own, other, bits, parts):
    tokens, width = x.shape
    rank = own[0].shape[0]
    kd = bits.shape[1]
    whole = pl.BlockSpec(memory_space=pltpu.VMEM)
    x, g = (pltpu.with_memory_space_constraint(v, pltpu.VMEM) for v in (x, g))
    return pl.pallas_call(
        share_kernel,
        in_specs=[pl.BlockSpec(memory_space=pltpu.SMEM)] + [whole] * (len(own) + 4),
        out_specs=[whole] * 2,
        out_shape=[jax.ShapeDtypeStruct((parts // 2, 2 * kd // parts, 128), jnp.float32)] * 2,
        scratch_shapes=[pltpu.VMEM((2, tokens // TB, rank, width), jnp.float32)],
        compiler_params=pltpu.CompilerParams(vmem_limit_bytes=VMEM),
        cost_estimate=pl.CostEstimate(
            flops=8 * tokens * width * rank, bytes_accessed=4 * tokens * width, transcendentals=0
        ),
        name="feature_shares",
    )(where, x, g, *own, other, bits)


def valid_kernel(rank, v_ref, hl_ref, sq_ref):
    v = v_ref[...]
    rows, cols = v.shape
    ks = cols // rank
    goes = lax.broadcasted_iota(jnp.int32, (cols, cols), 0)
    came = lax.broadcasted_iota(jnp.int32, (cols, cols), 1)
    move = jnp.where((came % rank) * ks + came // rank == goes, 1.0, 0.0).astype(jnp.bfloat16)
    hl_ref[...] = mm(move, halves(v), NT).astype(jnp.bfloat16)
    total = mm(jnp.ones((8, cols), jnp.bfloat16), halves(v * v), NT)
    sq_ref[...] = total[:, :rows] + total[:, rows:]


def valid_terms(v, rank):
    rows, cols = v.shape
    whole = pl.BlockSpec(memory_space=pltpu.VMEM)
    return pl.pallas_call(
        functools.partial(valid_kernel, rank),
        in_specs=[whole],
        out_specs=[whole, whole],
        out_shape=[
            jax.ShapeDtypeStruct((cols, 2 * rows), jnp.bfloat16),
            jax.ShapeDtypeStruct((8, rows), jnp.float32),
        ],
        compiler_params=pltpu.CompilerParams(vmem_limit_bytes=VMEM // 2),
        cost_estimate=pl.CostEstimate(
            flops=4 * rows * cols * cols, bytes_accessed=8 * rows * cols, transcendentals=0
        ),
        name="valid_terms",
    )(v)


def flip(step, z, y):
    if step == STEP_A:
        return z ^ 1, y
    if step == STEP_F:
        return z ^ 4, y
    if step == STEP_Y:
        return z, y ^ 1
    return (z + 2 * (z & 1) - 1) & 7, y


def flips(step):
    pairs = []
    for i in range(16):
        z, y = flip(step, i >> 1, i & 1)
        pairs.append((i, z * 2 + y))
    return pairs


def origin(place, index):
    z, y = index >> 1, index & 1
    for step in (3, 2, 1, 0):
        if place >> step & 1:
            z, y = flip(step, z, y)
    return z * 2 + y


def dot_kernel(rank, where_ref, f_ref, hl0_ref, sq0_ref, hl1_ref, sq1_ref, out_ref, t_ref):
    parts = out_ref.shape[0]
    rows = sq0_ref.shape[1]
    each = 2 * rows // parts
    t_ref[...] = jnp.transpose(jnp.sum(f_ref[...], 0))
    f = jnp.concatenate([t_ref[pl.ds(r, 8, stride=rank), :] for r in range(rank)], 1)
    own_sq = jnp.broadcast_to(jnp.sum(f * f, 1, keepdims=True), (8, each))
    f = halves(f)
    for half, (hl_ref, sq_ref) in enumerate(((hl0_ref, sq0_ref), (hl1_ref, sq1_ref))):
        prod = mm(f, hl_ref[...], NN)
        dots = prod[:8, :rows] + (prod[8:, :rows] + prod[:8, rows:]) + prod[8:, rows:]
        line = lax.broadcasted_iota(jnp.int32, dots.shape, 0)
        dots = jnp.where(line == 6, sq_ref[...], dots)
        for n in range(parts // 2):
            part = origin(half * parts // 2 + n, where_ref[1])
            out_ref[part, :, :each] = dots[:, n * each : (n + 1) * each]
            out_ref[part, :, each : 2 * each] = own_sq


def partial_dots(where, f, terms, rank):
    whole = pl.BlockSpec(memory_space=pltpu.VMEM)
    return pl.pallas_call(
        functools.partial(dot_kernel, rank),
        in_specs=[pl.BlockSpec(memory_space=pltpu.SMEM)] + [whole] * 5,
        out_specs=whole,
        out_shape=jax.ShapeDtypeStruct((2 * f.shape[0], 8, 128), jnp.float32),
        scratch_shapes=[pltpu.VMEM((128, f.shape[1]), jnp.float32)],
        compiler_params=pltpu.CompilerParams(vmem_limit_bytes=VMEM // 2),
        name="partial_dots",
    )(where, f, *terms)


def on_device(x, g, a, b, bits, valid):
    tp = lax.axis_size("tp")
    rank = b.shape[0]
    seqs = x.shape[0] // LEN
    each = 16 * valid.shape[0] // tp
    index = lax.axis_index("tp")
    where = jnp.stack([index & 1, lax.axis_index("grp"), index >> 1 & 3]).astype(jnp.int32)
    swap_core = [(i, i ^ 1) for i in range(tp)]
    swap_y = [(i, i ^ 8) for i in range(tp)]
    same_core = [list(range(c, tp, 2)) for c in range(2)]
    turn_x = [[(i, (i & 9) | (((i >> 1) + k & 3) << 1)) for i in range(tp)] for k in range(4)]

    def gather(step, rows):
        return rows, lax.ppermute(rows, "grp", flips(step))

    tie = lax.optimization_barrier

    def from_group(step, rows):
        return lax.ppermute(rows, "grp", flips(step))

    keep, send, x, g = rank_rows(where, x, g, jnp.transpose(a), b)
    send, near = tie((send, valid))
    far = from_group(STEP_A, near)
    mine = keep + lax.ppermute(send, "tp", swap_core)
    came = [lax.ppermute(mine[k], "tp", turn_x[k]) for k in (1, 2, 3)]
    came[0], near = tie((came[0], jnp.concatenate([near, far], 0)))
    far = from_group(STEP_F, near)
    mine = mine[0] + came[0] + came[1] + came[2]
    mine = mine + lax.ppermute(mine, "tp", swap_y)
    mine, near = tie((mine, jnp.concatenate([near, far], 0)))
    own = [mine] + [lax.ppermute(mine, "tp", turn_x[k]) for k in (1, 2, 3)]
    far = from_group(STEP_Y, near)
    own, near = tie((own, jnp.concatenate([near, far], 0)))
    far = from_group(STEP_B, near)
    other = lax.ppermute(jnp.stack(own), "tp", swap_core)
    near = valid_terms(near, rank)
    other, near = tie((other, near))
    keep, send = feature_shares(where, x, g, own, other, bits, tp)
    came = lax.ppermute(send, "tp", swap_core)
    shares = lax.all_to_all(keep + came, "tp", 0, 0, axis_index_groups=same_core, tiled=True)
    far = valid_terms(far, rank)
    dots = partial_dots(where, shares, [*near, *far], rank)
    dots = lax.all_to_all(dots, "tp", 0, 0, tiled=True)
    total = jnp.sum(dots, 0)
    train = math.sqrt(K) / jnp.sqrt(total[:seqs, each : 2 * each] + EPS)
    return total[:seqs, :each] * train / jnp.sqrt(total[6:7, :each] + EPS)


def solution(mesh):
    return jax.shard_map(
        on_device,
        mesh=mesh,
        in_specs=(
            P("grp", "tp"),
            P("grp", "tp"),
            P("tp", None),
            P(None, "tp"),
            P("tp", None),
            P("grp", "tp"),
        ),
        out_specs=P("grp", "tp"),
        check_vma=False,
    )
```

time: 77.6 us -> 73.6 us (0.948)
  Pallas kernels: 14.8 us -> 12.2 us
  starting transfers between devices: 31.5 us -> 29.7 us
  waiting for transfers between devices: 19.3 us -> 18 us
  blocking collectives: 10.6 us -> 11.7 us
    pallas_call x2 -> x3, Pallas kernels: 10.1 us -> 8.27 us  [the longest x1 7.05 us: rank_rows(): pl.pallas_call(rows_kernel, in_specs=[pl.BlockSpec(memory_space=pltpu.SME...]
    ppermute x4 -> x5, starting transfers between devices: 7.41 us -> 9.06 us  [the longest x4 8.42 us: from_group(): return lax.ppermute(rows, 'grp', flips(step))]
    ppermute x3, starting transfers between devices: 4.29 us -> 2.86 us  [on_device(): came = [lax.ppermute(mine[k], 'tp', turn_x[k]) for k in (1, 2, 3)]]
    ppermute x1, waiting for transfers between devices: 1.35 us -> 0.01 us  [on_device(): other = lax.ppermute(jnp.stack(own), 'tp', swap_core)]
    ppermute x1, waiting for transfers between devices: 0.01 us -> 1.34 us  [on_device(): mine = keep + lax.ppermute(send, 'tp', swap_core)]
    ppermute x3, waiting for transfers between devices: 3.54 us -> 2.41 us  [on_device(): came = [lax.ppermute(mine[k], 'tp', turn_x[k]) for k in (1, 2, 3)]]
    all_to_all x1, blocking collectives: 10.6 us -> 11.7 us  [on_device(): dots = lax.all_to_all(dots, 'tp', 0, 0, tiled=True)]
    all_to_all x1, starting transfers between devices: 5.53 us -> 4.57 us  [on_device(): lax.all_to_all(keep + came, 'tp', 0, 0, axis_index_groups=same_core, tile...]
  transfers between devices with their start and end apart: 14 -> 15, of which waited for: 9 -> 9; matrix products, arithmetic and copies ran while one was open for 0% -> 1% of each run, Pallas kernels for 6% -> 6%
where the time goes in v3:
time: 73.6 us; the launch traced here: 73.3 us
  starting transfers between devices  29.7 us (40%)
  waiting for transfers between devices  18 us (24%)
  Pallas kernels  12.2 us (17%)
  blocking collectives  11.7 us (16%)
  other arithmetic  1.62 us (2%)
    all_to_all x1, blocking collectives, on_device(): dots = lax.all_to_all(dots, 'tp', 0, 0, tiled=True)  11.7 us
    ppermute x4, starting transfers between devices, from_group(): return lax.ppermute(rows, 'grp', flips(step))  8.42 us
    pallas_call x1, Pallas kernels, rank_rows(): pl.pallas_call(rows_kernel, in_specs=[pl.BlockSpec(memory_space=pltpu.SME...  7.05 us
    all_to_all x1, starting transfers between devices, on_device(): lax.all_to_all(keep + came, 'tp', 0, 0, axis_index_groups=same_core, tile...  4.57 us
    ppermute x1, starting transfers between devices, on_device(): other = lax.ppermute(jnp.stack(own), 'tp', swap_core)  4.53 us
    all_to_all x1, waiting for transfers between devices, on_device(): lax.all_to_all(keep + came, 'tp', 0, 0, axis_index_groups=same_core, tile...  4.11 us
    ppermute x4, waiting for transfers between devices, from_group(): return lax.ppermute(rows, 'grp', flips(step))  3.74 us
    ppermute x1, starting transfers between devices, on_device(): mine = keep + lax.ppermute(send, 'tp', swap_core)  3.33 us
  transfers between devices with their start and end apart: 15, of which 9 were waited for; matrix products, arithmetic and copies ran while one was open for 1% of the time, Pallas kernels for 6%

profile of v3, /device:TPU:1, one launch (start us, length us, event | category | flops | bytes accessed | tf_op | source)
XLA Modules:
  0.0 73.3 jit_solution(10562525717073419971)
XLA Ops:
  0.0 0.1 pad_add_fusion.where_ref
  0.1 0.0 copy-start.1
  0.1 0.0 copy-start
  0.1 7.0 %rank_rows.1 = (f32[4,16,1536]{2,1,0:T(8,128)S(1)}, f32[4,16,1536]{2,1,0:T(8,128)S(1)}, bf16[6144,512]{1,0:T(8,128)(2,1)S(1)}, bf16[6144,512]{1,0:T(8,128)(2,1)S(1)}) custom-call(s32[3]{0:T(128)S(1)} %pad_add_fusion.where_ref, bf16[6144,512]{1,0:T(8,128)(2,1)} %x_ref.1, bf16[6144,512]{1,0:T(8,128)(2,1)} %g_ref.1, bf16[16,512]{1,0:T(8,128)(2,1)} %bitcast.28, ...), custom_call_target="tpu_custom_call" | custom-call | flops 201326592 | bytes 12582912 | tf_op jit(solution)/shard_map/rank_rows/pallas_call | solution.py:80
  7.1 3.3 %collective-permute-start = (f32[4,16,1536]{2,1,0:T(8,128)S(1)}, f32[4,16,1536]{2,1,0:T(8,128)S(1)}, u32[]{:S(2)}, u32[]{:S(2)}) collective-permute-start(f32[4,16,1536]{2,1,0:T(8,128)S(1)} %get-tuple-element.33), channel_id=1, source_target_pairs={{0,1},{1,0},{2,3},{3,2},{4,5},{5,4},{6,7},{7,6},{8,9},{9,8},{10,11... | collective-permute-start | bytes 1179656 | tf_op jit(solution)/shard_map/ppermute | solution.py:259
  10.5 0.0 copy-done.1
  10.5 0.0 collective-permute-start.2
  10.5 1.3 %collective-permute-done = f32[4,16,1536]{2,1,0:T(8,128)S(1)} collective-permute-done((f32[4,16,1536]{2,1,0:T(8,128)S(1)}, f32[4,16,1536]{2,1,0:T(8,128)S(1)}, u32[]{:S(2)}, u32[]{:S(2)}) %collective-permute-start) | collective-permute-done | bytes 393248 | tf_op jit(solution)/shard_map/ppermute | solution.py:259
  11.9 0.1 collective-permute-start.1
  12.0 2.7 %collective-permute-start.4 = (f32[16,1536]{1,0:T(8,128)S(1)}, f32[16,1536]{1,0:T(8,128)S(1)}, u32[]{:S(2)}, u32[]{:S(2)}) collective-permute-start(f32[16,1536]{1,0:T(8,128)S(1)} %get-tuple-element.54), channel_id=1, source_target_pairs={{0,6},{1,7},{2,0},{3,1},{4,2},{5,3},{6,4},{7,5},{8,14},{9,15},{10,... | collective-permute-start | bytes 294920 | tf_op jit(solution)/shard_map/ppermute | solution.py:260
  14.6 0.1 collective-permute-start.3
  14.8 0.0 collective-permute-done.2
  14.8 2.4 %collective-permute-done.1 = f32[16,1536]{1,0:T(8,128)S(1)} collective-permute-done((f32[16,1536]{1,0:T(8,128)S(1)}, f32[16,1536]{1,0:T(8,128)S(1)}, u32[]{:S(2)}, u32[]{:S(2)}) %collective-permute-start.1) | collective-permute-done | bytes 98336 | tf_op jit(solution)/shard_map/ppermute | solution.py:260
  17.2 5.2 %collective-permute-start.6 = (f32[64,512]{1,0:T(8,128)S(1)}, f32[64,512]{1,0:T(8,128)S(1)}, u32[]{:S(2)}, u32[]{:S(2)}) collective-permute-start(f32[64,512]{1,0:T(8,128)S(1)} %pad_maximum_fusion.3), channel_id=1, source_target_pairs={{0,128},{16,144},{32,160},{48,176},{64,192},{80,208},{96,224},{112... | collective-permute-start | bytes 393224 | tf_op jit(solution)/shard_map/ppermute | solution.py:254
  22.4 0.0 collective-permute-done.4
  22.4 0.0 collective-permute-done.3
  22.4 3.0 %collective-permute-start.5 = (f32[16,1536]{1,0:T(8,128)S(1)}, f32[16,1536]{1,0:T(8,128)S(1)}, u32[]{:S(2)}, u32[]{:S(2)}) collective-permute-start(f32[16,1536]{1,0:T(8,128)S(1)} %fusion.2), channel_id=1, source_target_pairs={{0,8},{1,9},{2,10},{3,11},{4,12},{5,13},{6,14},{7,15},{8,0},{9,1},... | collective-permute-start | bytes 294920 | tf_op jit(solution)/shard_map/ppermute | solution.py:264
  25.4 2.1 %collective-permute-done.5 = f32[16,1536]{1,0:T(8,128)S(1)} collective-permute-done((f32[16,1536]{1,0:T(8,128)S(1)}, f32[16,1536]{1,0:T(8,128)S(1)}, u32[]{:S(2)}, u32[]{:S(2)}) %collective-permute-start.5) | collective-permute-done | bytes 98336 | tf_op jit(solution)/shard_map/ppermute | solution.py:264
  27.5 0.0 collective-permute-done.6
  27.5 1.4 %collective-permute-start.10 = (f32[128,512]{1,0:T(8,128)S(1)}, f32[128,512]{1,0:T(8,128)S(1)}, u32[]{:S(2)}, u32[]{:S(2)}) collective-permute-start(f32[128,512]{1,0:T(8,128)S(1)} %pad_maximum_fusion.2), channel_id=1, source_target_pairs={{0,16},{16,0},{32,48},{48,32},{64,80},{80,64},{96,112},{112,96},{1... | collective-permute-start | bytes 786440 | tf_op jit(solution)/shard_map/ppermute | solution.py:254
  28.9 1.3 %collective-permute-start.9 = (f32[16,1536]{1,0:T(8,128)S(1)}, f32[16,1536]{1,0:T(8,128)S(1)}, u32[]{:S(2)}, u32[]{:S(2)}) collective-permute-start(f32[16,1536]{1,0:T(8,128)S(1)} %add.34.refs_0_), channel_id=1, source_target_pairs={{0,6},{1,7},{2,0},{3,1},{4,2},{5,3},{6,4},{7,5},{8,14},{9,15},{10,... | collective-permute-start | bytes 294920 | tf_op jit(solution)/shard_map/ppermute | solution.py:266
  30.2 0.5 collective-permute-start.8
  30.7 0.6 collective-permute-start.7
  31.3 1.5 %collective-permute-done.10 = f32[128,512]{1,0:T(8,128)S(1)} collective-permute-done((f32[128,512]{1,0:T(8,128)S(1)}, f32[128,512]{1,0:T(8,128)S(1)}, u32[]{:S(2)}, u32[]{:S(2)}) %collective-permute-start.10) | collective-permute-done | bytes 262176 | tf_op jit(solution)/shard_map/ppermute | solution.py:254
  32.9 0.0 collective-permute-done.9.refs_3_
  32.9 2.4 %collective-permute-done.8.refs_2_ = f32[16,1536]{1,0:T(8,128)S(1)} collective-permute-done((f32[16,1536]{1,0:T(8,128)S(1)}, f32[16,1536]{1,0:T(8,128)S(1)}, u32[]{:S(2)}, u32[]{:S(2)}) %collective-permute-start.8) | collective-permute-done | bytes 98336 | tf_op jit(solution)/shard_map/ppermute | solution.py:266
  35.2 1.0 %collective-permute-done.7.refs_1_ = f32[16,1536]{1,0:T(8,128)S(1)} collective-permute-done((f32[16,1536]{1,0:T(8,128)S(1)}, f32[16,1536]{1,0:T(8,128)S(1)}, u32[]{:S(2)}, u32[]{:S(2)}) %collective-permute-start.7) | collective-permute-done | bytes 98336 | tf_op jit(solution)/shard_map/ppermute | solution.py:266
  36.2 4.5 %collective-permute-start.11 = (f32[4,16,1536]{2,1,0:T(8,128)S(1)}, f32[4,16,1536]{2,1,0:T(8,128)S(1)}, u32[]{:S(2)}, u32[]{:S(2)}) collective-permute-start(f32[4,16,1536]{2,1,0:T(8,128)S(1)} %pad_maximum_fusion.1), channel_id=1, source_target_pairs={{0,1},{1,0},{2,3},{3,2},{4,5},{5,4},{6,7},{7,6},{8,9},{9,8},{10,11... | collective-permute-start | bytes 1179656 | tf_op jit(solution)/shard_map/ppermute | solution.py:270
  40.7 1.9 %collective-permute-start.13 = (f32[256,512]{1,0:T(8,128)S(1)}, f32[256,512]{1,0:T(8,128)S(1)}, u32[]{:S(2)}, u32[]{:S(2)}) collective-permute-start(f32[256,512]{1,0:T(8,128)S(1)} %pad_maximum_fusion.v_ref), channel_id=1, source_target_pairs={{0,224},{16,240},{32,64},{48,80},{64,32},{80,48},{96,128},{112,144... | collective-permute-start | bytes 1572872 | tf_op jit(solution)/shard_map/ppermute | solution.py:254
  42.6 0.6 valid_terms.2
  43.2 0.0 collective-permute-done.11.refs_4_
  43.2 0.0 copy-done
  43.2 2.9 %feature_shares.1 = (f32[8,32,128]{2,1,0:T(8,128)S(1)}, f32[8,32,128]{2,1,0:T(8,128)S(1)}) custom-call(s32[3]{0:T(128)S(1)} %pad_add_fusion.where_ref, bf16[6144,512]{1,0:T(8,128)(2,1)S(1)} %get-tuple-element.29.x_ref, bf16[6144,512]{1,0:T(8,128)(2,1)S(1)} %get-tuple-element.30.g_ref, f32[16,1536]{1,0:T(8,128)S(1)} %add.34.refs_0_, ...), custom_call_target="tpu_custom_call" | custom-call | flops 402653184 | bytes 12582912 | tf_op jit(solution)/shard_map/feature_shares/pallas_call | solution.py:133
  46.1 0.6 collective-permute-start.12
  46.8 1.0 %collective-permute-done.12 = f32[8,32,128]{2,1,0:T(8,128)S(1)} collective-permute-done((f32[8,32,128]{2,1,0:T(8,128)S(1)}, f32[8,32,128]{2,1,0:T(8,128)S(1)}, u32[]{:S(2)}, u32[]{:S(2)}) %collective-permute-start.12) | collective-permute-done | bytes 131104 | tf_op jit(solution)/shard_map/ppermute | solution.py:274
  47.8 0.7 add.35
  48.4 4.6 %all-to-all-start = ((f32[8,32,128]{2,1,0:T(8,128)}), f32[8,32,128]{2,1,0:T(8,128)S(1)}, u32[]{:S(2)}, u32[]{:S(2)}) async-start(f32[8,32,128]{2,1,0:T(8,128)} %add.35), calls=%async_computation | async-start | bytes 262144 | tf_op jit(solution)/shard_map/all_to_all | solution.py:275
  53.0 2.2 %collective-permute-done.13.v_ref = f32[256,512]{1,0:T(8,128)S(1)} collective-permute-done((f32[256,512]{1,0:T(8,128)S(1)}, f32[256,512]{1,0:T(8,128)S(1)}, u32[]{:S(2)}, u32[]{:S(2)}) %collective-permute-start.13) | collective-permute-done | bytes 524320 | tf_op jit(solution)/shard_map/ppermute | solution.py:254
  55.2 0.6 valid_terms.3
  55.8 4.1 %all-to-all-done.f_ref = f32[8,32,128]{2,1,0:T(8,128)S(1)} async-done(((f32[8,32,128]{2,1,0:T(8,128)}), f32[8,32,128]{2,1,0:T(8,128)S(1)}, u32[]{:S(2)}, u32[]{:S(2)}) %all-to-all-start) | async-done | bytes 131104 | tf_op jit(solution)/shard_map/all_to_all | solution.py:275
  59.9 1.0 %partial_dots.1 = f32[16,8,128]{2,1,0:T(8,128)S(1)} custom-call(s32[3]{0:T(128)S(1)} %pad_add_fusion.where_ref, f32[8,32,128]{2,1,0:T(8,128)S(1)} %all-to-all-done.f_ref, bf16[512,512]{1,0:T(8,128)(2,1)S(1)} %get-tuple-element.49.hl0_ref, f32[8,256]{1,0:T(8,128)S(1)} %get-tuple-element.50.sq0_ref, bf16[512,512]{1,0:T(8,128)(2,1)S(1)} %get-tuple-element.51.hl1_ref, ...), custom_call_target="tpu_custom_call" | custom-call | tf_op jit(solution)/shard_map/partial_dots/pallas_call | solution.py:225
  61.0 11.7 %all_to_all.10 = f32[16,8,128]{2,1,0:T(8,128)S(1)} all-to-all(f32[16,8,128]{2,1,0:T(8,128)S(1)} %partial_dots.1), channel_id=1, replica_groups=mesh['grp'=16,'tp'=16] {'tp'}, dimensions={0} | all-to-all | bytes 131072 | tf_op jit(solution)/shard_map/all_to_all | solution.py:278
  72.6 0.7 multiply_divide_fusion
  (10 shorter events, 0.2 us)
Async XLA Ops:
  0.1 10.4 %copy-start.1 = (f32[32,512]{1,0:T(8,128)S(1)}, f32[32,512]{1,0:T(8,128)}, u32[]{:S(2)}) copy-start(f32[32,512]{1,0:T(8,128)} %param.11) | copy-start | bytes 196612
  0.1 43.1 %copy-start = (s32[512,256]{1,0:T(8,128)S(1)}, s32[512,256]{1,0:T(8,128)}, u32[]{:S(2)}) copy-start(s32[512,256]{1,0:T(8,128)} %refs_5_.1) | copy-start | bytes 1572868
  7.1 4.7 %collective-permute-start = (f32[4,16,1536]{2,1,0:T(8,128)S(1)}, f32[4,16,1536]{2,1,0:T(8,128)S(1)}, u32[]{:S(2)}, u32[]{:S(2)}) collective-permute-start(f32[4,16,1536]{2,1,0:T(8,128)S(1)} %get-tuple-element.33), channel_id=1, source_target_pairs={{0,1},{1,0},{2,3},{3,2},{4,5},{5,4},{6,7},{7,6},{8,9},{9,8},{10,11... | collective-permute-start | bytes 1179656 | tf_op jit(solution)/shard_map/ppermute | solution.py:259
  10.5 4.3 %collective-permute-start.2 = (f32[32,512]{1,0:T(8,128)S(1)}, f32[32,512]{1,0:T(8,128)S(1)}, u32[]{:S(2)}, u32[]{:S(2)}) collective-permute-start(f32[32,512]{1,0:T(8,128)S(1)} %copy-done.1), channel_id=1, source_target_pairs={{0,32},{16,48},{32,0},{48,16},{64,96},{80,112},{96,64},{112,80},{1... | collective-permute-start | bytes 196616 | tf_op jit(solution)/shard_map/ppermute | solution.py:254
  11.9 5.3 %collective-permute-start.1 = (f32[16,1536]{1,0:T(8,128)S(1)}, f32[16,1536]{1,0:T(8,128)S(1)}, u32[]{:S(2)}, u32[]{:S(2)}) collective-permute-start(f32[16,1536]{1,0:T(8,128)S(1)} %get-tuple-element.53), channel_id=1, source_target_pairs={{0,2},{1,3},{2,4},{3,5},{4,6},{5,7},{6,0},{7,1},{8,10},{9,11},{10,... | collective-permute-start | bytes 294920 | tf_op jit(solution)/shard_map/ppermute | solution.py:260
  12.0 10.4 %collective-permute-start.4 = (f32[16,1536]{1,0:T(8,128)S(1)}, f32[16,1536]{1,0:T(8,128)S(1)}, u32[]{:S(2)}, u32[]{:S(2)}) collective-permute-start(f32[16,1536]{1,0:T(8,128)S(1)} %get-tuple-element.54), channel_id=1, source_target_pairs={{0,6},{1,7},{2,0},{3,1},{4,2},{5,3},{6,4},{7,5},{8,14},{9,15},{10,... | collective-permute-start | bytes 294920 | tf_op jit(solution)/shard_map/ppermute | solution.py:260
  14.6 7.7 %collective-permute-start.3 = (f32[16,1536]{1,0:T(8,128)S(1)}, f32[16,1536]{1,0:T(8,128)S(1)}, u32[]{:S(2)}, u32[]{:S(2)}) collective-permute-start(f32[16,1536]{1,0:T(8,128)S(1)} %get-tuple-element.55), channel_id=1, source_target_pairs={{0,4},{1,5},{2,6},{3,7},{4,0},{5,1},{6,2},{7,3},{8,12},{9,13},{10,... | collective-permute-start | bytes 294920 | tf_op jit(solution)/shard_map/ppermute | solution.py:260
  17.2 10.3 %collective-permute-start.6 = (f32[64,512]{1,0:T(8,128)S(1)}, f32[64,512]{1,0:T(8,128)S(1)}, u32[]{:S(2)}, u32[]{:S(2)}) collective-permute-start(f32[64,512]{1,0:T(8,128)S(1)} %pad_maximum_fusion.3), channel_id=1, source_target_pairs={{0,128},{16,144},{32,160},{48,176},{64,192},{80,208},{96,224},{112... | collective-permute-start | bytes 393224 | tf_op jit(solution)/shard_map/ppermute | solution.py:254
  22.4 5.1 %collective-permute-start.5 = (f32[16,1536]{1,0:T(8,128)S(1)}, f32[16,1536]{1,0:T(8,128)S(1)}, u32[]{:S(2)}, u32[]{:S(2)}) collective-permute-start(f32[16,1536]{1,0:T(8,128)S(1)} %fusion.2), channel_id=1, source_target_pairs={{0,8},{1,9},{2,10},{3,11},{4,12},{5,13},{6,14},{7,15},{8,0},{9,1},... | collective-permute-start | bytes 294920 | tf_op jit(solution)/shard_map/ppermute | solution.py:264
  27.5 5.3 %collective-permute-start.10 = (f32[128,512]{1,0:T(8,128)S(1)}, f32[128,512]{1,0:T(8,128)S(1)}, u32[]{:S(2)}, u32[]{:S(2)}) collective-permute-start(f32[128,512]{1,0:T(8,128)S(1)} %pad_maximum_fusion.2), channel_id=1, source_target_pairs={{0,16},{16,0},{32,48},{48,32},{64,80},{80,64},{96,112},{112,96},{1... | collective-permute-start | bytes 786440 | tf_op jit(solution)/shard_map/ppermute | solution.py:254
  28.9 4.0 %collective-permute-start.9 = (f32[16,1536]{1,0:T(8,128)S(1)}, f32[16,1536]{1,0:T(8,128)S(1)}, u32[]{:S(2)}, u32[]{:S(2)}) collective-permute-start(f32[16,1536]{1,0:T(8,128)S(1)} %add.34.refs_0_), channel_id=1, source_target_pairs={{0,6},{1,7},{2,0},{3,1},{4,2},{5,3},{6,4},{7,5},{8,14},{9,15},{10,... | collective-permute-start | bytes 294920 | tf_op jit(solution)/shard_map/ppermute | solution.py:266
  30.2 5.1 %collective-permute-start.8 = (f32[16,1536]{1,0:T(8,128)S(1)}, f32[16,1536]{1,0:T(8,128)S(1)}, u32[]{:S(2)}, u32[]{:S(2)}) collective-permute-start(f32[16,1536]{1,0:T(8,128)S(1)} %add.34.refs_0_), channel_id=1, source_target_pairs={{0,4},{1,5},{2,6},{3,7},{4,0},{5,1},{6,2},{7,3},{8,12},{9,13},{10,... | collective-permute-start | bytes 294920 | tf_op jit(solution)/shard_map/ppermute | solution.py:266
  30.7 5.5 %collective-permute-start.7 = (f32[16,1536]{1,0:T(8,128)S(1)}, f32[16,1536]{1,0:T(8,128)S(1)}, u32[]{:S(2)}, u32[]{:S(2)}) collective-permute-start(f32[16,1536]{1,0:T(8,128)S(1)} %add.34.refs_0_), channel_id=1, source_target_pairs={{0,2},{1,3},{2,4},{3,5},{4,6},{5,7},{6,0},{7,1},{8,10},{9,11},{10,... | collective-permute-start | bytes 294920 | tf_op jit(solution)/shard_map/ppermute | solution.py:266
  36.2 7.0 %collective-permute-start.11 = (f32[4,16,1536]{2,1,0:T(8,128)S(1)}, f32[4,16,1536]{2,1,0:T(8,128)S(1)}, u32[]{:S(2)}, u32[]{:S(2)}) collective-permute-start(f32[4,16,1536]{2,1,0:T(8,128)S(1)} %pad_maximum_fusion.1), channel_id=1, source_target_pairs={{0,1},{1,0},{2,3},{3,2},{4,5},{5,4},{6,7},{7,6},{8,9},{9,8},{10,11... | collective-permute-start | bytes 1179656 | tf_op jit(solution)/shard_map/ppermute | solution.py:270
  40.7 14.5 %collective-permute-start.13 = (f32[256,512]{1,0:T(8,128)S(1)}, f32[256,512]{1,0:T(8,128)S(1)}, u32[]{:S(2)}, u32[]{:S(2)}) collective-permute-start(f32[256,512]{1,0:T(8,128)S(1)} %pad_maximum_fusion.v_ref), channel_id=1, source_target_pairs={{0,224},{16,240},{32,64},{48,80},{64,32},{80,48},{96,128},{112,144... | collective-permute-start | bytes 1572872 | tf_op jit(solution)/shard_map/ppermute | solution.py:254
  46.1 1.6 %collective-permute-start.12 = (f32[8,32,128]{2,1,0:T(8,128)S(1)}, f32[8,32,128]{2,1,0:T(8,128)S(1)}, u32[]{:S(2)}, u32[]{:S(2)}) collective-permute-start(f32[8,32,128]{2,1,0:T(8,128)S(1)} %get-tuple-element.48), channel_id=1, source_target_pairs={{0,1},{1,0},{2,3},{3,2},{4,5},{5,4},{6,7},{7,6},{8,9},{9,8},{10,11... | collective-permute-start | bytes 393224 | tf_op jit(solution)/shard_map/ppermute | solution.py:274
  48.4 11.5 %all-to-all-start = ((f32[8,32,128]{2,1,0:T(8,128)}), f32[8,32,128]{2,1,0:T(8,128)S(1)}, u32[]{:S(2)}, u32[]{:S(2)}) async-start(f32[8,32,128]{2,1,0:T(8,128)} %add.35), calls=%async_computation | async-start | bytes 262144 | tf_op jit(solution)/shard_map/all_to_all | solution.py:275

commit v4 on v3

--- a/solution.py
+++ b/solution.py
@@ -12,9 +12,9 @@
 K = 8192
 TB = 512
 EPS = 1e-06
-STEP_A, STEP_F, STEP_Y, STEP_B = 0, 1, 2, 3
+STEP_A, STEP_F, STEP_B, STEP_Y = 0, 1, 2, 3
 VMEM = 20 * 1024 * 1024
-STEPS = (3, 3, 3, 3)
+STEPS = (4, 4, 4)
 DEPTH = 3
 
 NT = (((1,), (1,)), ((), ()))
@@ -258,20 +258,22 @@
     far = from_group(STEP_A, near)
     mine = keep + lax.ppermute(send, "tp", swap_core)
     came = [lax.ppermute(mine[k], "tp", turn_x[k]) for k in (1, 2, 3)]
-    came[0], near = tie((came[0], jnp.concatenate([near, far], 0)))
+    near = jnp.concatenate([near, far], 0)
     far = from_group(STEP_F, near)
     mine = mine[0] + came[0] + came[1] + came[2]
     mine = mine + lax.ppermute(mine, "tp", swap_y)
-    mine, near = tie((mine, jnp.concatenate([near, far], 0)))
+    mine, near, far = tie((mine, near, far))
+    near = jnp.concatenate([near, far], 0)
     own = [mine] + [lax.ppermute(mine, "tp", turn_x[k]) for k in (1, 2, 3)]
+    far = from_group(STEP_B, near)
+    own, near = tie((own, jnp.concatenate([near, far], 0)))
     far = from_group(STEP_Y, near)
-    own, near = tie((own, jnp.concatenate([near, far], 0)))
-    far = from_group(STEP_B, near)
     other = lax.ppermute(jnp.stack(own), "tp", swap_core)
+    keep, send = feature_shares(where, x, g, own, other, bits, tp)
+    send, near = tie((send, near))
     near = valid_terms(near, rank)
-    other, near = tie((other, near))
-    keep, send = feature_shares(where, x, g, own, other, bits, tp)
     came = lax.ppermute(send, "tp", swap_core)
+    came, near = tie((came, near))
     shares = lax.all_to_all(keep + came, "tp", 0, 0, axis_index_groups=same_core, tiled=True)
     far = valid_terms(far, rank)
     dots = partial_dots(where, shares, [*near, *far], rank)

time: 73.6 us -> 72.7 us (0.988)
  waiting for transfers between devices: 18 us -> 14.7 us
  starting transfers between devices: 29.7 us -> 32.6 us
    ppermute x4, starting transfers between devices: 8.42 us -> 11.4 us  [from_group(): return lax.ppermute(rows, 'grp', flips(step))]
    ppermute x3, waiting for transfers between devices: 2.41 us -> 0.01 us  [on_device(): came = [lax.ppermute(mine[k], 'tp', turn_x[k]) for k in (1, 2, 3)]]
    ppermute x3, waiting for transfers between devices: 3.32 us -> 2.47 us  [on_device(): own = [mine] + [lax.ppermute(mine, 'tp', turn_x[k]) for k in (1, 2, 3)]]
  transfers between devices with their start and end apart: 15 -> 15, of which waited for: 9 -> 8; matrix products, arithmetic and copies ran while one was open for 1% -> 1% of each run, Pallas kernels for 6% -> 6%
where the time goes in v4:
time: 72.7 us; the launch traced here: 72.5 us
  starting transfers between devices  32.6 us (45%)
  waiting for transfers between devices  14.7 us (20%)
  Pallas kernels  11.8 us (16%)
  blocking collectives  11.7 us (16%)
  other arithmetic  1.61 us (2%)
    all_to_all x1, blocking collectives, on_device(): dots = lax.all_to_all(dots, 'tp', 0, 0, tiled=True)  11.7 us
    ppermute x4, starting transfers between devices, from_group(): return lax.ppermute(rows, 'grp', flips(step))  11.4 us
    pallas_call x1, Pallas kernels, rank_rows(): pl.pallas_call(rows_kernel, in_specs=[pl.BlockSpec(memory_space=pltpu.SME...  6.69 us
    all_to_all x1, starting transfers between devices, on_device(): lax.all_to_all(keep + came, 'tp', 0, 0, axis_index_groups=same_core, tile...  4.85 us
    ppermute x4, waiting for transfers between devices, from_group(): return lax.ppermute(rows, 'grp', flips(step))  4.35 us
    ppermute x1, starting transfers between devices, on_device(): other = lax.ppermute(jnp.stack(own), 'tp', swap_core)  4.35 us
    all_to_all x1, waiting for transfers between devices, on_device(): lax.all_to_all(keep + came, 'tp', 0, 0, axis_index_groups=same_core, tile...  4.03 us
    ppermute x1, starting transfers between devices, on_device(): mine = keep + lax.ppermute(send, 'tp', swap_core)  3.33 us
  transfers between devices with their start and end apart: 15, of which 8 were waited for; matrix products, arithmetic and copies ran while one was open for 1% of the time, Pallas kernels for 6%

profile of v4, /device:TPU:1, one launch (start us, length us, event | category | flops | bytes accessed | tf_op | source)
XLA Modules:
  0.0 72.5 jit_solution(12987645899164556705)
XLA Ops:
  0.0 0.1 pad_add_fusion.where_ref
  0.1 0.0 copy-start.1
  0.1 0.0 copy-start
  0.1 6.7 %rank_rows.1 = (f32[4,16,1536]{2,1,0:T(8,128)S(1)}, f32[4,16,1536]{2,1,0:T(8,128)S(1)}, bf16[6144,512]{1,0:T(8,128)(2,1)S(1)}, bf16[6144,512]{1,0:T(8,128)(2,1)S(1)}) custom-call(s32[3]{0:T(128)S(1)} %pad_add_fusion.where_ref, bf16[6144,512]{1,0:T(8,128)(2,1)} %x_ref.1, bf16[6144,512]{1,0:T(8,128)(2,1)} %g_ref.1, bf16[16,512]{1,0:T(8,128)(2,1)} %bitcast.28, ...), custom_call_target="tpu_custom_call" | custom-call | flops 201326592 | bytes 12582912 | tf_op jit(solution)/shard_map/rank_rows/pallas_call | solution.py:80
  6.8 3.3 %collective-permute-start = (f32[4,16,1536]{2,1,0:T(8,128)S(1)}, f32[4,16,1536]{2,1,0:T(8,128)S(1)}, u32[]{:S(2)}, u32[]{:S(2)}) collective-permute-start(f32[4,16,1536]{2,1,0:T(8,128)S(1)} %get-tuple-element.34), channel_id=1, source_target_pairs={{0,1},{1,0},{2,3},{3,2},{4,5},{5,4},{6,7},{7,6},{8,9},{9,8},{10,11... | collective-permute-start | bytes 1179656 | tf_op jit(solution)/shard_map/ppermute | solution.py:259
  10.1 0.0 copy-done.1
  10.1 0.0 collective-permute-start.5
  10.1 1.3 %collective-permute-done = f32[4,16,1536]{2,1,0:T(8,128)S(1)} collective-permute-done((f32[4,16,1536]{2,1,0:T(8,128)S(1)}, f32[4,16,1536]{2,1,0:T(8,128)S(1)}, u32[]{:S(2)}, u32[]{:S(2)}) %collective-permute-start) | collective-permute-done | bytes 393248 | tf_op jit(solution)/shard_map/ppermute | solution.py:259
  11.5 0.1 collective-permute-start.1
  11.6 2.7 %collective-permute-start.3 = (f32[16,1536]{1,0:T(8,128)S(1)}, f32[16,1536]{1,0:T(8,128)S(1)}, u32[]{:S(2)}, u32[]{:S(2)}) collective-permute-start(f32[16,1536]{1,0:T(8,128)S(1)} %get-tuple-element.56), channel_id=1, source_target_pairs={{0,6},{1,7},{2,0},{3,1},{4,2},{5,3},{6,4},{7,5},{8,14},{9,15},{10,... | collective-permute-start | bytes 294920 | tf_op jit(solution)/shard_map/ppermute | solution.py:260
  14.3 0.1 collective-permute-start.2
  14.4 0.0 collective-permute-done.5
  14.4 6.7 %collective-permute-start.6 = (f32[64,512]{1,0:T(8,128)S(1)}, f32[64,512]{1,0:T(8,128)S(1)}, u32[]{:S(2)}, u32[]{:S(2)}) collective-permute-start(f32[64,512]{1,0:T(8,128)S(1)} %constant_dynamic-update-slice_fusion), channel_id=1, source_target_pairs={{0,128},{16,144},{32,160},{48,176},{64,192},{80,208},{96,224},{112... | collective-permute-start | bytes 393224 | tf_op jit(solution)/shard_map/ppermute | solution.py:254
  21.1 0.0 collective-permute-done.1
  21.1 0.0 collective-permute-done.3
  21.1 0.0 collective-permute-done.2
  21.1 3.0 %collective-permute-start.4 = (f32[16,1536]{1,0:T(8,128)S(1)}, f32[16,1536]{1,0:T(8,128)S(1)}, u32[]{:S(2)}, u32[]{:S(2)}) collective-permute-start(f32[16,1536]{1,0:T(8,128)S(1)} %fusion.2), channel_id=1, source_target_pairs={{0,8},{1,9},{2,10},{3,11},{4,12},{5,13},{6,14},{7,15},{8,0},{9,1},... | collective-permute-start | bytes 294920 | tf_op jit(solution)/shard_map/ppermute | solution.py:264
  24.1 2.1 %collective-permute-done.4 = f32[16,1536]{1,0:T(8,128)S(1)} collective-permute-done((f32[16,1536]{1,0:T(8,128)S(1)}, f32[16,1536]{1,0:T(8,128)S(1)}, u32[]{:S(2)}, u32[]{:S(2)}) %collective-permute-start.4) | collective-permute-done | bytes 98336 | tf_op jit(solution)/shard_map/ppermute | solution.py:264
  26.2 0.0 collective-permute-done.6
  26.3 3.4 %collective-permute-start.10 = (f32[128,512]{1,0:T(8,128)S(1)}, f32[128,512]{1,0:T(8,128)S(1)}, u32[]{:S(2)}, u32[]{:S(2)}) collective-permute-start(f32[128,512]{1,0:T(8,128)S(1)} %pad_maximum_fusion.2), channel_id=1, source_target_pairs={{0,224},{16,240},{32,64},{48,80},{64,32},{80,48},{96,128},{112,144... | collective-permute-start | bytes 786440 | tf_op jit(solution)/shard_map/ppermute | solution.py:254
  29.7 0.9 %collective-permute-start.9 = (f32[16,1536]{1,0:T(8,128)S(1)}, f32[16,1536]{1,0:T(8,128)S(1)}, u32[]{:S(2)}, u32[]{:S(2)}) collective-permute-start(f32[16,1536]{1,0:T(8,128)S(1)} %add.34.refs_0_), channel_id=1, source_target_pairs={{0,6},{1,7},{2,0},{3,1},{4,2},{5,3},{6,4},{7,5},{8,14},{9,15},{10,... | collective-permute-start | bytes 294920 | tf_op jit(solution)/shard_map/ppermute | solution.py:267
  30.5 1.2 %collective-permute-start.8 = (f32[16,1536]{1,0:T(8,128)S(1)}, f32[16,1536]{1,0:T(8,128)S(1)}, u32[]{:S(2)}, u32[]{:S(2)}) collective-permute-start(f32[16,1536]{1,0:T(8,128)S(1)} %add.34.refs_0_), channel_id=1, source_target_pairs={{0,4},{1,5},{2,6},{3,7},{4,0},{5,1},{6,2},{7,3},{8,12},{9,13},{10,... | collective-permute-start | bytes 294920 | tf_op jit(solution)/shard_map/ppermute | solution.py:267
  31.8 0.2 collective-permute-start.7
  32.0 2.1 %collective-permute-done.10 = f32[128,512]{1,0:T(8,128)S(1)} collective-permute-done((f32[128,512]{1,0:T(8,128)S(1)}, f32[128,512]{1,0:T(8,128)S(1)}, u32[]{:S(2)}, u32[]{:S(2)}) %collective-permute-start.10) | collective-permute-done | bytes 262176 | tf_op jit(solution)/shard_map/ppermute | solution.py:254
  34.1 0.0 collective-permute-done.9.refs_3_
  34.1 1.4 %collective-permute-done.8.refs_2_ = f32[16,1536]{1,0:T(8,128)S(1)} collective-permute-done((f32[16,1536]{1,0:T(8,128)S(1)}, f32[16,1536]{1,0:T(8,128)S(1)}, u32[]{:S(2)}, u32[]{:S(2)}) %collective-permute-start.8) | collective-permute-done | bytes 98336 | tf_op jit(solution)/shard_map/ppermute | solution.py:267
  35.5 1.0 %collective-permute-done.7.refs_1_ = f32[16,1536]{1,0:T(8,128)S(1)} collective-permute-done((f32[16,1536]{1,0:T(8,128)S(1)}, f32[16,1536]{1,0:T(8,128)S(1)}, u32[]{:S(2)}, u32[]{:S(2)}) %collective-permute-start.7) | collective-permute-done | bytes 98336 | tf_op jit(solution)/shard_map/ppermute | solution.py:267
  36.6 4.3 %collective-permute-start.11 = (f32[4,16,1536]{2,1,0:T(8,128)S(1)}, f32[4,16,1536]{2,1,0:T(8,128)S(1)}, u32[]{:S(2)}, u32[]{:S(2)}) collective-permute-start(f32[4,16,1536]{2,1,0:T(8,128)S(1)} %pad_maximum_fusion.1), channel_id=1, source_target_pairs={{0,1},{1,0},{2,3},{3,2},{4,5},{5,4},{6,7},{7,6},{8,9},{9,8},{10,11... | collective-permute-start | bytes 1179656 | tf_op jit(solution)/shard_map/ppermute | solution.py:271
  40.9 1.3 %collective-permute-start.13 = (f32[256,512]{1,0:T(8,128)S(1)}, f32[256,512]{1,0:T(8,128)S(1)}, u32[]{:S(2)}, u32[]{:S(2)}) collective-permute-start(f32[256,512]{1,0:T(8,128)S(1)} %pad_maximum_fusion.v_ref), channel_id=1, source_target_pairs={{0,16},{16,0},{32,48},{48,32},{64,80},{80,64},{96,112},{112,96},{1... | collective-permute-start | bytes 1572872 | tf_op jit(solution)/shard_map/ppermute | solution.py:254
  42.3 0.0 collective-permute-done.11.refs_4_
  42.3 0.0 copy-done
  42.3 2.9 %feature_shares.1 = (f32[8,32,128]{2,1,0:T(8,128)S(1)}, f32[8,32,128]{2,1,0:T(8,128)S(1)}) custom-call(s32[3]{0:T(128)S(1)} %pad_add_fusion.where_ref, bf16[6144,512]{1,0:T(8,128)(2,1)S(1)} %get-tuple-element.30.x_ref, bf16[6144,512]{1,0:T(8,128)(2,1)S(1)} %get-tuple-element.31.g_ref, f32[16,1536]{1,0:T(8,128)S(1)} %add.34.refs_0_, ...), custom_call_target="tpu_custom_call" | custom-call | flops 402653184 | bytes 12582912 | tf_op jit(solution)/shard_map/feature_shares/pallas_call | solution.py:133
  45.2 0.5 collective-permute-start.12
  45.6 0.6 valid_terms.2
  46.3 0.4 collective-permute-done.12
  46.6 0.7 add.35
  47.3 4.9 %all-to-all-start = ((f32[8,32,128]{2,1,0:T(8,128)}), f32[8,32,128]{2,1,0:T(8,128)S(1)}, u32[]{:S(2)}, u32[]{:S(2)}) async-start(f32[8,32,128]{2,1,0:T(8,128)} %add.35), calls=%async_computation | async-start | bytes 262144 | tf_op jit(solution)/shard_map/all_to_all | solution.py:277
  52.1 2.3 %collective-permute-done.13.v_ref = f32[256,512]{1,0:T(8,128)S(1)} collective-permute-done((f32[256,512]{1,0:T(8,128)S(1)}, f32[256,512]{1,0:T(8,128)S(1)}, u32[]{:S(2)}, u32[]{:S(2)}) %collective-permute-start.13) | collective-permute-done | bytes 524320 | tf_op jit(solution)/shard_map/ppermute | solution.py:254
  54.4 0.6 valid_terms.3
  55.1 4.0 %all-to-all-done.f_ref = f32[8,32,128]{2,1,0:T(8,128)S(1)} async-done(((f32[8,32,128]{2,1,0:T(8,128)}), f32[8,32,128]{2,1,0:T(8,128)S(1)}, u32[]{:S(2)}, u32[]{:S(2)}) %all-to-all-start) | async-done | bytes 131104 | tf_op jit(solution)/shard_map/all_to_all | solution.py:277
  59.1 1.0 %partial_dots.1 = f32[16,8,128]{2,1,0:T(8,128)S(1)} custom-call(s32[3]{0:T(128)S(1)} %pad_add_fusion.where_ref, f32[8,32,128]{2,1,0:T(8,128)S(1)} %all-to-all-done.f_ref, bf16[512,512]{1,0:T(8,128)(2,1)S(1)} %get-tuple-element.51.hl0_ref, f32[8,256]{1,0:T(8,128)S(1)} %get-tuple-element.52.sq0_ref, bf16[512,512]{1,0:T(8,128)(2,1)S(1)} %get-tuple-element.53.hl1_ref, ...), custom_call_target="tpu_custom_call" | custom-call | tf_op jit(solution)/shard_map/partial_dots/pallas_call | solution.py:225
  60.1 11.7 %all_to_all.10 = f32[16,8,128]{2,1,0:T(8,128)S(1)} all-to-all(f32[16,8,128]{2,1,0:T(8,128)S(1)} %partial_dots.1), channel_id=1, replica_groups=mesh['grp'=16,'tp'=16] {'tp'}, dimensions={0} | all-to-all | bytes 131072 | tf_op jit(solution)/shard_map/all_to_all | solution.py:280
  71.8 0.7 multiply_divide_fusion
  (11 shorter events, 0.2 us)
Async XLA Ops:
  0.1 10.0 %copy-start.1 = (f32[32,512]{1,0:T(8,128)S(1)}, f32[32,512]{1,0:T(8,128)}, u32[]{:S(2)}) copy-start(f32[32,512]{1,0:T(8,128)} %param.11) | copy-start | bytes 196612
  0.1 42.2 %copy-start = (s32[512,256]{1,0:T(8,128)S(1)}, s32[512,256]{1,0:T(8,128)}, u32[]{:S(2)}) copy-start(s32[512,256]{1,0:T(8,128)} %refs_5_.1) | copy-start | bytes 1572868
  6.8 4.7 %collective-permute-start = (f32[4,16,1536]{2,1,0:T(8,128)S(1)}, f32[4,16,1536]{2,1,0:T(8,128)S(1)}, u32[]{:S(2)}, u32[]{:S(2)}) collective-permute-start(f32[4,16,1536]{2,1,0:T(8,128)S(1)} %get-tuple-element.34), channel_id=1, source_target_pairs={{0,1},{1,0},{2,3},{3,2},{4,5},{5,4},{6,7},{7,6},{8,9},{9,8},{10,11... | collective-permute-start | bytes 1179656 | tf_op jit(solution)/shard_map/ppermute | solution.py:259
  10.1 4.3 %collective-permute-start.5 = (f32[32,512]{1,0:T(8,128)S(1)}, f32[32,512]{1,0:T(8,128)S(1)}, u32[]{:S(2)}, u32[]{:S(2)}) collective-permute-start(f32[32,512]{1,0:T(8,128)S(1)} %copy-done.1), channel_id=1, source_target_pairs={{0,32},{16,48},{32,0},{48,16},{64,96},{80,112},{96,64},{112,80},{1... | collective-permute-start | bytes 196616 | tf_op jit(solution)/shard_map/ppermute | solution.py:254
  11.5 9.6 %collective-permute-start.1 = (f32[16,1536]{1,0:T(8,128)S(1)}, f32[16,1536]{1,0:T(8,128)S(1)}, u32[]{:S(2)}, u32[]{:S(2)}) collective-permute-start(f32[16,1536]{1,0:T(8,128)S(1)} %get-tuple-element.55), channel_id=1, source_target_pairs={{0,2},{1,3},{2,4},{3,5},{4,6},{5,7},{6,0},{7,1},{8,10},{9,11},{10,... | collective-permute-start | bytes 294920 | tf_op jit(solution)/shard_map/ppermute | solution.py:260
  11.6 9.5 %collective-permute-start.3 = (f32[16,1536]{1,0:T(8,128)S(1)}, f32[16,1536]{1,0:T(8,128)S(1)}, u32[]{:S(2)}, u32[]{:S(2)}) collective-permute-start(f32[16,1536]{1,0:T(8,128)S(1)} %get-tuple-element.56), channel_id=1, source_target_pairs={{0,6},{1,7},{2,0},{3,1},{4,2},{5,3},{6,4},{7,5},{8,14},{9,15},{10,... | collective-permute-start | bytes 294920 | tf_op jit(solution)/shard_map/ppermute | solution.py:260
  14.3 6.8 %collective-permute-start.2 = (f32[16,1536]{1,0:T(8,128)S(1)}, f32[16,1536]{1,0:T(8,128)S(1)}, u32[]{:S(2)}, u32[]{:S(2)}) collective-permute-start(f32[16,1536]{1,0:T(8,128)S(1)} %get-tuple-element.57), channel_id=1, source_target_pairs={{0,4},{1,5},{2,6},{3,7},{4,0},{5,1},{6,2},{7,3},{8,12},{9,13},{10,... | collective-permute-start | bytes 294920 | tf_op jit(solution)/shard_map/ppermute | solution.py:260
  14.4 11.8 %collective-permute-start.6 = (f32[64,512]{1,0:T(8,128)S(1)}, f32[64,512]{1,0:T(8,128)S(1)}, u32[]{:S(2)}, u32[]{:S(2)}) collective-permute-start(f32[64,512]{1,0:T(8,128)S(1)} %constant_dynamic-update-slice_fusion), channel_id=1, source_target_pairs={{0,128},{16,144},{32,160},{48,176},{64,192},{80,208},{96,224},{112... | collective-permute-start | bytes 393224 | tf_op jit(solution)/shard_map/ppermute | solution.py:254
  21.1 5.1 %collective-permute-start.4 = (f32[16,1536]{1,0:T(8,128)S(1)}, f32[16,1536]{1,0:T(8,128)S(1)}, u32[]{:S(2)}, u32[]{:S(2)}) collective-permute-start(f32[16,1536]{1,0:T(8,128)S(1)} %fusion.2), channel_id=1, source_target_pairs={{0,8},{1,9},{2,10},{3,11},{4,12},{5,13},{6,14},{7,15},{8,0},{9,1},... | collective-permute-start | bytes 294920 | tf_op jit(solution)/shard_map/ppermute | solution.py:264
  26.3 7.8 %collective-permute-start.10 = (f32[128,512]{1,0:T(8,128)S(1)}, f32[128,512]{1,0:T(8,128)S(1)}, u32[]{:S(2)}, u32[]{:S(2)}) collective-permute-start(f32[128,512]{1,0:T(8,128)S(1)} %pad_maximum_fusion.2), channel_id=1, source_target_pairs={{0,224},{16,240},{32,64},{48,80},{64,32},{80,48},{96,128},{112,144... | collective-permute-start | bytes 786440 | tf_op jit(solution)/shard_map/ppermute | solution.py:254
  29.7 4.4 %collective-permute-start.9 = (f32[16,1536]{1,0:T(8,128)S(1)}, f32[16,1536]{1,0:T(8,128)S(1)}, u32[]{:S(2)}, u32[]{:S(2)}) collective-permute-start(f32[16,1536]{1,0:T(8,128)S(1)} %add.34.refs_0_), channel_id=1, source_target_pairs={{0,6},{1,7},{2,0},{3,1},{4,2},{5,3},{6,4},{7,5},{8,14},{9,15},{10,... | collective-permute-start | bytes 294920 | tf_op jit(solution)/shard_map/ppermute | solution.py:267
  30.5 5.0 %collective-permute-start.8 = (f32[16,1536]{1,0:T(8,128)S(1)}, f32[16,1536]{1,0:T(8,128)S(1)}, u32[]{:S(2)}, u32[]{:S(2)}) collective-permute-start(f32[16,1536]{1,0:T(8,128)S(1)} %add.34.refs_0_), channel_id=1, source_target_pairs={{0,4},{1,5},{2,6},{3,7},{4,0},{5,1},{6,2},{7,3},{8,12},{9,13},{10,... | collective-permute-start | bytes 294920 | tf_op jit(solution)/shard_map/ppermute | solution.py:267
  31.8 4.8 %collective-permute-start.7 = (f32[16,1536]{1,0:T(8,128)S(1)}, f32[16,1536]{1,0:T(8,128)S(1)}, u32[]{:S(2)}, u32[]{:S(2)}) collective-permute-start(f32[16,1536]{1,0:T(8,128)S(1)} %add.34.refs_0_), channel_id=1, source_target_pairs={{0,2},{1,3},{2,4},{3,5},{4,6},{5,7},{6,0},{7,1},{8,10},{9,11},{10,... | collective-permute-start | bytes 294920 | tf_op jit(solution)/shard_map/ppermute | solution.py:267
  36.6 5.7 %collective-permute-start.11 = (f32[4,16,1536]{2,1,0:T(8,128)S(1)}, f32[4,16,1536]{2,1,0:T(8,128)S(1)}, u32[]{:S(2)}, u32[]{:S(2)}) collective-permute-start(f32[4,16,1536]{2,1,0:T(8,128)S(1)} %pad_maximum_fusion.1), channel_id=1, source_target_pairs={{0,1},{1,0},{2,3},{3,2},{4,5},{5,4},{6,7},{7,6},{8,9},{9,8},{10,11... | collective-permute-start | bytes 1179656 | tf_op jit(solution)/shard_map/ppermute | solution.py:271
  40.9 13.5 %collective-permute-start.13 = (f32[256,512]{1,0:T(8,128)S(1)}, f32[256,512]{1,0:T(8,128)S(1)}, u32[]{:S(2)}, u32[]{:S(2)}) collective-permute-start(f32[256,512]{1,0:T(8,128)S(1)} %pad_maximum_fusion.v_ref), channel_id=1, source_target_pairs={{0,16},{16,0},{32,48},{48,32},{64,80},{80,64},{96,112},{112,96},{1... | collective-permute-start | bytes 1572872 | tf_op jit(solution)/shard_map/ppermute | solution.py:254
  45.2 1.4 %collective-permute-start.12 = (f32[8,32,128]{2,1,0:T(8,128)S(1)}, f32[8,32,128]{2,1,0:T(8,128)S(1)}, u32[]{:S(2)}, u32[]{:S(2)}) collective-permute-start(f32[8,32,128]{2,1,0:T(8,128)S(1)} %get-tuple-element.46), channel_id=1, source_target_pairs={{0,1},{1,0},{2,3},{3,2},{4,5},{5,4},{6,7},{7,6},{8,9},{9,8},{10,11... | collective-permute-start | bytes 393224 | tf_op jit(solution)/shard_map/ppermute | solution.py:275
  47.3 11.8 %all-to-all-start = ((f32[8,32,128]{2,1,0:T(8,128)}), f32[8,32,128]{2,1,0:T(8,128)S(1)}, u32[]{:S(2)}, u32[]{:S(2)}) async-start(f32[8,32,128]{2,1,0:T(8,128)} %add.35), calls=%async_computation | async-start | bytes 262144 | tf_op jit(solution)/shard_map/all_to_all | solution.py:277

commit v5 on v4

--- a/solution.py
+++ b/solution.py
@@ -14,8 +14,8 @@
 EPS = 1e-06
 STEP_A, STEP_F, STEP_B, STEP_Y = 0, 1, 2, 3
 VMEM = 20 * 1024 * 1024
-STEPS = (4, 4, 4)
-DEPTH = 3
+STEPS = (6, 6)
+DEPTH = 2
 
 NT = (((1,), (1,)), ((), ()))
 NN = (((1,), (0,)), ((), ()))
@@ -31,8 +31,8 @@
     return jnp.concatenate([hi, lo], 0)
 
 
-def rows_kernel(where_ref, x_ref, g_ref, a_ref, b_ref, keep_ref, send_ref, xs_ref, gs_ref, at_ref, bs_ref, sem, sem_w):
-    first = where_ref[0] == 0
+def rows_kernel(x_ref, g_ref, a_ref, b_ref, keep_ref, send_ref, xs_ref, gs_ref, at_ref, bs_ref, sem, sem_w):
+    first = (lax.axis_index("tp") & 1) == 0
     per = keep_ref.shape[2] // TB
     weights = [
         pltpu.make_async_copy(src, dst, sem_w.at[j])
@@ -58,7 +58,7 @@
         for i in blocks:
             rows = slice(i * TB, (i + 1) * TB)
             cols = slice(i % per * TB, (i % per + 1) * TB)
-            slot = (i // per - where_ref[2]) & 3
+            slot = (i // per - (lax.axis_index("tp") >> 1 & 3)) & 3
             if j == 0:
                 keep_ref[slot, :, cols] = mm(at_ref[...], xs_ref[rows], NT)
             else:
@@ -68,7 +68,7 @@
                 send_ref[slot, :, cols] = jnp.where(first, up, down)
 
 
-def rank_rows(where, x, g, a, b):
+def rank_rows(x, g, a, b):
     tokens, width = x.shape
     rank = b.shape[0]
     chunk = tokens // 4
@@ -79,7 +79,7 @@
     x, g, a, b = (pltpu.with_memory_space_constraint(v, pltpu.HBM) for v in (x, g, a, b))
     return pl.pallas_call(
         rows_kernel,
-        in_specs=[pl.BlockSpec(memory_space=pltpu.SMEM), far, far, far, far],
+        in_specs=[far] * 4,
         out_specs=[whole] * 4,
         out_shape=[out, out, near, near],
         scratch_shapes=[
@@ -93,16 +93,16 @@
             flops=4 * tokens * width * rank, bytes_accessed=4 * tokens * width, transcendentals=0
         ),
         name="rank_rows",
-    )(where, x, g, a, b)
-
-
-def share_kernel(where_ref, x_ref, g_ref, *refs):
+    )(x, g, a, b)
+
+
+def share_kernel(x_ref, g_ref, *refs):
     own_refs, (other_ref, s_ref, keep_ref, send_ref, v_ref) = refs[:4], refs[4:]
     rank, chunk = own_refs[0].shape
     per = chunk // TB
-    first = where_ref[0] == 0
+    first = (lax.axis_index("tp") & 1) == 0
     for j, own_ref in enumerate(own_refs):
-        begin = ((where_ref[2] - j) & 3) * per
+        begin = (((lax.axis_index("tp") >> 1 & 3) - j) & 3) * per
         for c in range(per):
             rows = pl.ds(pl.multiple_of((begin + c) * TB, TB), TB)
             cols = slice(c * TB, (c + 1) * TB)
@@ -124,7 +124,7 @@
             send_ref[m * each + n] = jnp.where(first, f[n, 1], f[n, 0])
 
 
-def feature_shares(where, x, g, own, other, bits, parts):
+def feature_shares(x, g, own, other, bits, parts):
     tokens, width = x.shape
     rank = own[0].shape[0]
     kd = bits.shape[1]
@@ -132,7 +132,7 @@
     x, g = (pltpu.with_memory_space_constraint(v, pltpu.VMEM) for v in (x, g))
     return pl.pallas_call(
         share_kernel,
-        in_specs=[pl.BlockSpec(memory_space=pltpu.SMEM)] + [whole] * (len(own) + 4),
+        in_specs=[whole] * (len(own) + 4),
         out_specs=[whole] * 2,
         out_shape=[jax.ShapeDtypeStruct((parts // 2, 2 * kd // parts, 128), jnp.float32)] * 2,
         scratch_shapes=[pltpu.VMEM((2, tokens // TB, rank, width), jnp.float32)],
@@ -141,7 +141,7 @@
             flops=8 * tokens * width * rank, bytes_accessed=4 * tokens * width, transcendentals=0
         ),
         name="feature_shares",
-    )(where, x, g, *own, other, bits)
+    )(x, g, *own, other, bits)
 
 
 def valid_kernel(rank, v_ref, hl_ref, sq_ref):
@@ -201,36 +201,40 @@
     return z * 2 + y
 
 
-def dot_kernel(rank, where_ref, f_ref, hl0_ref, sq0_ref, hl1_ref, sq1_ref, out_ref, t_ref):
+def dot_kernel(rank, f_ref, hl0_ref, sq0_ref, hl1_ref, sq1_ref, out_ref, t_ref):
     parts = out_ref.shape[0]
     rows = sq0_ref.shape[1]
     each = 2 * rows // parts
     t_ref[...] = jnp.transpose(jnp.sum(f_ref[...], 0))
     f = jnp.concatenate([t_ref[pl.ds(r, 8, stride=rank), :] for r in range(rank)], 1)
-    own_sq = jnp.broadcast_to(jnp.sum(f * f, 1, keepdims=True), (8, each))
+    own_sq = jnp.broadcast_to(jnp.sum(f * f, 1, keepdims=True), (8, 128))
+    lane = lax.broadcasted_iota(jnp.int32, (8, 128), 1)
+    origins = [origin(n, lax.axis_index("grp")) for n in range(parts // 2)]
     f = halves(f)
     for half, (hl_ref, sq_ref) in enumerate(((hl0_ref, sq0_ref), (hl1_ref, sq1_ref))):
         prod = mm(f, hl_ref[...], NN)
         dots = prod[:8, :rows] + (prod[8:, :rows] + prod[:8, rows:]) + prod[8:, rows:]
         line = lax.broadcasted_iota(jnp.int32, dots.shape, 0)
         dots = jnp.where(line == 6, sq_ref[...], dots)
-        for n in range(parts // 2):
-            part = origin(half * parts // 2 + n, where_ref[1])
-            out_ref[part, :, :each] = dots[:, n * each : (n + 1) * each]
-            out_ref[part, :, each : 2 * each] = own_sq
-
-
-def partial_dots(where, f, terms, rank):
+        for n, part in enumerate(origins):
+            begin, turn = divmod(n * each, 128)
+            tile = dots[:, begin * 128 : (begin + 1) * 128]
+            if turn:
+                tile = pltpu.roll(tile, 128 - turn, 1)
+            out_ref[part ^ half] = jnp.where(lane < each, tile, own_sq)
+
+
+def partial_dots(f, terms, rank):
     whole = pl.BlockSpec(memory_space=pltpu.VMEM)
     return pl.pallas_call(
         functools.partial(dot_kernel, rank),
-        in_specs=[pl.BlockSpec(memory_space=pltpu.SMEM)] + [whole] * 5,
+        in_specs=[whole] * 5,
         out_specs=whole,
         out_shape=jax.ShapeDtypeStruct((2 * f.shape[0], 8, 128), jnp.float32),
         scratch_shapes=[pltpu.VMEM((128, f.shape[1]), jnp.float32)],
         compiler_params=pltpu.CompilerParams(vmem_limit_bytes=VMEM // 2),
         name="partial_dots",
-    )(where, f, *terms)
+    )(f, *terms)
 
 
 def on_device(x, g, a, b, bits, valid):
@@ -238,8 +242,6 @@
     rank = b.shape[0]
     seqs = x.shape[0] // LEN
     each = 16 * valid.shape[0] // tp
-    index = lax.axis_index("tp")
-    where = jnp.stack([index & 1, lax.axis_index("grp"), index >> 1 & 3]).astype(jnp.int32)
     swap_core = [(i, i ^ 1) for i in range(tp)]
     swap_y = [(i, i ^ 8) for i in range(tp)]
     same_core = [list(range(c, tp, 2)) for c in range(2)]
@@ -253,7 +255,7 @@
     def from_group(step, rows):
         return lax.ppermute(rows, "grp", flips(step))
 
-    keep, send, x, g = rank_rows(where, x, g, jnp.transpose(a), b)
+    keep, send, x, g = rank_rows(x, g, jnp.transpose(a), b)
     send, near = tie((send, valid))
     far = from_group(STEP_A, near)
     mine = keep + lax.ppermute(send, "tp", swap_core)
@@ -269,14 +271,14 @@
     own, near = tie((own, jnp.concatenate([near, far], 0)))
     far = from_group(STEP_Y, near)
     other = lax.ppermute(jnp.stack(own), "tp", swap_core)
-    keep, send = feature_shares(where, x, g, own, other, bits, tp)
+    keep, send = feature_shares(x, g, own, other, bits, tp)
     send, near = tie((send, near))
     near = valid_terms(near, rank)
     came = lax.ppermute(send, "tp", swap_core)
     came, near = tie((came, near))
     shares = lax.all_to_all(keep + came, "tp", 0, 0, axis_index_groups=same_core, tiled=True)
     far = valid_terms(far, rank)
-    dots = partial_dots(where, shares, [*near, *far], rank)
+    dots = partial_dots(shares, [*near, *far], rank)
     dots = lax.all_to_all(dots, "tp", 0, 0, tiled=True)
     total = jnp.sum(dots, 0)
     train = math.sqrt(K) / jnp.sqrt(total[:seqs, each : 2 * each] + EPS)

time: 72.7 us -> 71 us (0.977)
  Pallas kernels: 11.8 us -> 10.1 us
    pallas_call x3, Pallas kernels: 10.6 us -> 8.92 us  [the longest x1 6.1 us: rank_rows(): pl.pallas_call(rows_kernel, in_specs=[far] * 4, out_specs=[whole] * 4, ou...]
  transfers between devices with their start and end apart: 15 -> 15, of which waited for: 8 -> 8; matrix products, arithmetic and copies ran while one was open for 1% -> 1% of each run, Pallas kernels for 6% -> 5%
where the time goes in v5:
time: 71 us; the launch traced here: 70.7 us
  starting transfers between devices  32.6 us (46%)
  waiting for transfers between devices  14.7 us (21%)
  blocking collectives  11.7 us (16%)
  Pallas kernels  10.1 us (14%)
  other arithmetic  1.54 us (2%)
    all_to_all x1, blocking collectives, on_device(): dots = lax.all_to_all(dots, 'tp', 0, 0, tiled=True)  11.7 us
    ppermute x4, starting transfers between devices, from_group(): return lax.ppermute(rows, 'grp', flips(step))  11.4 us
    pallas_call x1, Pallas kernels, rank_rows(): pl.pallas_call(rows_kernel, in_specs=[far] * 4, out_specs=[whole] * 4, ou...  6.1 us
    ppermute x4, waiting for transfers between devices, from_group(): return lax.ppermute(rows, 'grp', flips(step))  4.89 us
    all_to_all x1, starting transfers between devices, on_device(): lax.all_to_all(keep + came, 'tp', 0, 0, axis_index_groups=same_core, tile...  4.85 us
    ppermute x1, starting transfers between devices, on_device(): other = lax.ppermute(jnp.stack(own), 'tp', swap_core)  4.35 us
    all_to_all x1, waiting for transfers between devices, on_device(): lax.all_to_all(keep + came, 'tp', 0, 0, axis_index_groups=same_core, tile...  3.5 us
    ppermute x1, starting transfers between devices, on_device(): mine = keep + lax.ppermute(send, 'tp', swap_core)  3.33 us
  transfers between devices with their start and end apart: 15, of which 8 were waited for; matrix products, arithmetic and copies ran while one was open for 1% of the time, Pallas kernels for 5%

profile of v5, /device:TPU:1, one launch (start us, length us, event | category | flops | bytes accessed | tf_op | source)
XLA Modules:
  0.0 70.7 jit_solution(16022464024578057772)
XLA Ops:
  0.0 0.0 copy-start.1
  0.0 0.0 copy-start
  0.0 6.1 %rank_rows.1 = (f32[4,16,1536]{2,1,0:T(8,128)S(1)}, f32[4,16,1536]{2,1,0:T(8,128)S(1)}, bf16[6144,512]{1,0:T(8,128)(2,1)S(1)}, bf16[6144,512]{1,0:T(8,128)(2,1)S(1)}) custom-call(bf16[6144,512]{1,0:T(8,128)(2,1)} %x_ref.1, bf16[6144,512]{1,0:T(8,128)(2,1)} %g_ref.1, bf16[16,512]{1,0:T(8,128)(2,1)} %bitcast.25, bf16[16,512]{1,0:T(8,128)(2,1)} %b_ref.1), custom_call_target="tpu_custom_call" | custom-call | flops 201326592 | bytes 12582912 | tf_op jit(solution)/shard_map/rank_rows/pallas_call | solution.py:80
  6.1 3.3 %collective-permute-start = (f32[4,16,1536]{2,1,0:T(8,128)S(1)}, f32[4,16,1536]{2,1,0:T(8,128)S(1)}, u32[]{:S(2)}, u32[]{:S(2)}) collective-permute-start(f32[4,16,1536]{2,1,0:T(8,128)S(1)} %get-tuple-element.34), channel_id=1, source_target_pairs={{0,1},{1,0},{2,3},{3,2},{4,5},{5,4},{6,7},{7,6},{8,9},{9,8},{10,11... | collective-permute-start | bytes 1179656 | tf_op jit(solution)/shard_map/ppermute | solution.py:261
  9.4 0.0 copy-done.1
  9.4 0.0 collective-permute-start.5
  9.5 1.3 %collective-permute-done = f32[4,16,1536]{2,1,0:T(8,128)S(1)} collective-permute-done((f32[4,16,1536]{2,1,0:T(8,128)S(1)}, f32[4,16,1536]{2,1,0:T(8,128)S(1)}, u32[]{:S(2)}, u32[]{:S(2)}) %collective-permute-start) | collective-permute-done | bytes 393248 | tf_op jit(solution)/shard_map/ppermute | solution.py:261
  10.9 0.1 collective-permute-start.1
  11.0 2.7 %collective-permute-start.3 = (f32[16,1536]{1,0:T(8,128)S(1)}, f32[16,1536]{1,0:T(8,128)S(1)}, u32[]{:S(2)}, u32[]{:S(2)}) collective-permute-start(f32[16,1536]{1,0:T(8,128)S(1)} %get-tuple-element.56), channel_id=1, source_target_pairs={{0,6},{1,7},{2,0},{3,1},{4,2},{5,3},{6,4},{7,5},{8,14},{9,15},{10,... | collective-permute-start | bytes 294920 | tf_op jit(solution)/shard_map/ppermute | solution.py:262
  13.6 0.1 collective-permute-start.2
  13.8 0.0 collective-permute-done.5
  13.8 6.7 %collective-permute-start.6 = (f32[64,512]{1,0:T(8,128)S(1)}, f32[64,512]{1,0:T(8,128)S(1)}, u32[]{:S(2)}, u32[]{:S(2)}) collective-permute-start(f32[64,512]{1,0:T(8,128)S(1)} %constant_dynamic-update-slice_fusion), channel_id=1, source_target_pairs={{0,128},{16,144},{32,160},{48,176},{64,192},{80,208},{96,224},{112... | collective-permute-start | bytes 393224 | tf_op jit(solution)/shard_map/ppermute | solution.py:256
  20.4 0.0 collective-permute-done.1
  20.4 0.0 collective-permute-done.3
  20.4 0.0 collective-permute-done.2
  20.5 3.0 %collective-permute-start.4 = (f32[16,1536]{1,0:T(8,128)S(1)}, f32[16,1536]{1,0:T(8,128)S(1)}, u32[]{:S(2)}, u32[]{:S(2)}) collective-permute-start(f32[16,1536]{1,0:T(8,128)S(1)} %fusion.2), channel_id=1, source_target_pairs={{0,8},{1,9},{2,10},{3,11},{4,12},{5,13},{6,14},{7,15},{8,0},{9,1},... | collective-permute-start | bytes 294920 | tf_op jit(solution)/shard_map/ppermute | solution.py:266
  23.5 2.1 %collective-permute-done.4 = f32[16,1536]{1,0:T(8,128)S(1)} collective-permute-done((f32[16,1536]{1,0:T(8,128)S(1)}, f32[16,1536]{1,0:T(8,128)S(1)}, u32[]{:S(2)}, u32[]{:S(2)}) %collective-permute-start.4) | collective-permute-done | bytes 98336 | tf_op jit(solution)/shard_map/ppermute | solution.py:266
  25.6 0.0 collective-permute-done.6
  25.6 3.4 %collective-permute-start.10 = (f32[128,512]{1,0:T(8,128)S(1)}, f32[128,512]{1,0:T(8,128)S(1)}, u32[]{:S(2)}, u32[]{:S(2)}) collective-permute-start(f32[128,512]{1,0:T(8,128)S(1)} %pad_maximum_fusion.2), channel_id=1, source_target_pairs={{0,224},{16,240},{32,64},{48,80},{64,32},{80,48},{96,128},{112,144... | collective-permute-start | bytes 786440 | tf_op jit(solution)/shard_map/ppermute | solution.py:256
  29.0 0.9 %collective-permute-start.9 = (f32[16,1536]{1,0:T(8,128)S(1)}, f32[16,1536]{1,0:T(8,128)S(1)}, u32[]{:S(2)}, u32[]{:S(2)}) collective-permute-start(f32[16,1536]{1,0:T(8,128)S(1)} %add.34.refs_0_), channel_id=1, source_target_pairs={{0,6},{1,7},{2,0},{3,1},{4,2},{5,3},{6,4},{7,5},{8,14},{9,15},{10,... | collective-permute-start | bytes 294920 | tf_op jit(solution)/shard_map/ppermute | solution.py:269
  29.9 1.2 %collective-permute-start.8 = (f32[16,1536]{1,0:T(8,128)S(1)}, f32[16,1536]{1,0:T(8,128)S(1)}, u32[]{:S(2)}, u32[]{:S(2)}) collective-permute-start(f32[16,1536]{1,0:T(8,128)S(1)} %add.34.refs_0_), channel_id=1, source_target_pairs={{0,4},{1,5},{2,6},{3,7},{4,0},{5,1},{6,2},{7,3},{8,12},{9,13},{10,... | collective-permute-start | bytes 294920 | tf_op jit(solution)/shard_map/ppermute | solution.py:269
  31.1 0.2 collective-permute-start.7
  31.3 2.1 %collective-permute-done.10 = f32[128,512]{1,0:T(8,128)S(1)} collective-permute-done((f32[128,512]{1,0:T(8,128)S(1)}, f32[128,512]{1,0:T(8,128)S(1)}, u32[]{:S(2)}, u32[]{:S(2)}) %collective-permute-start.10) | collective-permute-done | bytes 262176 | tf_op jit(solution)/shard_map/ppermute | solution.py:256
  33.4 0.0 collective-permute-done.9.refs_3_
  33.4 1.4 %collective-permute-done.8.refs_2_ = f32[16,1536]{1,0:T(8,128)S(1)} collective-permute-done((f32[16,1536]{1,0:T(8,128)S(1)}, f32[16,1536]{1,0:T(8,128)S(1)}, u32[]{:S(2)}, u32[]{:S(2)}) %collective-permute-start.8) | collective-permute-done | bytes 98336 | tf_op jit(solution)/shard_map/ppermute | solution.py:269
  34.9 1.0 %collective-permute-done.7.refs_1_ = f32[16,1536]{1,0:T(8,128)S(1)} collective-permute-done((f32[16,1536]{1,0:T(8,128)S(1)}, f32[16,1536]{1,0:T(8,128)S(1)}, u32[]{:S(2)}, u32[]{:S(2)}) %collective-permute-start.7) | collective-permute-done | bytes 98336 | tf_op jit(solution)/shard_map/ppermute | solution.py:269
  35.9 4.3 %collective-permute-start.11 = (f32[4,16,1536]{2,1,0:T(8,128)S(1)}, f32[4,16,1536]{2,1,0:T(8,128)S(1)}, u32[]{:S(2)}, u32[]{:S(2)}) collective-permute-start(f32[4,16,1536]{2,1,0:T(8,128)S(1)} %pad_maximum_fusion.1), channel_id=1, source_target_pairs={{0,1},{1,0},{2,3},{3,2},{4,5},{5,4},{6,7},{7,6},{8,9},{9,8},{10,11... | collective-permute-start | bytes 1179656 | tf_op jit(solution)/shard_map/ppermute | solution.py:273
  40.3 1.3 %collective-permute-start.13 = (f32[256,512]{1,0:T(8,128)S(1)}, f32[256,512]{1,0:T(8,128)S(1)}, u32[]{:S(2)}, u32[]{:S(2)}) collective-permute-start(f32[256,512]{1,0:T(8,128)S(1)} %pad_maximum_fusion.v_ref), channel_id=1, source_target_pairs={{0,16},{16,0},{32,48},{48,32},{64,80},{80,64},{96,112},{112,96},{1... | collective-permute-start | bytes 1572872 | tf_op jit(solution)/shard_map/ppermute | solution.py:256
  41.6 0.0 collective-permute-done.11.refs_4_
  41.6 0.0 copy-done
  41.6 2.3 %feature_shares.1 = (f32[8,32,128]{2,1,0:T(8,128)S(1)}, f32[8,32,128]{2,1,0:T(8,128)S(1)}) custom-call(bf16[6144,512]{1,0:T(8,128)(2,1)S(1)} %get-tuple-element.30.x_ref, bf16[6144,512]{1,0:T(8,128)(2,1)S(1)} %get-tuple-element.31.g_ref, f32[16,1536]{1,0:T(8,128)S(1)} %add.34.refs_0_, f32[16,1536]{1,0:T(8,128)S(1)} %collective-permute-done.7.refs_1_, ...), custom_call_target="tpu_custom_call" | custom-call | flops 402653184 | bytes 12582912 | tf_op jit(solution)/shard_map/feature_shares/pallas_call | solution.py:133
  44.0 0.5 collective-permute-start.12
  44.4 0.6 valid_terms.2
  45.1 0.4 collective-permute-done.12
  45.4 0.7 add.35
  46.1 4.9 %all-to-all-start = ((f32[8,32,128]{2,1,0:T(8,128)}), f32[8,32,128]{2,1,0:T(8,128)S(1)}, u32[]{:S(2)}, u32[]{:S(2)}) async-start(f32[8,32,128]{2,1,0:T(8,128)} %add.35), calls=%async_computation | async-start | bytes 262144 | tf_op jit(solution)/shard_map/all_to_all | solution.py:279
  50.9 2.8 %collective-permute-done.13.v_ref = f32[256,512]{1,0:T(8,128)S(1)} collective-permute-done((f32[256,512]{1,0:T(8,128)S(1)}, f32[256,512]{1,0:T(8,128)S(1)}, u32[]{:S(2)}, u32[]{:S(2)}) %collective-permute-start.13) | collective-permute-done | bytes 524320 | tf_op jit(solution)/shard_map/ppermute | solution.py:256
  53.8 0.6 valid_terms.3
  54.4 3.5 %all-to-all-done.f_ref = f32[8,32,128]{2,1,0:T(8,128)S(1)} async-done(((f32[8,32,128]{2,1,0:T(8,128)}), f32[8,32,128]{2,1,0:T(8,128)S(1)}, u32[]{:S(2)}, u32[]{:S(2)}) %all-to-all-start) | async-done | bytes 131104 | tf_op jit(solution)/shard_map/all_to_all | solution.py:279
  57.9 0.5 partial_dots.1
  58.4 11.7 %all_to_all.10 = f32[16,8,128]{2,1,0:T(8,128)S(1)} all-to-all(f32[16,8,128]{2,1,0:T(8,128)S(1)} %partial_dots.1), channel_id=1, replica_groups=mesh['grp'=16,'tp'=16] {'tp'}, dimensions={0} | all-to-all | bytes 131072 | tf_op jit(solution)/shard_map/all_to_all | solution.py:282
  70.1 0.7 multiply_divide_fusion
  (11 shorter events, 0.2 us)
Async XLA Ops:
  0.0 9.4 %copy-start.1 = (f32[32,512]{1,0:T(8,128)S(1)}, f32[32,512]{1,0:T(8,128)}, u32[]{:S(2)}) copy-start(f32[32,512]{1,0:T(8,128)} %param.11) | copy-start | bytes 196612
  0.0 41.6 %copy-start = (s32[512,256]{1,0:T(8,128)S(1)}, s32[512,256]{1,0:T(8,128)}, u32[]{:S(2)}) copy-start(s32[512,256]{1,0:T(8,128)} %refs_5_.1) | copy-start | bytes 1572868
  6.1 4.7 %collective-permute-start = (f32[4,16,1536]{2,1,0:T(8,128)S(1)}, f32[4,16,1536]{2,1,0:T(8,128)S(1)}, u32[]{:S(2)}, u32[]{:S(2)}) collective-permute-start(f32[4,16,1536]{2,1,0:T(8,128)S(1)} %get-tuple-element.34), channel_id=1, source_target_pairs={{0,1},{1,0},{2,3},{3,2},{4,5},{5,4},{6,7},{7,6},{8,9},{9,8},{10,11... | collective-permute-start | bytes 1179656 | tf_op jit(solution)/shard_map/ppermute | solution.py:261
  9.4 4.3 %collective-permute-start.5 = (f32[32,512]{1,0:T(8,128)S(1)}, f32[32,512]{1,0:T(8,128)S(1)}, u32[]{:S(2)}, u32[]{:S(2)}) collective-permute-start(f32[32,512]{1,0:T(8,128)S(1)} %copy-done.1), channel_id=1, source_target_pairs={{0,32},{16,48},{32,0},{48,16},{64,96},{80,112},{96,64},{112,80},{1... | collective-permute-start | bytes 196616 | tf_op jit(solution)/shard_map/ppermute | solution.py:256
  10.9 9.6 %collective-permute-start.1 = (f32[16,1536]{1,0:T(8,128)S(1)}, f32[16,1536]{1,0:T(8,128)S(1)}, u32[]{:S(2)}, u32[]{:S(2)}) collective-permute-start(f32[16,1536]{1,0:T(8,128)S(1)} %get-tuple-element.55), channel_id=1, source_target_pairs={{0,2},{1,3},{2,4},{3,5},{4,6},{5,7},{6,0},{7,1},{8,10},{9,11},{10,... | collective-permute-start | bytes 294920 | tf_op jit(solution)/shard_map/ppermute | solution.py:262
  11.0 9.5 %collective-permute-start.3 = (f32[16,1536]{1,0:T(8,128)S(1)}, f32[16,1536]{1,0:T(8,128)S(1)}, u32[]{:S(2)}, u32[]{:S(2)}) collective-permute-start(f32[16,1536]{1,0:T(8,128)S(1)} %get-tuple-element.56), channel_id=1, source_target_pairs={{0,6},{1,7},{2,0},{3,1},{4,2},{5,3},{6,4},{7,5},{8,14},{9,15},{10,... | collective-permute-start | bytes 294920 | tf_op jit(solution)/shard_map/ppermute | solution.py:262
  13.6 6.8 %collective-permute-start.2 = (f32[16,1536]{1,0:T(8,128)S(1)}, f32[16,1536]{1,0:T(8,128)S(1)}, u32[]{:S(2)}, u32[]{:S(2)}) collective-permute-start(f32[16,1536]{1,0:T(8,128)S(1)} %get-tuple-element.57), channel_id=1, source_target_pairs={{0,4},{1,5},{2,6},{3,7},{4,0},{5,1},{6,2},{7,3},{8,12},{9,13},{10,... | collective-permute-start | bytes 294920 | tf_op jit(solution)/shard_map/ppermute | solution.py:262
  13.8 11.8 %collective-permute-start.6 = (f32[64,512]{1,0:T(8,128)S(1)}, f32[64,512]{1,0:T(8,128)S(1)}, u32[]{:S(2)}, u32[]{:S(2)}) collective-permute-start(f32[64,512]{1,0:T(8,128)S(1)} %constant_dynamic-update-slice_fusion), channel_id=1, source_target_pairs={{0,128},{16,144},{32,160},{48,176},{64,192},{80,208},{96,224},{112... | collective-permute-start | bytes 393224 | tf_op jit(solution)/shard_map/ppermute | solution.py:256
  20.5 5.1 %collective-permute-start.4 = (f32[16,1536]{1,0:T(8,128)S(1)}, f32[16,1536]{1,0:T(8,128)S(1)}, u32[]{:S(2)}, u32[]{:S(2)}) collective-permute-start(f32[16,1536]{1,0:T(8,128)S(1)} %fusion.2), channel_id=1, source_target_pairs={{0,8},{1,9},{2,10},{3,11},{4,12},{5,13},{6,14},{7,15},{8,0},{9,1},... | collective-permute-start | bytes 294920 | tf_op jit(solution)/shard_map/ppermute | solution.py:266
  25.6 7.8 %collective-permute-start.10 = (f32[128,512]{1,0:T(8,128)S(1)}, f32[128,512]{1,0:T(8,128)S(1)}, u32[]{:S(2)}, u32[]{:S(2)}) collective-permute-start(f32[128,512]{1,0:T(8,128)S(1)} %pad_maximum_fusion.2), channel_id=1, source_target_pairs={{0,224},{16,240},{32,64},{48,80},{64,32},{80,48},{96,128},{112,144... | collective-permute-start | bytes 786440 | tf_op jit(solution)/shard_map/ppermute | solution.py:256
  29.0 4.4 %collective-permute-start.9 = (f32[16,1536]{1,0:T(8,128)S(1)}, f32[16,1536]{1,0:T(8,128)S(1)}, u32[]{:S(2)}, u32[]{:S(2)}) collective-permute-start(f32[16,1536]{1,0:T(8,128)S(1)} %add.34.refs_0_), channel_id=1, source_target_pairs={{0,6},{1,7},{2,0},{3,1},{4,2},{5,3},{6,4},{7,5},{8,14},{9,15},{10,... | collective-permute-start | bytes 294920 | tf_op jit(solution)/shard_map/ppermute | solution.py:269
  29.9 5.0 %collective-permute-start.8 = (f32[16,1536]{1,0:T(8,128)S(1)}, f32[16,1536]{1,0:T(8,128)S(1)}, u32[]{:S(2)}, u32[]{:S(2)}) collective-permute-start(f32[16,1536]{1,0:T(8,128)S(1)} %add.34.refs_0_), channel_id=1, source_target_pairs={{0,4},{1,5},{2,6},{3,7},{4,0},{5,1},{6,2},{7,3},{8,12},{9,13},{10,... | collective-permute-start | bytes 294920 | tf_op jit(solution)/shard_map/ppermute | solution.py:269
  31.1 4.8 %collective-permute-start.7 = (f32[16,1536]{1,0:T(8,128)S(1)}, f32[16,1536]{1,0:T(8,128)S(1)}, u32[]{:S(2)}, u32[]{:S(2)}) collective-permute-start(f32[16,1536]{1,0:T(8,128)S(1)} %add.34.refs_0_), channel_id=1, source_target_pairs={{0,2},{1,3},{2,4},{3,5},{4,6},{5,7},{6,0},{7,1},{8,10},{9,11},{10,... | collective-permute-start | bytes 294920 | tf_op jit(solution)/shard_map/ppermute | solution.py:269
  35.9 5.7 %collective-permute-start.11 = (f32[4,16,1536]{2,1,0:T(8,128)S(1)}, f32[4,16,1536]{2,1,0:T(8,128)S(1)}, u32[]{:S(2)}, u32[]{:S(2)}) collective-permute-start(f32[4,16,1536]{2,1,0:T(8,128)S(1)} %pad_maximum_fusion.1), channel_id=1, source_target_pairs={{0,1},{1,0},{2,3},{3,2},{4,5},{5,4},{6,7},{7,6},{8,9},{9,8},{10,11... | collective-permute-start | bytes 1179656 | tf_op jit(solution)/shard_map/ppermute | solution.py:273
  40.3 13.5 %collective-permute-start.13 = (f32[256,512]{1,0:T(8,128)S(1)}, f32[256,512]{1,0:T(8,128)S(1)}, u32[]{:S(2)}, u32[]{:S(2)}) collective-permute-start(f32[256,512]{1,0:T(8,128)S(1)} %pad_maximum_fusion.v_ref), channel_id=1, source_target_pairs={{0,16},{16,0},{32,48},{48,32},{64,80},{80,64},{96,112},{112,96},{1... | collective-permute-start | bytes 1572872 | tf_op jit(solution)/shard_map/ppermute | solution.py:256
  44.0 1.5 %collective-permute-start.12 = (f32[8,32,128]{2,1,0:T(8,128)S(1)}, f32[8,32,128]{2,1,0:T(8,128)S(1)}, u32[]{:S(2)}, u32[]{:S(2)}) collective-permute-start(f32[8,32,128]{2,1,0:T(8,128)S(1)} %get-tuple-element.46), channel_id=1, source_target_pairs={{0,1},{1,0},{2,3},{3,2},{4,5},{5,4},{6,7},{7,6},{8,9},{9,8},{10,11... | collective-permute-start | bytes 393224 | tf_op jit(solution)/shard_map/ppermute | solution.py:277
  46.1 11.8 %all-to-all-start = ((f32[8,32,128]{2,1,0:T(8,128)}), f32[8,32,128]{2,1,0:T(8,128)S(1)}, u32[]{:S(2)}, u32[]{:S(2)}) async-start(f32[8,32,128]{2,1,0:T(8,128)} %add.35), calls=%async_computation | async-start | bytes 262144 | tf_op jit(solution)/shard_map/all_to_all | solution.py:279

commit v6 on v5

--- a/solution.py
+++ b/solution.py
@@ -12,7 +12,7 @@
 K = 8192
 TB = 512
 EPS = 1e-06
-STEP_A, STEP_F, STEP_B, STEP_Y = 0, 1, 2, 3
+STEP_B, STEP_F, STEP_A, STEP_Y = 0, 1, 2, 3
 VMEM = 20 * 1024 * 1024
 STEPS = (6, 6)
 DEPTH = 2
@@ -257,7 +257,7 @@
 
     keep, send, x, g = rank_rows(x, g, jnp.transpose(a), b)
     send, near = tie((send, valid))
-    far = from_group(STEP_A, near)
+    far = from_group(STEP_B, near)
     mine = keep + lax.ppermute(send, "tp", swap_core)
     came = [lax.ppermute(mine[k], "tp", turn_x[k]) for k in (1, 2, 3)]
     near = jnp.concatenate([near, far], 0)
@@ -267,7 +267,7 @@
     mine, near, far = tie((mine, near, far))
     near = jnp.concatenate([near, far], 0)
     own = [mine] + [lax.ppermute(mine, "tp", turn_x[k]) for k in (1, 2, 3)]
-    far = from_group(STEP_B, near)
+    far = from_group(STEP_A, near)
     own, near = tie((own, jnp.concatenate([near, far], 0)))
     far = from_group(STEP_Y, near)
     other = lax.ppermute(jnp.stack(own), "tp", swap_core)

time: 71 us -> 70.1 us (0.987)
  starting transfers between devices: 32.6 us -> 31.8 us
    ppermute x4, starting transfers between devices: 11.4 us -> 8 us  [from_group(): return lax.ppermute(rows, 'grp', flips(step))]
    ppermute x3, starting transfers between devices: 2.88 us -> 4.29 us  [on_device(): came = [lax.ppermute(mine[k], 'tp', turn_x[k]) for k in (1, 2, 3)]]
    ppermute x1, waiting for transfers between devices: 1.33 us -> 0.01 us  [on_device(): mine = keep + lax.ppermute(send, 'tp', swap_core)]
    ppermute x3, waiting for transfers between devices: 0.01 us -> 0.82 us  [on_device(): came = [lax.ppermute(mine[k], 'tp', turn_x[k]) for k in (1, 2, 3)]]
    ppermute x3, starting transfers between devices: 2.3 us -> 3.09 us  [on_device(): own = [mine] + [lax.ppermute(mine, 'tp', turn_x[k]) for k in (1, 2, 3)]]
where the time goes in v6:
time: 70.1 us; the launch traced here: 69.9 us
  starting transfers between devices  31.8 us (45%)
  waiting for transfers between devices  14.5 us (21%)
  blocking collectives  11.7 us (17%)
  Pallas kernels  10.1 us (14%)
  other arithmetic  1.54 us (2%)
    all_to_all x1, blocking collectives, on_device(): dots = lax.all_to_all(dots, 'tp', 0, 0, tiled=True)  11.7 us
    ppermute x4, starting transfers between devices, from_group(): return lax.ppermute(rows, 'grp', flips(step))  8 us
    pallas_call x1, Pallas kernels, rank_rows(): pl.pallas_call(rows_kernel, in_specs=[far] * 4, out_specs=[whole] * 4, ou...  6.1 us
    all_to_all x1, starting transfers between devices, on_device(): lax.all_to_all(keep + came, 'tp', 0, 0, axis_index_groups=same_core, tile...  4.97 us
    ppermute x4, waiting for transfers between devices, from_group(): return lax.ppermute(rows, 'grp', flips(step))  4.83 us
    ppermute x1, starting transfers between devices, on_device(): other = lax.ppermute(jnp.stack(own), 'tp', swap_core)  4.7 us
    ppermute x3, starting transfers between devices, on_device(): came = [lax.ppermute(mine[k], 'tp', turn_x[k]) for k in (1, 2, 3)]  4.29 us
    all_to_all x1, waiting for transfers between devices, on_device(): lax.all_to_all(keep + came, 'tp', 0, 0, axis_index_groups=same_core, tile...  3.61 us
  transfers between devices with their start and end apart: 15, of which 8 were waited for; matrix products, arithmetic and copies ran while one was open for 1% of the time, Pallas kernels for 5%

profile of v6, /device:TPU:1, one launch (start us, length us, event | category | flops | bytes accessed | tf_op | source)
XLA Modules:
  0.0 69.9 jit_solution(11534366120372579442)
XLA Ops:
  0.0 0.0 copy-start.1
  0.0 0.0 copy-start
  0.0 6.1 %rank_rows.1 = (f32[4,16,1536]{2,1,0:T(8,128)S(1)}, f32[4,16,1536]{2,1,0:T(8,128)S(1)}, bf16[6144,512]{1,0:T(8,128)(2,1)S(1)}, bf16[6144,512]{1,0:T(8,128)(2,1)S(1)}) custom-call(bf16[6144,512]{1,0:T(8,128)(2,1)} %x_ref.1, bf16[6144,512]{1,0:T(8,128)(2,1)} %g_ref.1, bf16[16,512]{1,0:T(8,128)(2,1)} %bitcast.25, bf16[16,512]{1,0:T(8,128)(2,1)} %b_ref.1), custom_call_target="tpu_custom_call" | custom-call | flops 201326592 | bytes 12582912 | tf_op jit(solution)/shard_map/rank_rows/pallas_call | solution.py:80
  6.1 3.3 %collective-permute-start = (f32[4,16,1536]{2,1,0:T(8,128)S(1)}, f32[4,16,1536]{2,1,0:T(8,128)S(1)}, u32[]{:S(2)}, u32[]{:S(2)}) collective-permute-start(f32[4,16,1536]{2,1,0:T(8,128)S(1)} %get-tuple-element.34), channel_id=1, source_target_pairs={{0,1},{1,0},{2,3},{3,2},{4,5},{5,4},{6,7},{7,6},{8,9},{9,8},{10,11... | collective-permute-start | bytes 1179656 | tf_op jit(solution)/shard_map/ppermute | solution.py:261
  9.4 0.0 copy-done.1
  9.4 3.9 %collective-permute-start.5 = (f32[32,512]{1,0:T(8,128)S(1)}, f32[32,512]{1,0:T(8,128)S(1)}, u32[]{:S(2)}, u32[]{:S(2)}) collective-permute-start(f32[32,512]{1,0:T(8,128)S(1)} %copy-done.1), channel_id=1, source_target_pairs={{0,224},{16,240},{32,64},{48,80},{64,32},{80,48},{96,128},{112,144... | collective-permute-start | bytes 196616 | tf_op jit(solution)/shard_map/ppermute | solution.py:256
  13.3 0.0 collective-permute-done
  13.4 1.3 %collective-permute-start.1 = (f32[16,1536]{1,0:T(8,128)S(1)}, f32[16,1536]{1,0:T(8,128)S(1)}, u32[]{:S(2)}, u32[]{:S(2)}) collective-permute-start(f32[16,1536]{1,0:T(8,128)S(1)} %get-tuple-element.55), channel_id=1, source_target_pairs={{0,2},{1,3},{2,4},{3,5},{4,6},{5,7},{6,0},{7,1},{8,10},{9,11},{10,... | collective-permute-start | bytes 294920 | tf_op jit(solution)/shard_map/ppermute | solution.py:262
  14.7 1.5 %collective-permute-start.3 = (f32[16,1536]{1,0:T(8,128)S(1)}, f32[16,1536]{1,0:T(8,128)S(1)}, u32[]{:S(2)}, u32[]{:S(2)}) collective-permute-start(f32[16,1536]{1,0:T(8,128)S(1)} %get-tuple-element.56), channel_id=1, source_target_pairs={{0,6},{1,7},{2,0},{3,1},{4,2},{5,3},{6,4},{7,5},{8,14},{9,15},{10,... | collective-permute-start | bytes 294920 | tf_op jit(solution)/shard_map/ppermute | solution.py:262
  16.2 1.5 %collective-permute-start.2 = (f32[16,1536]{1,0:T(8,128)S(1)}, f32[16,1536]{1,0:T(8,128)S(1)}, u32[]{:S(2)}, u32[]{:S(2)}) collective-permute-start(f32[16,1536]{1,0:T(8,128)S(1)} %get-tuple-element.57), channel_id=1, source_target_pairs={{0,4},{1,5},{2,6},{3,7},{4,0},{5,1},{6,2},{7,3},{8,12},{9,13},{10,... | collective-permute-start | bytes 294920 | tf_op jit(solution)/shard_map/ppermute | solution.py:262
  17.7 0.0 collective-permute-done.5
  17.7 2.7 %collective-permute-start.6 = (f32[64,512]{1,0:T(8,128)S(1)}, f32[64,512]{1,0:T(8,128)S(1)}, u32[]{:S(2)}, u32[]{:S(2)}) collective-permute-start(f32[64,512]{1,0:T(8,128)S(1)} %constant_dynamic-update-slice_fusion), channel_id=1, source_target_pairs={{0,128},{16,144},{32,160},{48,176},{64,192},{80,208},{96,224},{112... | collective-permute-start | bytes 393224 | tf_op jit(solution)/shard_map/ppermute | solution.py:256
  20.4 0.0 collective-permute-done.1
  20.4 0.0 collective-permute-done.3
  20.4 0.8 %collective-permute-done.2 = f32[16,1536]{1,0:T(8,128)S(1)} collective-permute-done((f32[16,1536]{1,0:T(8,128)S(1)}, f32[16,1536]{1,0:T(8,128)S(1)}, u32[]{:S(2)}, u32[]{:S(2)}) %collective-permute-start.2) | collective-permute-done | bytes 98336 | tf_op jit(solution)/shard_map/ppermute | solution.py:262
  21.3 3.0 %collective-permute-start.4 = (f32[16,1536]{1,0:T(8,128)S(1)}, f32[16,1536]{1,0:T(8,128)S(1)}, u32[]{:S(2)}, u32[]{:S(2)}) collective-permute-start(f32[16,1536]{1,0:T(8,128)S(1)} %fusion.2), channel_id=1, source_target_pairs={{0,8},{1,9},{2,10},{3,11},{4,12},{5,13},{6,14},{7,15},{8,0},{9,1},... | collective-permute-start | bytes 294920 | tf_op jit(solution)/shard_map/ppermute | solution.py:266
  24.3 2.4 %collective-permute-done.4 = f32[16,1536]{1,0:T(8,128)S(1)} collective-permute-done((f32[16,1536]{1,0:T(8,128)S(1)}, f32[16,1536]{1,0:T(8,128)S(1)}, u32[]{:S(2)}, u32[]{:S(2)}) %collective-permute-start.4) | collective-permute-done | bytes 98336 | tf_op jit(solution)/shard_map/ppermute | solution.py:266
  26.6 0.0 collective-permute-done.6
  26.7 0.1 collective-permute-start.10
  26.8 1.6 %collective-permute-start.9 = (f32[16,1536]{1,0:T(8,128)S(1)}, f32[16,1536]{1,0:T(8,128)S(1)}, u32[]{:S(2)}, u32[]{:S(2)}) collective-permute-start(f32[16,1536]{1,0:T(8,128)S(1)} %add.34.refs_0_), channel_id=1, source_target_pairs={{0,6},{1,7},{2,0},{3,1},{4,2},{5,3},{6,4},{7,5},{8,14},{9,15},{10,... | collective-permute-start | bytes 294920 | tf_op jit(solution)/shard_map/ppermute | solution.py:269
  28.4 1.5 %collective-permute-start.8 = (f32[16,1536]{1,0:T(8,128)S(1)}, f32[16,1536]{1,0:T(8,128)S(1)}, u32[]{:S(2)}, u32[]{:S(2)}) collective-permute-start(f32[16,1536]{1,0:T(8,128)S(1)} %add.34.refs_0_), channel_id=1, source_target_pairs={{0,4},{1,5},{2,6},{3,7},{4,0},{5,1},{6,2},{7,3},{8,12},{9,13},{10,... | collective-permute-start | bytes 294920 | tf_op jit(solution)/shard_map/ppermute | solution.py:269
  29.9 0.0 collective-permute-start.7
  29.9 2.1 %collective-permute-done.10 = f32[128,512]{1,0:T(8,128)S(1)} collective-permute-done((f32[128,512]{1,0:T(8,128)S(1)}, f32[128,512]{1,0:T(8,128)S(1)}, u32[]{:S(2)}, u32[]{:S(2)}) %collective-permute-start.10) | collective-permute-done | bytes 262176 | tf_op jit(solution)/shard_map/ppermute | solution.py:256
  32.0 0.0 collective-permute-done.9.refs_3_
  32.0 1.3 %collective-permute-done.8.refs_2_ = f32[16,1536]{1,0:T(8,128)S(1)} collective-permute-done((f32[16,1536]{1,0:T(8,128)S(1)}, f32[16,1536]{1,0:T(8,128)S(1)}, u32[]{:S(2)}, u32[]{:S(2)}) %collective-permute-start.8) | collective-permute-done | bytes 98336 | tf_op jit(solution)/shard_map/ppermute | solution.py:269
  33.4 1.2 %collective-permute-done.7.refs_1_ = f32[16,1536]{1,0:T(8,128)S(1)} collective-permute-done((f32[16,1536]{1,0:T(8,128)S(1)}, f32[16,1536]{1,0:T(8,128)S(1)}, u32[]{:S(2)}, u32[]{:S(2)}) %collective-permute-start.7) | collective-permute-done | bytes 98336 | tf_op jit(solution)/shard_map/ppermute | solution.py:269
  34.6 4.7 %collective-permute-start.11 = (f32[4,16,1536]{2,1,0:T(8,128)S(1)}, f32[4,16,1536]{2,1,0:T(8,128)S(1)}, u32[]{:S(2)}, u32[]{:S(2)}) collective-permute-start(f32[4,16,1536]{2,1,0:T(8,128)S(1)} %pad_maximum_fusion.1), channel_id=1, source_target_pairs={{0,1},{1,0},{2,3},{3,2},{4,5},{5,4},{6,7},{7,6},{8,9},{9,8},{10,11... | collective-permute-start | bytes 1179656 | tf_op jit(solution)/shard_map/ppermute | solution.py:273
  39.3 1.3 %collective-permute-start.13 = (f32[256,512]{1,0:T(8,128)S(1)}, f32[256,512]{1,0:T(8,128)S(1)}, u32[]{:S(2)}, u32[]{:S(2)}) collective-permute-start(f32[256,512]{1,0:T(8,128)S(1)} %pad_maximum_fusion.v_ref), channel_id=1, source_target_pairs={{0,16},{16,0},{32,48},{48,32},{64,80},{80,64},{96,112},{112,96},{1... | collective-permute-start | bytes 1572872 | tf_op jit(solution)/shard_map/ppermute | solution.py:256
  40.6 0.0 collective-permute-done.11.refs_4_
  40.6 0.0 copy-done
  40.6 2.3 %feature_shares.1 = (f32[8,32,128]{2,1,0:T(8,128)S(1)}, f32[8,32,128]{2,1,0:T(8,128)S(1)}) custom-call(bf16[6144,512]{1,0:T(8,128)(2,1)S(1)} %get-tuple-element.30.x_ref, bf16[6144,512]{1,0:T(8,128)(2,1)S(1)} %get-tuple-element.31.g_ref, f32[16,1536]{1,0:T(8,128)S(1)} %add.34.refs_0_, f32[16,1536]{1,0:T(8,128)S(1)} %collective-permute-done.7.refs_1_, ...), custom_call_target="tpu_custom_call" | custom-call | flops 402653184 | bytes 12582912 | tf_op jit(solution)/shard_map/feature_shares/pallas_call | solution.py:133
  43.0 0.5 collective-permute-start.12
  43.4 0.6 valid_terms.2
  44.1 0.4 collective-permute-done.12
  44.4 0.7 add.35
  45.1 5.0 %all-to-all-start = ((f32[8,32,128]{2,1,0:T(8,128)}), f32[8,32,128]{2,1,0:T(8,128)S(1)}, u32[]{:S(2)}, u32[]{:S(2)}) async-start(f32[8,32,128]{2,1,0:T(8,128)} %add.35), calls=%async_computation | async-start | bytes 262144 | tf_op jit(solution)/shard_map/all_to_all | solution.py:279
  50.1 2.7 %collective-permute-done.13.v_ref = f32[256,512]{1,0:T(8,128)S(1)} collective-permute-done((f32[256,512]{1,0:T(8,128)S(1)}, f32[256,512]{1,0:T(8,128)S(1)}, u32[]{:S(2)}, u32[]{:S(2)}) %collective-permute-start.13) | collective-permute-done | bytes 524320 | tf_op jit(solution)/shard_map/ppermute | solution.py:256
  52.8 0.6 valid_terms.3
  53.4 3.6 %all-to-all-done.f_ref = f32[8,32,128]{2,1,0:T(8,128)S(1)} async-done(((f32[8,32,128]{2,1,0:T(8,128)}), f32[8,32,128]{2,1,0:T(8,128)S(1)}, u32[]{:S(2)}, u32[]{:S(2)}) %all-to-all-start) | async-done | bytes 131104 | tf_op jit(solution)/shard_map/all_to_all | solution.py:279
  57.0 0.5 partial_dots.1
  57.5 11.7 %all_to_all.10 = f32[16,8,128]{2,1,0:T(8,128)S(1)} all-to-all(f32[16,8,128]{2,1,0:T(8,128)S(1)} %partial_dots.1), channel_id=1, replica_groups=mesh['grp'=16,'tp'=16] {'tp'}, dimensions={0} | all-to-all | bytes 131072 | tf_op jit(solution)/shard_map/all_to_all | solution.py:282
  69.2 0.7 multiply_divide_fusion
  (11 shorter events, 0.2 us)
Async XLA Ops:
  0.0 9.4 %copy-start.1 = (f32[32,512]{1,0:T(8,128)S(1)}, f32[32,512]{1,0:T(8,128)}, u32[]{:S(2)}) copy-start(f32[32,512]{1,0:T(8,128)} %param.11) | copy-start | bytes 196612
  0.0 40.6 %copy-start = (s32[512,256]{1,0:T(8,128)S(1)}, s32[512,256]{1,0:T(8,128)}, u32[]{:S(2)}) copy-start(s32[512,256]{1,0:T(8,128)} %refs_5_.1) | copy-start | bytes 1572868
  6.1 7.2 %collective-permute-start = (f32[4,16,1536]{2,1,0:T(8,128)S(1)}, f32[4,16,1536]{2,1,0:T(8,128)S(1)}, u32[]{:S(2)}, u32[]{:S(2)}) collective-permute-start(f32[4,16,1536]{2,1,0:T(8,128)S(1)} %get-tuple-element.34), channel_id=1, source_target_pairs={{0,1},{1,0},{2,3},{3,2},{4,5},{5,4},{6,7},{7,6},{8,9},{9,8},{10,11... | collective-permute-start | bytes 1179656 | tf_op jit(solution)/shard_map/ppermute | solution.py:261
  9.4 8.3 %collective-permute-start.5 = (f32[32,512]{1,0:T(8,128)S(1)}, f32[32,512]{1,0:T(8,128)S(1)}, u32[]{:S(2)}, u32[]{:S(2)}) collective-permute-start(f32[32,512]{1,0:T(8,128)S(1)} %copy-done.1), channel_id=1, source_target_pairs={{0,224},{16,240},{32,64},{48,80},{64,32},{80,48},{96,128},{112,144... | collective-permute-start | bytes 196616 | tf_op jit(solution)/shard_map/ppermute | solution.py:256
  13.4 7.0 %collective-permute-start.1 = (f32[16,1536]{1,0:T(8,128)S(1)}, f32[16,1536]{1,0:T(8,128)S(1)}, u32[]{:S(2)}, u32[]{:S(2)}) collective-permute-start(f32[16,1536]{1,0:T(8,128)S(1)} %get-tuple-element.55), channel_id=1, source_target_pairs={{0,2},{1,3},{2,4},{3,5},{4,6},{5,7},{6,0},{7,1},{8,10},{9,11},{10,... | collective-permute-start | bytes 294920 | tf_op jit(solution)/shard_map/ppermute | solution.py:262
  14.7 5.7 %collective-permute-start.3 = (f32[16,1536]{1,0:T(8,128)S(1)}, f32[16,1536]{1,0:T(8,128)S(1)}, u32[]{:S(2)}, u32[]{:S(2)}) collective-permute-start(f32[16,1536]{1,0:T(8,128)S(1)} %get-tuple-element.56), channel_id=1, source_target_pairs={{0,6},{1,7},{2,0},{3,1},{4,2},{5,3},{6,4},{7,5},{8,14},{9,15},{10,... | collective-permute-start | bytes 294920 | tf_op jit(solution)/shard_map/ppermute | solution.py:262
  16.2 5.1 %collective-permute-start.2 = (f32[16,1536]{1,0:T(8,128)S(1)}, f32[16,1536]{1,0:T(8,128)S(1)}, u32[]{:S(2)}, u32[]{:S(2)}) collective-permute-start(f32[16,1536]{1,0:T(8,128)S(1)} %get-tuple-element.57), channel_id=1, source_target_pairs={{0,4},{1,5},{2,6},{3,7},{4,0},{5,1},{6,2},{7,3},{8,12},{9,13},{10,... | collective-permute-start | bytes 294920 | tf_op jit(solution)/shard_map/ppermute | solution.py:262
  17.7 8.9 %collective-permute-start.6 = (f32[64,512]{1,0:T(8,128)S(1)}, f32[64,512]{1,0:T(8,128)S(1)}, u32[]{:S(2)}, u32[]{:S(2)}) collective-permute-start(f32[64,512]{1,0:T(8,128)S(1)} %constant_dynamic-update-slice_fusion), channel_id=1, source_target_pairs={{0,128},{16,144},{32,160},{48,176},{64,192},{80,208},{96,224},{112... | collective-permute-start | bytes 393224 | tf_op jit(solution)/shard_map/ppermute | solution.py:256
  21.3 5.4 %collective-permute-start.4 = (f32[16,1536]{1,0:T(8,128)S(1)}, f32[16,1536]{1,0:T(8,128)S(1)}, u32[]{:S(2)}, u32[]{:S(2)}) collective-permute-start(f32[16,1536]{1,0:T(8,128)S(1)} %fusion.2), channel_id=1, source_target_pairs={{0,8},{1,9},{2,10},{3,11},{4,12},{5,13},{6,14},{7,15},{8,0},{9,1},... | collective-permute-start | bytes 294920 | tf_op jit(solution)/shard_map/ppermute | solution.py:266
  26.7 5.3 %collective-permute-start.10 = (f32[128,512]{1,0:T(8,128)S(1)}, f32[128,512]{1,0:T(8,128)S(1)}, u32[]{:S(2)}, u32[]{:S(2)}) collective-permute-start(f32[128,512]{1,0:T(8,128)S(1)} %pad_maximum_fusion.2), channel_id=1, source_target_pairs={{0,32},{16,48},{32,0},{48,16},{64,96},{80,112},{96,64},{112,80},{1... | collective-permute-start | bytes 786440 | tf_op jit(solution)/shard_map/ppermute | solution.py:256
  26.8 5.3 %collective-permute-start.9 = (f32[16,1536]{1,0:T(8,128)S(1)}, f32[16,1536]{1,0:T(8,128)S(1)}, u32[]{:S(2)}, u32[]{:S(2)}) collective-permute-start(f32[16,1536]{1,0:T(8,128)S(1)} %add.34.refs_0_), channel_id=1, source_target_pairs={{0,6},{1,7},{2,0},{3,1},{4,2},{5,3},{6,4},{7,5},{8,14},{9,15},{10,... | collective-permute-start | bytes 294920 | tf_op jit(solution)/shard_map/ppermute | solution.py:269
  28.4 5.0 %collective-permute-start.8 = (f32[16,1536]{1,0:T(8,128)S(1)}, f32[16,1536]{1,0:T(8,128)S(1)}, u32[]{:S(2)}, u32[]{:S(2)}) collective-permute-start(f32[16,1536]{1,0:T(8,128)S(1)} %add.34.refs_0_), channel_id=1, source_target_pairs={{0,4},{1,5},{2,6},{3,7},{4,0},{5,1},{6,2},{7,3},{8,12},{9,13},{10,... | collective-permute-start | bytes 294920 | tf_op jit(solution)/shard_map/ppermute | solution.py:269
  29.9 4.7 %collective-permute-start.7 = (f32[16,1536]{1,0:T(8,128)S(1)}, f32[16,1536]{1,0:T(8,128)S(1)}, u32[]{:S(2)}, u32[]{:S(2)}) collective-permute-start(f32[16,1536]{1,0:T(8,128)S(1)} %add.34.refs_0_), channel_id=1, source_target_pairs={{0,2},{1,3},{2,4},{3,5},{4,6},{5,7},{6,0},{7,1},{8,10},{9,11},{10,... | collective-permute-start | bytes 294920 | tf_op jit(solution)/shard_map/ppermute | solution.py:269
  34.6 6.1 %collective-permute-start.11 = (f32[4,16,1536]{2,1,0:T(8,128)S(1)}, f32[4,16,1536]{2,1,0:T(8,128)S(1)}, u32[]{:S(2)}, u32[]{:S(2)}) collective-permute-start(f32[4,16,1536]{2,1,0:T(8,128)S(1)} %pad_maximum_fusion.1), channel_id=1, source_target_pairs={{0,1},{1,0},{2,3},{3,2},{4,5},{5,4},{6,7},{7,6},{8,9},{9,8},{10,11... | collective-permute-start | bytes 1179656 | tf_op jit(solution)/shard_map/ppermute | solution.py:273
  39.3 13.5 %collective-permute-start.13 = (f32[256,512]{1,0:T(8,128)S(1)}, f32[256,512]{1,0:T(8,128)S(1)}, u32[]{:S(2)}, u32[]{:S(2)}) collective-permute-start(f32[256,512]{1,0:T(8,128)S(1)} %pad_maximum_fusion.v_ref), channel_id=1, source_target_pairs={{0,16},{16,0},{32,48},{48,32},{64,80},{80,64},{96,112},{112,96},{1... | collective-permute-start | bytes 1572872 | tf_op jit(solution)/shard_map/ppermute | solution.py:256
  43.0 1.4 %collective-permute-start.12 = (f32[8,32,128]{2,1,0:T(8,128)S(1)}, f32[8,32,128]{2,1,0:T(8,128)S(1)}, u32[]{:S(2)}, u32[]{:S(2)}) collective-permute-start(f32[8,32,128]{2,1,0:T(8,128)S(1)} %get-tuple-element.46), channel_id=1, source_target_pairs={{0,1},{1,0},{2,3},{3,2},{4,5},{5,4},{6,7},{7,6},{8,9},{9,8},{10,11... | collective-permute-start | bytes 393224 | tf_op jit(solution)/shard_map/ppermute | solution.py:277
  45.1 11.9 %all-to-all-start = ((f32[8,32,128]{2,1,0:T(8,128)}), f32[8,32,128]{2,1,0:T(8,128)S(1)}, u32[]{:S(2)}, u32[]{:S(2)}) async-start(f32[8,32,128]{2,1,0:T(8,128)} %add.35), calls=%async_computation | async-start | bytes 262144 | tf_op jit(solution)/shard_map/all_to_all | solution.py:279

commit v7 on v6

--- a/solution.py
+++ b/solution.py
@@ -111,7 +111,7 @@
             b = mm(halves(jnp.where(first, own, other)), g_ref[rows], NN)
             v_ref[0, begin + c] = a[:rank] + a[rank:]
             v_ref[1, begin + c] = b[:rank] + b[rank:]
-    sign = (2 * s_ref[...] - 1).astype(jnp.float32).astype(jnp.bfloat16)
+    sign = s_ref[...]
     each = keep_ref.shape[0] // 2
     blocks, step = v_ref.shape[1], LEN // TB
     pad = jnp.zeros((128 - blocks // step * rank, x_ref.shape[1]), jnp.float32)
@@ -271,7 +271,7 @@
     own, near = tie((own, jnp.concatenate([near, far], 0)))
     far = from_group(STEP_Y, near)
     other = lax.ppermute(jnp.stack(own), "tp", swap_core)
-    keep, send = feature_shares(x, g, own, other, bits, tp)
+    keep, send = feature_shares(x, g, own, other, (2 * bits - 1).astype(jnp.bfloat16), tp)
     send, near = tie((send, near))
     near = valid_terms(near, rank)
     came = lax.ppermute(send, "tp", swap_core)

time: 70.1 us -> 71.2 us (1.016)
  starting transfers between devices: 31.8 us -> 35.2 us
  waiting for transfers between devices: 14.5 us -> 12.2 us
    ppermute x4, waiting for transfers between devices: 4.83 us -> 2.75 us  [from_group(): return lax.ppermute(rows, 'grp', flips(step))]
    ppermute x3, waiting for transfers between devices: 2.51 us -> 1.13 us  [on_device(): own = [mine] + [lax.ppermute(mine, 'tp', turn_x[k]) for k in (1, 2, 3)]]
    all_to_all x1, waiting for transfers between devices: 3.61 us -> 4.82 us  [on_device(): lax.all_to_all(keep + came, 'tp', 0, 0, axis_index_groups=same_core, tile...]
    all_to_all x1, starting transfers between devices: 4.97 us -> 6.14 us  [on_device(): lax.all_to_all(keep + came, 'tp', 0, 0, axis_index_groups=same_core, tile...]
    ppermute x3, starting transfers between devices: 3.09 us -> 3.96 us  [on_device(): own = [mine] + [lax.ppermute(mine, 'tp', turn_x[k]) for k in (1, 2, 3)]]
    ppermute x1, starting transfers between devices: 4.7 us -> 5.43 us  [on_device(): other = lax.ppermute(jnp.stack(own), 'tp', swap_core)]
where the time goes in v7:
time: 71.2 us; the launch traced here: 71 us
  starting transfers between devices  35.2 us (49%)
  waiting for transfers between devices  12.2 us (17%)
  blocking collectives  11.7 us (16%)
  Pallas kernels  10.2 us (14%)
  other arithmetic  1.6 us (2%)
    all_to_all x1, blocking collectives, on_device(): dots = lax.all_to_all(dots, 'tp', 0, 0, tiled=True)  11.7 us
    ppermute x4, starting transfers between devices, from_group(): return lax.ppermute(rows, 'grp', flips(step))  8 us
    all_to_all x1, starting transfers between devices, on_device(): lax.all_to_all(keep + came, 'tp', 0, 0, axis_index_groups=same_core, tile...  6.14 us
    pallas_call x1, Pallas kernels, rank_rows(): pl.pallas_call(rows_kernel, in_specs=[far] * 4, out_specs=[whole] * 4, ou...  6.1 us
    ppermute x1, starting transfers between devices, on_device(): other = lax.ppermute(jnp.stack(own), 'tp', swap_core)  5.43 us
    ppermute x3, starting transfers between devices, on_device(): came = [lax.ppermute(mine[k], 'tp', turn_x[k]) for k in (1, 2, 3)]  4.89 us
    all_to_all x1, waiting for transfers between devices, on_device(): lax.all_to_all(keep + came, 'tp', 0, 0, axis_index_groups=same_core, tile...  4.82 us
    ppermute x3, starting transfers between devices, on_device(): own = [mine] + [lax.ppermute(mine, 'tp', turn_x[k]) for k in (1, 2, 3)]  3.96 us
  transfers between devices with their start and end apart: 15, of which 8 were waited for; matrix products, arithmetic and copies ran while one was open for 1% of the time, Pallas kernels for 5%

profile of v7, /device:TPU:1, one launch (start us, length us, event | category | flops | bytes accessed | tf_op | source)
XLA Modules:
  0.0 71.0 jit_solution(13965461624839490329)
XLA Ops:
  0.0 0.0 copy-start.1
  0.0 0.0 copy-start
  0.0 6.1 %rank_rows.1 = (f32[4,16,1536]{2,1,0:T(8,128)S(1)}, f32[4,16,1536]{2,1,0:T(8,128)S(1)}, bf16[6144,512]{1,0:T(8,128)(2,1)S(1)}, bf16[6144,512]{1,0:T(8,128)(2,1)S(1)}) custom-call(bf16[6144,512]{1,0:T(8,128)(2,1)} %x_ref.1, bf16[6144,512]{1,0:T(8,128)(2,1)} %g_ref.1, bf16[16,512]{1,0:T(8,128)(2,1)} %bitcast.25, bf16[16,512]{1,0:T(8,128)(2,1)} %b_ref.1), custom_call_target="tpu_custom_call" | custom-call | flops 201326592 | bytes 12582912 | tf_op jit(solution)/shard_map/rank_rows/pallas_call | solution.py:80
  6.1 3.3 %collective-permute-start = (f32[4,16,1536]{2,1,0:T(8,128)S(1)}, f32[4,16,1536]{2,1,0:T(8,128)S(1)}, u32[]{:S(2)}, u32[]{:S(2)}) collective-permute-start(f32[4,16,1536]{2,1,0:T(8,128)S(1)} %get-tuple-element.34), channel_id=1, source_target_pairs={{0,1},{1,0},{2,3},{3,2},{4,5},{5,4},{6,7},{7,6},{8,9},{9,8},{10,11... | collective-permute-start | bytes 1179656 | tf_op jit(solution)/shard_map/ppermute | solution.py:261
  9.4 0.0 copy-done.1
  9.4 3.9 %collective-permute-start.5 = (f32[32,512]{1,0:T(8,128)S(1)}, f32[32,512]{1,0:T(8,128)S(1)}, u32[]{:S(2)}, u32[]{:S(2)}) collective-permute-start(f32[32,512]{1,0:T(8,128)S(1)} %copy-done.1), channel_id=1, source_target_pairs={{0,224},{16,240},{32,64},{48,80},{64,32},{80,48},{96,128},{112,144... | collective-permute-start | bytes 196616 | tf_op jit(solution)/shard_map/ppermute | solution.py:256
  13.3 0.0 collective-permute-done
  13.4 1.3 %collective-permute-start.1 = (f32[16,1536]{1,0:T(8,128)S(1)}, f32[16,1536]{1,0:T(8,128)S(1)}, u32[]{:S(2)}, u32[]{:S(2)}) collective-permute-start(f32[16,1536]{1,0:T(8,128)S(1)} %get-tuple-element.55), channel_id=1, source_target_pairs={{0,2},{1,3},{2,4},{3,5},{4,6},{5,7},{6,0},{7,1},{8,10},{9,11},{10,... | collective-permute-start | bytes 294920 | tf_op jit(solution)/shard_map/ppermute | solution.py:262
  14.7 2.5 %collective-permute-start.2 = (f32[16,1536]{1,0:T(8,128)S(1)}, f32[16,1536]{1,0:T(8,128)S(1)}, u32[]{:S(2)}, u32[]{:S(2)}) collective-permute-start(f32[16,1536]{1,0:T(8,128)S(1)} %get-tuple-element.57), channel_id=1, source_target_pairs={{0,4},{1,5},{2,6},{3,7},{4,0},{5,1},{6,2},{7,3},{8,12},{9,13},{10,... | collective-permute-start | bytes 294920 | tf_op jit(solution)/shard_map/ppermute | solution.py:262
  17.1 1.2 %collective-permute-start.3 = (f32[16,1536]{1,0:T(8,128)S(1)}, f32[16,1536]{1,0:T(8,128)S(1)}, u32[]{:S(2)}, u32[]{:S(2)}) collective-permute-start(f32[16,1536]{1,0:T(8,128)S(1)} %get-tuple-element.56), channel_id=1, source_target_pairs={{0,6},{1,7},{2,0},{3,1},{4,2},{5,3},{6,4},{7,5},{8,14},{9,15},{10,... | collective-permute-start | bytes 294920 | tf_op jit(solution)/shard_map/ppermute | solution.py:262
  18.3 0.0 collective-permute-done.5
  18.3 2.7 %collective-permute-start.6 = (f32[64,512]{1,0:T(8,128)S(1)}, f32[64,512]{1,0:T(8,128)S(1)}, u32[]{:S(2)}, u32[]{:S(2)}) collective-permute-start(f32[64,512]{1,0:T(8,128)S(1)} %constant_dynamic-update-slice_fusion), channel_id=1, source_target_pairs={{0,128},{16,144},{32,160},{48,176},{64,192},{80,208},{96,224},{112... | collective-permute-start | bytes 393224 | tf_op jit(solution)/shard_map/ppermute | solution.py:256
  21.0 0.0 collective-permute-done.1
  21.0 0.8 %collective-permute-done.2 = f32[16,1536]{1,0:T(8,128)S(1)} collective-permute-done((f32[16,1536]{1,0:T(8,128)S(1)}, f32[16,1536]{1,0:T(8,128)S(1)}, u32[]{:S(2)}, u32[]{:S(2)}) %collective-permute-start.2) | collective-permute-done | bytes 98336 | tf_op jit(solution)/shard_map/ppermute | solution.py:262
  21.8 0.0 collective-permute-done.3
  21.8 3.0 %collective-permute-start.4 = (f32[16,1536]{1,0:T(8,128)S(1)}, f32[16,1536]{1,0:T(8,128)S(1)}, u32[]{:S(2)}, u32[]{:S(2)}) collective-permute-start(f32[16,1536]{1,0:T(8,128)S(1)} %fusion.2), channel_id=1, source_target_pairs={{0,8},{1,9},{2,10},{3,11},{4,12},{5,13},{6,14},{7,15},{8,0},{9,1},... | collective-permute-start | bytes 294920 | tf_op jit(solution)/shard_map/ppermute | solution.py:266
  24.8 2.4 %collective-permute-done.4 = f32[16,1536]{1,0:T(8,128)S(1)} collective-permute-done((f32[16,1536]{1,0:T(8,128)S(1)}, f32[16,1536]{1,0:T(8,128)S(1)}, u32[]{:S(2)}, u32[]{:S(2)}) %collective-permute-start.4) | collective-permute-done | bytes 98336 | tf_op jit(solution)/shard_map/ppermute | solution.py:266
  27.2 0.0 collective-permute-done.6
  27.2 0.1 collective-permute-start.10
  27.3 0.6 collective-permute-start.7
  27.9 2.1 %collective-permute-start.8 = (f32[16,1536]{1,0:T(8,128)S(1)}, f32[16,1536]{1,0:T(8,128)S(1)}, u32[]{:S(2)}, u32[]{:S(2)}) collective-permute-start(f32[16,1536]{1,0:T(8,128)S(1)} %add.35.refs_0_), channel_id=1, source_target_pairs={{0,4},{1,5},{2,6},{3,7},{4,0},{5,1},{6,2},{7,3},{8,12},{9,13},{10,... | collective-permute-start | bytes 294920 | tf_op jit(solution)/shard_map/ppermute | solution.py:269
  30.1 1.2 %collective-permute-start.9 = (f32[16,1536]{1,0:T(8,128)S(1)}, f32[16,1536]{1,0:T(8,128)S(1)}, u32[]{:S(2)}, u32[]{:S(2)}) collective-permute-start(f32[16,1536]{1,0:T(8,128)S(1)} %add.35.refs_0_), channel_id=1, source_target_pairs={{0,6},{1,7},{2,0},{3,1},{4,2},{5,3},{6,4},{7,5},{8,14},{9,15},{10,... | collective-permute-start | bytes 294920 | tf_op jit(solution)/shard_map/ppermute | solution.py:269
  31.3 1.2 %collective-permute-done.10 = f32[128,512]{1,0:T(8,128)S(1)} collective-permute-done((f32[128,512]{1,0:T(8,128)S(1)}, f32[128,512]{1,0:T(8,128)S(1)}, u32[]{:S(2)}, u32[]{:S(2)}) %collective-permute-start.10) | collective-permute-done | bytes 262176 | tf_op jit(solution)/shard_map/ppermute | solution.py:256
  32.6 0.0 collective-permute-done.7.refs_1_
  32.6 0.6 collective-permute-done.8.refs_2_
  33.2 0.6 collective-permute-done.9.refs_3_
  33.8 5.4 %collective-permute-start.11 = (f32[4,16,1536]{2,1,0:T(8,128)S(1)}, f32[4,16,1536]{2,1,0:T(8,128)S(1)}, u32[]{:S(2)}, u32[]{:S(2)}) collective-permute-start(f32[4,16,1536]{2,1,0:T(8,128)S(1)} %pad_maximum_fusion.1), channel_id=1, source_target_pairs={{0,1},{1,0},{2,3},{3,2},{4,5},{5,4},{6,7},{7,6},{8,9},{9,8},{10,11... | collective-permute-start | bytes 1179656 | tf_op jit(solution)/shard_map/ppermute | solution.py:273
  39.2 1.3 %collective-permute-start.13 = (f32[256,512]{1,0:T(8,128)S(1)}, f32[256,512]{1,0:T(8,128)S(1)}, u32[]{:S(2)}, u32[]{:S(2)}) collective-permute-start(f32[256,512]{1,0:T(8,128)S(1)} %pad_maximum_fusion.v_ref), channel_id=1, source_target_pairs={{0,16},{16,0},{32,48},{48,32},{64,80},{80,64},{96,112},{112,96},{1... | collective-permute-start | bytes 1572872 | tf_op jit(solution)/shard_map/ppermute | solution.py:256
  40.5 0.0 copy-done
  40.5 0.1 add_convert_fusion.refs_5_
  40.6 0.0 collective-permute-done.11.refs_4_
  40.6 2.3 %feature_shares.1 = (f32[8,32,128]{2,1,0:T(8,128)S(1)}, f32[8,32,128]{2,1,0:T(8,128)S(1)}) custom-call(bf16[6144,512]{1,0:T(8,128)(2,1)S(1)} %get-tuple-element.30.x_ref, bf16[6144,512]{1,0:T(8,128)(2,1)S(1)} %get-tuple-element.31.g_ref, f32[16,1536]{1,0:T(8,128)S(1)} %add.35.refs_0_, f32[16,1536]{1,0:T(8,128)S(1)} %collective-permute-done.7.refs_1_, ...), custom_call_target="tpu_custom_call" | custom-call | flops 402653184 | bytes 12582912 | tf_op jit(solution)/shard_map/feature_shares/pallas_call | solution.py:133
  42.9 0.4 collective-permute-start.12
  43.4 0.6 valid_terms.2
  44.0 0.4 collective-permute-done.12
  44.4 0.7 add.36
  45.0 6.1 %all-to-all-start = ((f32[8,32,128]{2,1,0:T(8,128)}), f32[8,32,128]{2,1,0:T(8,128)S(1)}, u32[]{:S(2)}, u32[]{:S(2)}) async-start(f32[8,32,128]{2,1,0:T(8,128)} %add.36), calls=%async_computation | async-start | bytes 262144 | tf_op jit(solution)/shard_map/all_to_all | solution.py:279
  51.2 1.5 %collective-permute-done.13.v_ref = f32[256,512]{1,0:T(8,128)S(1)} collective-permute-done((f32[256,512]{1,0:T(8,128)S(1)}, f32[256,512]{1,0:T(8,128)S(1)}, u32[]{:S(2)}, u32[]{:S(2)}) %collective-permute-start.13) | collective-permute-done | bytes 524320 | tf_op jit(solution)/shard_map/ppermute | solution.py:256
  52.7 0.6 valid_terms.3
  53.3 4.8 %all-to-all-done.f_ref = f32[8,32,128]{2,1,0:T(8,128)S(1)} async-done(((f32[8,32,128]{2,1,0:T(8,128)}), f32[8,32,128]{2,1,0:T(8,128)S(1)}, u32[]{:S(2)}, u32[]{:S(2)}) %all-to-all-start) | async-done | bytes 131104 | tf_op jit(solution)/shard_map/all_to_all | solution.py:279
  58.1 0.5 partial_dots.1
  58.6 11.7 %all_to_all.10 = f32[16,8,128]{2,1,0:T(8,128)S(1)} all-to-all(f32[16,8,128]{2,1,0:T(8,128)S(1)} %partial_dots.1), channel_id=1, replica_groups=mesh['grp'=16,'tp'=16] {'tp'}, dimensions={0} | all-to-all | bytes 131072 | tf_op jit(solution)/shard_map/all_to_all | solution.py:282
  70.3 0.7 multiply_divide_fusion
  (11 shorter events, 0.2 us)
Async XLA Ops:
  0.0 9.4 %copy-start.1 = (f32[32,512]{1,0:T(8,128)S(1)}, f32[32,512]{1,0:T(8,128)}, u32[]{:S(2)}) copy-start(f32[32,512]{1,0:T(8,128)} %param.11) | copy-start | bytes 196612
  0.0 40.5 %copy-start = (s32[512,256]{1,0:T(8,128)S(1)}, s32[512,256]{1,0:T(8,128)}, u32[]{:S(2)}) copy-start(s32[512,256]{1,0:T(8,128)} %param.10) | copy-start | bytes 1572868
  6.1 7.2 %collective-permute-start = (f32[4,16,1536]{2,1,0:T(8,128)S(1)}, f32[4,16,1536]{2,1,0:T(8,128)S(1)}, u32[]{:S(2)}, u32[]{:S(2)}) collective-permute-start(f32[4,16,1536]{2,1,0:T(8,128)S(1)} %get-tuple-element.34), channel_id=1, source_target_pairs={{0,1},{1,0},{2,3},{3,2},{4,5},{5,4},{6,7},{7,6},{8,9},{9,8},{10,11... | collective-permute-start | bytes 1179656 | tf_op jit(solution)/shard_map/ppermute | solution.py:261
  9.4 8.9 %collective-permute-start.5 = (f32[32,512]{1,0:T(8,128)S(1)}, f32[32,512]{1,0:T(8,128)S(1)}, u32[]{:S(2)}, u32[]{:S(2)}) collective-permute-start(f32[32,512]{1,0:T(8,128)S(1)} %copy-done.1), channel_id=1, source_target_pairs={{0,224},{16,240},{32,64},{48,80},{64,32},{80,48},{96,128},{112,144... | collective-permute-start | bytes 196616 | tf_op jit(solution)/shard_map/ppermute | solution.py:256
  13.4 7.6 %collective-permute-start.1 = (f32[16,1536]{1,0:T(8,128)S(1)}, f32[16,1536]{1,0:T(8,128)S(1)}, u32[]{:S(2)}, u32[]{:S(2)}) collective-permute-start(f32[16,1536]{1,0:T(8,128)S(1)} %get-tuple-element.55), channel_id=1, source_target_pairs={{0,2},{1,3},{2,4},{3,5},{4,6},{5,7},{6,0},{7,1},{8,10},{9,11},{10,... | collective-permute-start | bytes 294920 | tf_op jit(solution)/shard_map/ppermute | solution.py:262
  14.7 7.1 %collective-permute-start.2 = (f32[16,1536]{1,0:T(8,128)S(1)}, f32[16,1536]{1,0:T(8,128)S(1)}, u32[]{:S(2)}, u32[]{:S(2)}) collective-permute-start(f32[16,1536]{1,0:T(8,128)S(1)} %get-tuple-element.57), channel_id=1, source_target_pairs={{0,4},{1,5},{2,6},{3,7},{4,0},{5,1},{6,2},{7,3},{8,12},{9,13},{10,... | collective-permute-start | bytes 294920 | tf_op jit(solution)/shard_map/ppermute | solution.py:262
  17.1 4.7 %collective-permute-start.3 = (f32[16,1536]{1,0:T(8,128)S(1)}, f32[16,1536]{1,0:T(8,128)S(1)}, u32[]{:S(2)}, u32[]{:S(2)}) collective-permute-start(f32[16,1536]{1,0:T(8,128)S(1)} %get-tuple-element.56), channel_id=1, source_target_pairs={{0,6},{1,7},{2,0},{3,1},{4,2},{5,3},{6,4},{7,5},{8,14},{9,15},{10,... | collective-permute-start | bytes 294920 | tf_op jit(solution)/shard_map/ppermute | solution.py:262
  18.3 8.9 %collective-permute-start.6 = (f32[64,512]{1,0:T(8,128)S(1)}, f32[64,512]{1,0:T(8,128)S(1)}, u32[]{:S(2)}, u32[]{:S(2)}) collective-permute-start(f32[64,512]{1,0:T(8,128)S(1)} %constant_dynamic-update-slice_fusion), channel_id=1, source_target_pairs={{0,128},{16,144},{32,160},{48,176},{64,192},{80,208},{96,224},{112... | collective-permute-start | bytes 393224 | tf_op jit(solution)/shard_map/ppermute | solution.py:256
  21.8 5.4 %collective-permute-start.4 = (f32[16,1536]{1,0:T(8,128)S(1)}, f32[16,1536]{1,0:T(8,128)S(1)}, u32[]{:S(2)}, u32[]{:S(2)}) collective-permute-start(f32[16,1536]{1,0:T(8,128)S(1)} %fusion.2), channel_id=1, source_target_pairs={{0,8},{1,9},{2,10},{3,11},{4,12},{5,13},{6,14},{7,15},{8,0},{9,1},... | collective-permute-start | bytes 294920 | tf_op jit(solution)/shard_map/ppermute | solution.py:266
  27.2 5.3 %collective-permute-start.10 = (f32[128,512]{1,0:T(8,128)S(1)}, f32[128,512]{1,0:T(8,128)S(1)}, u32[]{:S(2)}, u32[]{:S(2)}) collective-permute-start(f32[128,512]{1,0:T(8,128)S(1)} %pad_maximum_fusion.2), channel_id=1, source_target_pairs={{0,32},{16,48},{32,0},{48,16},{64,96},{80,112},{96,64},{112,80},{1... | collective-permute-start | bytes 786440 | tf_op jit(solution)/shard_map/ppermute | solution.py:256
  27.3 5.3 %collective-permute-start.7 = (f32[16,1536]{1,0:T(8,128)S(1)}, f32[16,1536]{1,0:T(8,128)S(1)}, u32[]{:S(2)}, u32[]{:S(2)}) collective-permute-start(f32[16,1536]{1,0:T(8,128)S(1)} %add.35.refs_0_), channel_id=1, source_target_pairs={{0,2},{1,3},{2,4},{3,5},{4,6},{5,7},{6,0},{7,1},{8,10},{9,11},{10,... | collective-permute-start | bytes 294920 | tf_op jit(solution)/shard_map/ppermute | solution.py:269
  27.9 5.2 %collective-permute-start.8 = (f32[16,1536]{1,0:T(8,128)S(1)}, f32[16,1536]{1,0:T(8,128)S(1)}, u32[]{:S(2)}, u32[]{:S(2)}) collective-permute-start(f32[16,1536]{1,0:T(8,128)S(1)} %add.35.refs_0_), channel_id=1, source_target_pairs={{0,4},{1,5},{2,6},{3,7},{4,0},{5,1},{6,2},{7,3},{8,12},{9,13},{10,... | collective-permute-start | bytes 294920 | tf_op jit(solution)/shard_map/ppermute | solution.py:269
  30.1 3.6 %collective-permute-start.9 = (f32[16,1536]{1,0:T(8,128)S(1)}, f32[16,1536]{1,0:T(8,128)S(1)}, u32[]{:S(2)}, u32[]{:S(2)}) collective-permute-start(f32[16,1536]{1,0:T(8,128)S(1)} %add.35.refs_0_), channel_id=1, source_target_pairs={{0,6},{1,7},{2,0},{3,1},{4,2},{5,3},{6,4},{7,5},{8,14},{9,15},{10,... | collective-permute-start | bytes 294920 | tf_op jit(solution)/shard_map/ppermute | solution.py:269
  33.8 6.8 %collective-permute-start.11 = (f32[4,16,1536]{2,1,0:T(8,128)S(1)}, f32[4,16,1536]{2,1,0:T(8,128)S(1)}, u32[]{:S(2)}, u32[]{:S(2)}) collective-permute-start(f32[4,16,1536]{2,1,0:T(8,128)S(1)} %pad_maximum_fusion.1), channel_id=1, source_target_pairs={{0,1},{1,0},{2,3},{3,2},{4,5},{5,4},{6,7},{7,6},{8,9},{9,8},{10,11... | collective-permute-start | bytes 1179656 | tf_op jit(solution)/shard_map/ppermute | solution.py:273
  39.2 13.5 %collective-permute-start.13 = (f32[256,512]{1,0:T(8,128)S(1)}, f32[256,512]{1,0:T(8,128)S(1)}, u32[]{:S(2)}, u32[]{:S(2)}) collective-permute-start(f32[256,512]{1,0:T(8,128)S(1)} %pad_maximum_fusion.v_ref), channel_id=1, source_target_pairs={{0,16},{16,0},{32,48},{48,32},{64,80},{80,64},{96,112},{112,96},{1... | collective-permute-start | bytes 1572872 | tf_op jit(solution)/shard_map/ppermute | solution.py:256
  42.9 1.4 %collective-permute-start.12 = (f32[8,32,128]{2,1,0:T(8,128)S(1)}, f32[8,32,128]{2,1,0:T(8,128)S(1)}, u32[]{:S(2)}, u32[]{:S(2)}) collective-permute-start(f32[8,32,128]{2,1,0:T(8,128)S(1)} %get-tuple-element.46), channel_id=1, source_target_pairs={{0,1},{1,0},{2,3},{3,2},{4,5},{5,4},{6,7},{7,6},{8,9},{9,8},{10,11... | collective-permute-start | bytes 393224 | tf_op jit(solution)/shard_map/ppermute | solution.py:277
  45.0 13.1 %all-to-all-start = ((f32[8,32,128]{2,1,0:T(8,128)}), f32[8,32,128]{2,1,0:T(8,128)S(1)}, u32[]{:S(2)}, u32[]{:S(2)}) async-start(f32[8,32,128]{2,1,0:T(8,128)} %add.36), calls=%async_computation | async-start | bytes 262144 | tf_op jit(solution)/shard_map/all_to_all | solution.py:279
